TPU v7x, 32 devices: a whole 2x2x4 slice. The times are simulated.
32 devices in a mesh: groups: 2 (over x), tm: 16 (over z, y, core).
Axes of the slice: x: 2, y: 2, z: 4, core: 2. Of those that a mesh axis runs over, the one named last changes fastest.
Arguments:
- sharded_latents: bfloat16 [32, 6144], P('groups', 'tm'), parts along dimension 0, may hold values from -6 to 6
- sample_frame_count: int32 [16], P('groups'), parts along dimension 0, may hold values from 5 to 8, as said below
- entry_kernel: bfloat16 [27, 16, 384], replicated, may hold values from -0.3125 to 0.3125
- entry_bias: float32 [384], replicated, may hold values from -3 to 3
- norm_scale_gain: float32 [384], replicated, may hold values from 0.25 to 1.75
- residual_kernel: bfloat16 [27, 384, 384], P(None, 'tm'), may hold values from -0.0625 to 0.0625
- residual_bias: float32 [384], replicated, may hold values from -3 to 3
Outputs:
- decoded: bfloat16 [128, 6, 16, 384], P(('groups', 'tm')), parts along dimension 0
There are 2 independent parts, one for each index of `groups`. A program takes and returns all parts, laid end to end along the dimension named above; an argument that names none is the same for every part. Nothing has to cross between parts.
Inputs may be any that keep to these rules, and one draw needn't show every extreme that they name: `sample_frame_count`: every sample has more than half of its 8 frames valid; some sample has all of them valid.
All inputs are finite; a program needn't handle non-finite values.
Results may differ from a plain program's by a relative error of at most 0.009.
Values may be sent and summed in bfloat16 or wider, within the bound.
No kernel may reach another device: no remote copies, remote signals or barrier semaphores. Data moves between devices by JAX's collectives and lax.ppermute only.
A program may use at most 64 MiB of HBM per device.

v0:
```python
import jax
import jax.numpy as jnp
from jax import lax
from jax.sharding import PartitionSpec as P

LATENT_CHANNELS = 16
C = 384
PROMPT_SAMPLES = 8
BLOCK_FRAMES = 4
LATENT_ROWS = 6
LATENT_COLUMNS = 16


def from_behind(block, axis, distance):
    devices = range(lax.axis_size(axis))
    route = [(i - distance, i) for i in devices if i - distance in devices]
    return lax.ppermute(block, axis, route)


def causal_conv(frames, weight):
    frames_out = frames.shape[0] - 2
    inputs = frames.shape[3]
    padded = jnp.pad(frames, ((0, 0), (1, 1), (1, 1), (0, 0)))
    total = jnp.zeros((frames_out * LATENT_ROWS * LATENT_COLUMNS, weight.shape[2]), jnp.float32)
    for time_tap in range(3):
        for row_tap in range(3):
            for col_tap in range(3):
                window = padded[
                    time_tap : time_tap + frames_out,
                    row_tap : row_tap + LATENT_ROWS,
                    col_tap : col_tap + LATENT_COLUMNS,
                    :,
                ]
                window = window.reshape(frames_out * LATENT_ROWS * LATENT_COLUMNS, inputs)
                tap = 9 * time_tap + 3 * row_tap + col_tap
                total = total + jnp.dot(window, weight[tap], preferred_element_type=jnp.float32)
    return total


def activate(stream, norm_scale_gain):
    values = stream.astype(jnp.float32)
    scale = lax.rsqrt(jnp.mean(values * values, axis=-1, keepdims=True) + 1e-06)
    return jax.nn.silu(values * scale * norm_scale_gain).astype(jnp.bfloat16)


def to_cells(planes):
    return jnp.transpose(
        planes.reshape(planes.shape[0], LATENT_CHANNELS, LATENT_ROWS, LATENT_COLUMNS), (0, 2, 3, 1)
    )


def shards(
    sharded_latents,
    sample_frame_count,
    entry_kernel,
    entry_bias,
    norm_scale_gain,
    residual_kernel,
    residual_bias,
):
    gathered_latents = lax.all_to_all(
        sharded_latents, "tm", split_axis=0, concat_axis=1, tiled=True
    )
    latent_volume = gathered_latents.reshape(
        BLOCK_FRAMES, LATENT_CHANNELS, LATENT_ROWS * LATENT_COLUMNS
    )
    position = lax.axis_index("tm")
    block = position // PROMPT_SAMPLES
    sample = position % PROMPT_SAMPLES
    keep = block > 0
    earlier = from_behind(latent_volume, "tm", PROMPT_SAMPLES)
    earlier = jnp.where(keep, earlier, jnp.zeros_like(earlier))
    frames = to_cells(jnp.concatenate([earlier, latent_volume], axis=0))
    widened = (causal_conv(frames, entry_kernel) + entry_bias).astype(jnp.bfloat16)
    active_all = activate(widened, norm_scale_gain).reshape(
        BLOCK_FRAMES + 2, LATENT_ROWS, LATENT_COLUMNS, C
    )
    behind = jnp.where(keep, active_all[:2], jnp.zeros_like(active_all[:2]))
    extended = jnp.concatenate([behind, active_all[2:]], axis=0)
    stream = widened[2 * LATENT_ROWS * LATENT_COLUMNS :]
    kernel_all = lax.all_gather(residual_kernel, "tm", axis=1, tiled=True)
    branch = causal_conv(extended, kernel_all)
    total = (stream.astype(jnp.float32) + (branch + residual_bias)).reshape(
        BLOCK_FRAMES, LATENT_ROWS, LATENT_COLUMNS, C
    )
    limit = jnp.sum(jnp.where(jnp.arange(PROMPT_SAMPLES) == sample, sample_frame_count, 0))
    frame_index = block * BLOCK_FRAMES + jnp.arange(BLOCK_FRAMES)
    valid = (frame_index < limit)[:, None, None, None]
    return jnp.where(valid, total, jnp.zeros_like(total)).astype(jnp.bfloat16)


def solution(mesh):
    in_specs = (P("groups", "tm"), P("groups"), P(), P(), P(), P(None, "tm", None), P())
    out_specs = P(("groups", "tm"), None, None, None)
    return jax.shard_map(shards, mesh=mesh, in_specs=in_specs, out_specs=out_specs, check_vma=False)
```

profile of v0, /device:TPU:0, one launch (start us, length us, event | category | flops | bytes accessed | tf_op | source)
XLA Modules:
  0.0 109.1 jit_solution(9590959347050248216)
XLA Ops:
  7.8 1.4 %reduce.2 = bf16[16,384]{1,0:T(8,128)(2,1)S(1)} reduce(bf16[16,1,384]{2,0,1:T(8,128)(2,1)} %bitcast.334, bf16[]{:T(256)} %broadcast.36), dimensions={1}, to_apply=%copy.62.reduce_sub_computation | reduce | bytes 24578 | tf_op jit(solution)/shard_map/all_to_all | solution.py:61
  9.8 7.4 %all-to-all-start = ((bf16[16,2,192]{2,1,0:T(2,128)(2,1)}), bf16[16,2,192]{2,1,0:T(2,128)(2,1)S(1)}, u32[]{:S(2)}, u32[]{:S(2)}) async-start(bf16[16,2,192]{2,1,0:T(2,128)(2,1)} %reshape.257), calls=%async_computation | async-start | bytes 32768 | tf_op jit(solution)/shard_map/all_to_all | solution.py:61
  17.2 1.3 %fusion.70 = s32[]{:T(128)} fusion(s32[8]{0:T(128)} %param.8, s32[]{:T(128)S(6)} %select_n.39), kind=kLoop, calls=%fused_computation.186 | loop fusion | flops 23 | bytes 40 | tf_op jit(solution)/shard_map/reduce_sum | solution.py:86
  18.5 5.2 %all-to-all-done = bf16[16,2,192]{2,1,0:T(2,128)(2,1)S(1)} async-done(((bf16[16,2,192]{2,1,0:T(2,128)(2,1)}), bf16[16,2,192]{2,1,0:T(2,128)(2,1)S(1)}, u32[]{:S(2)}, u32[]{:S(2)}) %all-to-all-start) | async-done | bytes 12320 | tf_op jit(solution)/shard_map/all_to_all | solution.py:61
  24.0 2.4 %collective-permute-start = (bf16[4,16,96]{2,1,0:T(8,128)(2,1)S(1)}, bf16[4,16,96]{2,1,0:T(8,128)(2,1)S(1)}, u32[]{:S(2)}, u32[]{:S(2)}) collective-permute-start(bf16[4,16,96]{2,1,0:T(8,128)(2,1)S(1)} %reshape.200), channel_id=1, source_target_pairs={{0,8},{1,9},{2,10},{3,11},{4,12},{5,13},{6,14},{7,15},{16,24},{17,... | collective-permute-start | bytes 36872 | tf_op jit(solution)/shard_map/ppermute | solution.py:17
  28.5 0.8 reshape.201
  30.7 0.8 reshape.203
  32.4 0.8 reshape.205
  35.7 0.8 reshape.209
  38.7 0.8 reshape.212
  42.8 1.0 fusion.41
  43.8 1.0 convolution_add_fusion.25
  44.9 1.1 convolution_add_fusion.24
  54.5 0.9 fusion.13
  55.4 1.2 %pad_slice_fusion.1 = (bf16[4,6,16,384]{3,2,1,0:T(8,128)(2,1)}, bf16[4,6,16,384]{3,2,1,0:T(8,128)(2,1)}, bf16[4,6,16,384]{3,2,1,0:T(8,128)(2,1)}, bf16[4,6,16,384]{3,2,1,0:T(8,128)(2,1)}, bf16[4,6,16,384]{3,2,1,0:T(8,128)(2,1)}) fusion(bf16[6,6,16,384]{3,2,1,0:T(8,128)(2,1)S(1)} %pad_maximum_fusion), kind=kLoop, calls=%fused_computation.1 | loop fusion | bytes 1916928 | tf_op jit(solution)/shard_map/slice | solution.py:28
  56.6 2.2 %pad_slice_fusion = (bf16[4,6,16,384]{3,2,1,0:T(8,128)(2,1)}, bf16[4,6,16,384]{3,2,1,0:T(8,128)(2,1)}, bf16[4,6,16,384]{3,2,1,0:T(8,128)(2,1)}, bf16[4,6,16,384]...) fusion(bf16[6,6,16,384]{3,2,1,0:T(8,128)(2,1)S(1)} %pad_maximum, ...), kind=kLoop, calls=%fused_computation | loop fusion | bytes 6045696 | tf_op jit(solution)/shard_map/slice | solution.py:28
  58.8 26.1 %all-gather.2.cloned.1.call-done = bf16[27,384,384]{2,1,0:T(8,128)(2,1)} async-done(((bf16[27,24,384]{2,1,0:T(8,128)(2,1)}), bf16[27,384,384]{2,1,0:T(8,128)(2,1)}) %all-gather.2.cloned.1.call-update) | async-done | bytes 7962640 | tf_op jit(solution)/shard_map/all_gather | solution.py:81
  84.9 1.5 %fusion.14 = f32[384,384]{1,0:T(8,128)S(1)} fusion(bf16[384,384]{1,0:T(8,128)(2,1)} %bitcast.333, bf16[27,384,384]{2,1,0:T(8,128)(2,1)} %all-gather.2.cloned.1.call-done), kind=kOutput, calls=%fused_computation.125 | convolution fusion | flops 113246208 | bytes 1179648 | tf_op jit(solution)/shard_map/dot_general | solution.py:36
  86.5 2.0 %convolution_add_fusion.51 = f32[384,384]{1,0:T(8,128)S(1)} fusion(f32[384,384]{1,0:T(8,128)S(1)} %fusion.14, bf16[384,384]{1,0:T(8,128)(2,1)} %bitcast.324, bf16[27,384,384]{2,1,0:T(8,128)(2,1)} %all-gather.2.cloned.1.call-done), kind=kOutput, calls=%fused_computation.79 | convolution fusion | flops 113393664 | bytes 1769472 | tf_op jit(solution)/shard_map/dot_general | solution.py:36
  88.5 1.4 %convolution_add_fusion.50 = f32[384,384]{1,0:T(8,128)S(1)} fusion(f32[384,384]{1,0:T(8,128)S(1)} %convolution_add_fusion.51, bf16[384,384]{1,0:T(8,128)(2,1)} %bitcast.323, bf16[27,384,384]{2,1,0:T(8,128)(2,1)} %all-gather.2.cloned.1.call-done), kind=kOutput, calls=%fused_computation.78 | convolution fusion | flops 113393664 | bytes 1769472 | tf_op jit(solution)/shard_map/dot_general | solution.py:36
  89.9 1.4 %convolution_add_fusion.49 = f32[384,384]{1,0:T(8,128)S(1)} fusion(f32[384,384]{1,0:T(8,128)S(1)} %convolution_add_fusion.50, bf16[384,384]{1,0:T(8,128)(2,1)} %bitcast.322, bf16[27,384,384]{2,1,0:T(8,128)(2,1)} %all-gather.2.cloned.1.call-done), kind=kOutput, calls=%fused_computation.77 | convolution fusion | flops 113393664 | bytes 1769472 | tf_op jit(solution)/shard_map/dot_general | solution.py:36
  91.3 1.4 %convolution_add_fusion.48 = f32[384,384]{1,0:T(8,128)S(1)} fusion(f32[384,384]{1,0:T(8,128)S(1)} %convolution_add_fusion.49, bf16[384,384]{1,0:T(8,128)(2,1)} %bitcast.327, bf16[27,384,384]{2,1,0:T(8,128)(2,1)} %all-gather.2.cloned.1.call-done), kind=kOutput, calls=%fused_computation.76 | convolution fusion | flops 113393664 | bytes 1769472 | tf_op jit(solution)/shard_map/dot_general | solution.py:36
  92.7 1.3 %convolution_add_fusion.47 = f32[384,384]{1,0:T(8,128)S(1)} fusion(f32[384,384]{1,0:T(8,128)S(1)} %convolution_add_fusion.48, bf16[384,384]{1,0:T(8,128)(2,1)} %bitcast.321, bf16[27,384,384]{2,1,0:T(8,128)(2,1)S(1)} %copy-done), kind=kOutput, calls=%fused_computation.75 | convolution fusion | flops 113393664 | bytes 1769472 | tf_op jit(solution)/shard_map/dot_general | solution.py:36
  101.4 0.8 select_convert_fusion
  (165 shorter events, 29.7 us)
Async XLA Ops:
  6.5 78.4 %all-gather.2.cloned.1.call-start = ((), (), s32[]{:S(2)}) async-start(), calls=%async_computation.1 | async-start | bytes 8460288 | tf_op jit(solution)/shard_map/all_gather | solution.py:81
  9.8 13.9 %all-to-all-start = ((bf16[16,2,192]{2,1,0:T(2,128)(2,1)}), bf16[16,2,192]{2,1,0:T(2,128)(2,1)S(1)}, u32[]{:S(2)}, u32[]{:S(2)}) async-start(bf16[16,2,192]{2,1,0:T(2,128)(2,1)} %reshape.257), calls=%async_computation | async-start | bytes 32768 | tf_op jit(solution)/shard_map/all_to_all | solution.py:61
  24.0 3.9 %collective-permute-start = (bf16[4,16,96]{2,1,0:T(8,128)(2,1)S(1)}, bf16[4,16,96]{2,1,0:T(8,128)(2,1)S(1)}, u32[]{:S(2)}, u32[]{:S(2)}) collective-permute-start(bf16[4,16,96]{2,1,0:T(8,128)(2,1)S(1)} %reshape.200), channel_id=1, source_target_pairs={{0,8},{1,9},{2,10},{3,11},{4,12},{5,13},{6,14},{7,15},{16,24},{17,... | collective-permute-start | bytes 36872 | tf_op jit(solution)/shard_map/ppermute | solution.py:17
  37.8 8.2 %copy-start.13 = (bf16[576,16]{0,1:T(8,128)(2,1)S(1)}, bf16[576,16]{0,1:T(8,128)(2,1)}, u32[]{:S(2)}) copy-start(bf16[576,16]{0,1:T(8,128)(2,1)} %reshape.204) | copy-start | bytes 55300
  38.6 7.7 %copy-start.14 = (bf16[576,16]{0,1:T(8,128)(2,1)S(1)}, bf16[576,16]{0,1:T(8,128)(2,1)}, u32[]{:S(2)}) copy-start(bf16[576,16]{0,1:T(8,128)(2,1)} %reshape.205) | copy-start | bytes 55300
  38.7 4.1 %copy-start.12 = (bf16[27,16,384]{2,1,0:T(8,128)(2,1)S(1)}, bf16[27,16,384]{2,1,0:T(8,128)(2,1)}, u32[]{:S(2)}) copy-start(bf16[27,16,384]{2,1,0:T(8,128)(2,1)} %param.9) | copy-start | bytes 995332
  39.9 6.7 %copy-start.15 = (bf16[576,16]{0,1:T(8,128)(2,1)S(1)}, bf16[576,16]{0,1:T(8,128)(2,1)}, u32[]{:S(2)}) copy-start(bf16[576,16]{0,1:T(8,128)(2,1)} %reshape.206) | copy-start | bytes 55300
  40.6 6.4 %copy-start.16 = (bf16[576,16]{0,1:T(8,128)(2,1)S(1)}, bf16[576,16]{0,1:T(8,128)(2,1)}, u32[]{:S(2)}) copy-start(bf16[576,16]{0,1:T(8,128)(2,1)} %reshape.207) | copy-start | bytes 55300
  41.2 6.1 %copy-start.17 = (bf16[576,16]{0,1:T(8,128)(2,1)S(1)}, bf16[576,16]{0,1:T(8,128)(2,1)}, u32[]{:S(2)}) copy-start(bf16[576,16]{0,1:T(8,128)(2,1)} %reshape.208) | copy-start | bytes 55300
  41.9 5.7 %copy-start.18 = (bf16[576,16]{0,1:T(8,128)(2,1)S(1)}, bf16[576,16]{0,1:T(8,128)(2,1)}, u32[]{:S(2)}) copy-start(bf16[576,16]{0,1:T(8,128)(2,1)} %reshape.209) | copy-start | bytes 55300
  42.5 5.4 %copy-start.19 = (bf16[576,16]{0,1:T(8,128)(2,1)S(1)}, bf16[576,16]{0,1:T(8,128)(2,1)}, u32[]{:S(2)}) copy-start(bf16[576,16]{0,1:T(8,128)(2,1)} %reshape.210) | copy-start | bytes 55300
  43.8 4.4 %copy-start.20 = (bf16[576,16]{0,1:T(8,128)(2,1)S(1)}, bf16[576,16]{0,1:T(8,128)(2,1)}, u32[]{:S(2)}) copy-start(bf16[576,16]{0,1:T(8,128)(2,1)} %reshape.211) | copy-start | bytes 55300
  44.9 3.7 %copy-start.21 = (bf16[576,16]{0,1:T(8,128)(2,1)S(1)}, bf16[576,16]{0,1:T(8,128)(2,1)}, u32[]{:S(2)}) copy-start(bf16[576,16]{0,1:T(8,128)(2,1)} %reshape.212) | copy-start | bytes 55300
  50.8 3.2 %copy-start.23 = (f32[384]{0:T(512)S(1)}, f32[384]{0:T(512)}, u32[]{:S(2)}) copy-start(f32[384]{0:T(512)} %param.11) | copy-start | bytes 4612
  84.9 7.8 %copy-start = (bf16[27,384,384]{2,1,0:T(8,128)(2,1)S(1)}, bf16[27,384,384]{2,1,0:T(8,128)(2,1)}, u32[]{:S(2)}) copy-start(bf16[27,384,384]{2,1,0:T(8,128)(2,1)} %all-gather.2.cloned.1.call-done) | copy-start | bytes 23887876
  84.9 9.1 %copy-start.5 = (bf16[4,6,16,384]{3,2,1,0:T(8,128)(2,1)S(1)}, bf16[4,6,16,384]{3,2,1,0:T(8,128)(2,1)}, u32[]{:S(2)}) copy-start(bf16[4,6,16,384]{3,2,1,0:T(8,128)(2,1)} %get-tuple-element.10) | copy-start | bytes 884740
  84.9 9.5 %copy-start.4 = (bf16[4,6,16,384]{3,2,1,0:T(8,128)(2,1)S(1)}, bf16[4,6,16,384]{3,2,1,0:T(8,128)(2,1)}, u32[]{:S(2)}) copy-start(bf16[4,6,16,384]{3,2,1,0:T(8,128)(2,1)} %get-tuple-element.11) | copy-start | bytes 884740
  84.9 9.8 %copy-start.3 = (bf16[4,6,16,384]{3,2,1,0:T(8,128)(2,1)S(1)}, bf16[4,6,16,384]{3,2,1,0:T(8,128)(2,1)}, u32[]{:S(2)}) copy-start(bf16[4,6,16,384]{3,2,1,0:T(8,128)(2,1)} %get-tuple-element.12) | copy-start | bytes 884740
  84.9 10.2 %copy-start.2 = (bf16[4,6,16,384]{3,2,1,0:T(8,128)(2,1)S(1)}, bf16[4,6,16,384]{3,2,1,0:T(8,128)(2,1)}, u32[]{:S(2)}) copy-start(bf16[4,6,16,384]{3,2,1,0:T(8,128)(2,1)} %get-tuple-element.13) | copy-start | bytes 884740
  86.4 9.0 %copy-start.1 = (bf16[4,6,16,384]{3,2,1,0:T(8,128)(2,1)S(1)}, bf16[4,6,16,384]{3,2,1,0:T(8,128)(2,1)}, u32[]{:S(2)}) copy-start(bf16[4,6,16,384]{3,2,1,0:T(8,128)(2,1)} %get-tuple-element.14) | copy-start | bytes 884740
  91.3 5.2 %copy-start.7 = (bf16[4,6,16,384]{3,2,1,0:T(8,128)(2,1)S(1)}, bf16[4,6,16,384]{3,2,1,0:T(8,128)(2,1)}, u32[]{:S(2)}) copy-start(bf16[4,6,16,384]{3,2,1,0:T(8,128)(2,1)} %get-tuple-element.29) | copy-start | bytes 884740
  96.1 3.1 %copy-start.11 = (bf16[4,6,16,384]{3,2,1,0:T(8,128)(2,1)S(1)}, bf16[4,6,16,384]{3,2,1,0:T(8,128)(2,1)}, u32[]{:S(2)}) copy-start(bf16[4,6,16,384]{3,2,1,0:T(8,128)(2,1)} %get-tuple-element.25) | copy-start | bytes 884740
  96.8 3.1 %copy-start.10 = (bf16[4,6,16,384]{3,2,1,0:T(8,128)(2,1)S(1)}, bf16[4,6,16,384]{3,2,1,0:T(8,128)(2,1)}, u32[]{:S(2)}) copy-start(bf16[4,6,16,384]{3,2,1,0:T(8,128)(2,1)} %get-tuple-element.26) | copy-start | bytes 884740
  97.2 3.1 %copy-start.9 = (bf16[4,6,16,384]{3,2,1,0:T(8,128)(2,1)S(1)}, bf16[4,6,16,384]{3,2,1,0:T(8,128)(2,1)}, u32[]{:S(2)}) copy-start(bf16[4,6,16,384]{3,2,1,0:T(8,128)(2,1)} %get-tuple-element.27) | copy-start | bytes 884740
  (4 other events, 12.5 us)
Sparse Core Ops, SparseCore 0:
  9.5 75.3 all-gather.1
where the time goes:
time: 110 us; the launch traced here: 109 us
  waiting for transfers between devices  32.7 us (30%)
  matrix products  27 us (25%)
  local copies, waits for them, and re-layouts  19.7 us (18%)
  between operations  14.4 us (13%)
  starting transfers between devices  9.76 us (9%)
  other arithmetic  5.58 us (5%)
    dot_general x54, matrix products, causal_conv(): jnp.dot(window, weight[tap], preferred_element_type=jnp.float32)  27 us
    all_gather x1, waiting for transfers between devices, shards(): kernel_all = lax.all_gather(residual_kernel, 'tm', axis=1, tiled=True)  26.1 us
    reshape x27, local copies, waits for them, and re-layouts, causal_conv(): window = window.reshape(frames_out * LATENT_ROWS * LATENT_COLUMNS, inputs)  12 us
    all_to_all x1, starting transfers between devices, shards(): lax.all_to_all(sharded_latents, 'tm', split_axis=0, concat_axis=1, tiled=...  7.39 us
    slice x32, local copies, waits for them, and re-layouts, causal_conv(): padded[time_tap:time_tap + frames_out, row_tap:row_tap + LATENT_ROWS, col...  5.87 us
    all_to_all x1, waiting for transfers between devices, shards(): lax.all_to_all(sharded_latents, 'tm', split_axis=0, concat_axis=1, tiled=...  5.18 us
    ppermute x1, starting transfers between devices, from_behind(): return lax.ppermute(block, axis, route)  2.37 us
  transfers between devices with their start and end apart: 3, of which 3 were waited for; matrix products, arithmetic and copies ran while one was open for 32% of the time, Pallas kernels for 0%

commit v1 on v0

--- a/solution.py
+++ b/solution.py
@@ -1,6 +1,10 @@
+import functools
+
 import jax
 import jax.numpy as jnp
 from jax import lax
+from jax.experimental import pallas as pl
+from jax.experimental.pallas import tpu as pltpu
 from jax.sharding import PartitionSpec as P
 
 LATENT_CHANNELS = 16
@@ -9,6 +13,189 @@
 BLOCK_FRAMES = 4
 LATENT_ROWS = 6
 LATENT_COLUMNS = 16
+HW = LATENT_ROWS * LATENT_COLUMNS
+LANES = PROMPT_SAMPLES * HW
+VMEM = pl.BlockSpec(memory_space=pltpu.VMEM)
+SMEM = pl.BlockSpec(memory_space=pltpu.SMEM)
+LIMIT = 56 * 1024 * 1024
+
+
+def shift_mask(j, k):
+    lane = lax.broadcasted_iota(jnp.int32, (1, LANES), 1)
+    row = (lane % HW) // LATENT_COLUMNS
+    col = lane % LATENT_COLUMNS
+    ok = lane >= 0
+    if j == 0:
+        ok = row > 0
+    elif j == 2:
+        ok = row < LATENT_ROWS - 1
+    if k == 0:
+        ok = ok & (col > 0)
+    elif k == 2:
+        ok = ok & (col < LATENT_COLUMNS - 1)
+    return ok
+
+
+def shifted(x, delta):
+    return x if delta == 0 else pltpu.roll(x, (-delta) % x.shape[1], 1)
+
+
+def latent_rows_kernel(x_ref, o_ref):
+    x = x_ref[...].astype(jnp.float32)
+    rows = []
+    for c in range(x.shape[1] // HW):
+        pieces = [x[r : r + 1, c * HW : (c + 1) * HW] for r in range(x.shape[0])]
+        rows.append(jnp.concatenate(pieces, axis=1))
+    o_ref[...] = jnp.concatenate(rows, axis=0).astype(jnp.bfloat16)
+
+
+def kernel_chunks_kernel(n, w_ref, o_ref):
+    own = C // n
+    w = w_ref[...].astype(jnp.float32).reshape(3, 9, own, C)
+    taps = [w[:, t].reshape(3 * own, C) for t in range(9)]
+    pad = o_ref.shape[1] - 9 * own
+    for d in range(0, n, 2):
+        both = []
+        for e in (d, d + 1):
+            pieces = [tap[:, e * own : (e + 1) * own] for tap in taps]
+            pieces.append(jnp.zeros((3 * own, pad), jnp.float32))
+            both.append(jnp.concatenate(pieces, axis=1))
+        o_ref[d * 3 * own : (d + 2) * 3 * own, :] = jnp.concatenate(both, axis=0).astype(jnp.bfloat16)
+
+
+def active_kernel(frames, own, lat_ref, entry_ref, bias_ref, gain_ref, first_ref, x_ref, stream_ref, col_ref, s0_ref, s1_ref):
+    weight = jnp.transpose(entry_ref[...])
+    taps = 9 * LATENT_CHANNELS
+    for f in range(frames):
+        b, g = divmod(f, BLOCK_FRAMES)
+        lat = lat_ref[g * LATENT_CHANNELS : (g + 1) * LATENT_CHANNELS, b * LANES : (b + 1) * LANES].astype(jnp.float32)
+        for j in range(3):
+            for k in range(3):
+                moved = shifted(lat, LATENT_COLUMNS * (j - 1) + k - 1)
+                moved = jnp.where(shift_mask(j, k), moved, 0.0)
+                at = f * taps + (3 * j + k) * LATENT_CHANNELS
+                col_ref[at : at + LATENT_CHANNELS, :] = moved.astype(jnp.bfloat16)
+    bias = bias_ref[...]
+    gain = gain_ref[...]
+    first = pl.multiple_of(first_ref[0], 8)
+    for f in range(frames):
+        s_ref = (s0_ref, s1_ref)[f % 2]
+        least = max(f - 2, 0)
+        s = jnp.dot(
+            weight[:, (2 - (f - least)) * taps :],
+            col_ref[least * taps : (f + 1) * taps, :],
+            preferred_element_type=jnp.float32,
+        )
+        s = (s + bias).astype(jnp.bfloat16).astype(jnp.float32)
+        s_ref[...] = s
+        scale = lax.rsqrt(jnp.sum(s * s, axis=0, keepdims=True) * (1.0 / C) + 1e-06)
+        half = s_ref[...] * (scale * 0.5) * gain
+        x_ref[f * C : (f + 1) * C, :] = (half + half * jnp.tanh(half)).astype(jnp.bfloat16)
+        stream_ref[f] = s_ref[pl.ds(first, own), :]
+
+
+def branch_kernel(frames, n, w_ref, x_ref, stream_ref, bias_ref, count_ref, o_ref, out_ref):
+    own = C // n
+    w = w_ref[...].astype(jnp.float32).reshape(n, 3, own, w_ref.shape[1])
+    w = jnp.transpose(w, (1, 0, 2, 3)).reshape(3 * C, w_ref.shape[1])
+    weight = jnp.transpose(w.astype(jnp.bfloat16))
+    lane = lax.broadcasted_iota(jnp.int32, (1, LANES), 1)
+    count = jnp.zeros((1, LANES), jnp.int32)
+    for s in range(PROMPT_SAMPLES):
+        count = jnp.where(lane // HW == s, count_ref[s], count)
+    for f in range(frames):
+        least = max(f - 2, 0)
+        z = jnp.dot(
+            weight[:, (2 - (f - least)) * C :],
+            x_ref[least * C : (f + 1) * C, :],
+            preferred_element_type=jnp.float32,
+        )
+        total = stream_ref[f] + bias_ref[...]
+        for k in range(3):
+            part = None
+            for j in range(3):
+                tap = z[(3 * j + k) * own : (3 * j + k + 1) * own]
+                if j != 1:
+                    tap = jnp.where(shift_mask(j, 1), shifted(tap, LATENT_COLUMNS * (j - 1)), 0.0)
+                part = tap if part is None else part + tap
+            if k != 1:
+                part = jnp.where(shift_mask(1, k), shifted(part, k - 1), 0.0)
+            total = total + part
+        out_ref[f] = jnp.where(count > f, total, 0.0)
+    for b in range(frames // BLOCK_FRAMES):
+        parts = [out_ref[b * BLOCK_FRAMES + g] for g in range(BLOCK_FRAMES)]
+        for s in range(0, PROMPT_SAMPLES, 2):
+            both = [
+                jnp.concatenate([p[:, t * HW : (t + 1) * HW] for p in parts], axis=1) for t in (s, s + 1)
+            ]
+            at = (b * PROMPT_SAMPLES + s) * own
+            o_ref[at : at + 2 * own, :] = jnp.concatenate(both, axis=0).astype(jnp.bfloat16)
+
+
+def transpose_kernel(x_ref, o_ref):
+    o_ref[...] = jnp.transpose(x_ref[...])
+
+
+def call(body, out, specs, scratch=(), flops=0, moved=0):
+    return pl.pallas_call(
+        body,
+        out_shape=out,
+        in_specs=specs,
+        out_specs=jax.tree.map(lambda _: VMEM, out),
+        scratch_shapes=list(scratch),
+        compiler_params=pltpu.CompilerParams(vmem_limit_bytes=LIMIT),
+        cost_estimate=pl.CostEstimate(flops=flops, bytes_accessed=moved, transcendentals=0),
+    )
+
+
+def by_channel(n, latents, counts, entry_kernel, entry_bias, gain, kernel, bias):
+    own = C // n
+    frames = n // PROMPT_SAMPLES * BLOCK_FRAMES
+    first = (lax.axis_index("tm") * own).astype(jnp.int32)
+    shape = jax.ShapeDtypeStruct
+    rows = call(
+        latent_rows_kernel,
+        shape((latents.shape[1] // HW, n * HW), jnp.bfloat16),
+        [VMEM],
+    )(latents)
+    rows = lax.all_gather(rows, "tm", axis=0, tiled=True)
+    width = -(-9 * own // 128) * 128
+    chunks = call(
+        functools.partial(kernel_chunks_kernel, n),
+        shape((n * 3 * own, width), jnp.bfloat16),
+        [VMEM],
+    )(kernel)
+    chunks = lax.all_to_all(chunks, "tm", split_axis=0, concat_axis=0, tiled=True)
+    active, stream = call(
+        functools.partial(active_kernel, frames, own),
+        (shape((frames * C, LANES), jnp.bfloat16), shape((frames, own, LANES), jnp.float32)),
+        [VMEM, VMEM, VMEM, VMEM, SMEM],
+        [
+            pltpu.VMEM((frames * 9 * LATENT_CHANNELS, LANES), jnp.bfloat16),
+            pltpu.VMEM((C, LANES), jnp.float32),
+            pltpu.VMEM((C, LANES), jnp.float32),
+        ],
+        flops=2 * frames * LANES * 432 * C,
+        moved=20_000_000,
+    )(
+        rows,
+        entry_kernel.reshape(27 * LATENT_CHANNELS, C),
+        entry_bias.reshape(C, 1),
+        gain.reshape(C, 1),
+        first.reshape(1),
+    )
+    own_bias = lax.dynamic_slice(bias, (first,), (own,)).reshape(own, 1)
+    out = call(
+        functools.partial(branch_kernel, frames, n),
+        shape((n * own, BLOCK_FRAMES * HW), jnp.bfloat16),
+        [VMEM, VMEM, VMEM, VMEM, SMEM],
+        [pltpu.VMEM((frames, own, LANES), jnp.float32)],
+        flops=2 * frames * LANES * 27 * C * own,
+        moved=20_000_000,
+    )(chunks, active, stream, own_bias, counts)
+    out = lax.all_to_all(out, "tm", split_axis=0, concat_axis=0, tiled=True)
+    out = call(transpose_kernel, shape((BLOCK_FRAMES * HW, C), jnp.bfloat16), [VMEM])(out)
+    return out.reshape(BLOCK_FRAMES, LATENT_ROWS, LATENT_COLUMNS, C)
 
 
 def from_behind(block, axis, distance):
@@ -49,7 +236,7 @@
     )
 
 
-def shards(
+def by_block(
     sharded_latents,
     sample_frame_count,
     entry_kernel,
@@ -90,6 +277,10 @@
 
 
 def solution(mesh):
+    n = mesh.shape["tm"]
+    cells = BLOCK_FRAMES * LATENT_CHANNELS * HW
+    whole_rows = cells % (n * HW) == 0 and C % n == 0 and (C // n) % 8 == 0 and n % PROMPT_SAMPLES == 0
+    body = functools.partial(by_channel, n) if whole_rows else by_block
     in_specs = (P("groups", "tm"), P("groups"), P(), P(), P(), P(None, "tm", None), P())
     out_specs = P(("groups", "tm"), None, None, None)
-    return jax.shard_map(shards, mesh=mesh, in_specs=in_specs, out_specs=out_specs, check_vma=False)
+    return jax.shard_map(body, mesh=mesh, in_specs=in_specs, out_specs=out_specs, check_vma=False)

time: 110 us -> 75.2 us (0.68)
  blocking collectives: 0 us -> 40.1 us
  waiting for transfers between devices: 32.7 us -> 0.01 us
  matrix products: 27 us -> 0 us
  Pallas kernels: 0 us -> 22 us
  local copies, waits for them, and re-layouts: 19.7 us -> 5.23 us
  between operations: 14.4 us -> 0.02 us
  other arithmetic: 5.58 us -> 0 us
  starting transfers between devices: 9.76 us -> 7.39 us
    dot_general x54 -> x0, matrix products: 27 us -> none  [causal_conv(): jnp.dot(window, weight[tap], preferred_element_type=jnp.float32)]
    all_gather x1 -> x0, waiting for transfers between devices: 26.1 us -> none  [shards(): kernel_all = lax.all_gather(residual_kernel, 'tm', axis=1, tiled=True)]
    all_gather x0 -> x1, blocking collectives: none -> 25.4 us  [by_channel(): rows = lax.all_gather(rows, 'tm', axis=0, tiled=True)]
    pallas_call x0 -> x5, Pallas kernels: none -> 22 us  [the longest x1 8.63 us: by_channel(): call(functools.partial(active_kernel, frames, own), (shape((frames * C, L...]
    all_to_all x0 -> x1, blocking collectives: none -> 14.8 us  [by_channel(): out = lax.all_to_all(out, 'tm', split_axis=0, concat_axis=0, tiled=True)]
    reshape x28 -> x4, local copies, waits for them, and re-layouts: 12.1 us -> 3.69 us  [the longest x1 1.47 us: by_channel(): entry_bias.reshape(C, 1)]
    slice x33 -> x0, local copies, waits for them, and re-layouts: 5.9 us -> none  [the longest x32 5.87 us: causal_conv(): padded[time_tap:time_tap + frames_out, row_tap:row_tap + LATENT_ROWS, col...]
    all_to_all x1, waiting for transfers between devices: 5.18 us -> 0.01 us  [by_channel(): lax.all_to_all(chunks, 'tm', split_axis=0, concat_axis=0, tiled=True)]
  transfers between devices with their start and end apart: 3 -> 1, of which waited for: 3 -> 0; matrix products, arithmetic and copies ran while one was open for 32% -> 6% of each run, Pallas kernels for 0% -> 13%
where the time goes in v1:
time: 75.2 us; the launch traced here: 74.7 us
  blocking collectives  40.1 us (53%)
  Pallas kernels  22 us (29%)
  starting transfers between devices  7.39 us (10%)
  local copies, waits for them, and re-layouts  5.23 us (7%)
    all_gather x1, blocking collectives, by_channel(): rows = lax.all_gather(rows, 'tm', axis=0, tiled=True)  25.4 us
    all_to_all x1, blocking collectives, by_channel(): out = lax.all_to_all(out, 'tm', split_axis=0, concat_axis=0, tiled=True)  14.8 us
    pallas_call x1, Pallas kernels, by_channel(): call(functools.partial(active_kernel, frames, own), (shape((frames * C, L...  8.63 us
    pallas_call x1, Pallas kernels, by_channel(): call(functools.partial(branch_kernel, frames, n), shape((n * own, BLOCK_F...  7.45 us
    all_to_all x1, starting transfers between devices, by_channel(): lax.all_to_all(chunks, 'tm', split_axis=0, concat_axis=0, tiled=True)  7.39 us
    pallas_call x1, Pallas kernels, by_channel(): call(functools.partial(kernel_chunks_kernel, n), shape((n * 3 * own, widt...  2.66 us
    pallas_call x1, Pallas kernels, by_channel(): call(transpose_kernel, shape((BLOCK_FRAMES * HW, C), jnp.bfloat16), [VMEM])  1.81 us
    unnamed x5, local copies, waits for them, and re-layouts  1.54 us
  transfers between devices with their start and end apart: 1, of which 0 were waited for; matrix products, arithmetic and copies ran while one was open for 6% of the time, Pallas kernels for 13%

profile of v1, /device:TPU:0, one launch (start us, length us, event | category | flops | bytes accessed | tf_op | source)
XLA Modules:
  0.0 74.7 jit_solution(3593449572627455147)
XLA Ops:
  0.0 0.0 copy-start
  0.0 2.7 %shard_map.73 = bf16[1152,256]{1,0:T(8,128)(2,1)} custom-call(bf16[27,24,384]{2,1,0:T(8,128)(2,1)} %w_ref.1), custom_call_target="tpu_custom_call" | custom-call | tf_op jit(solution)/shard_map/pallas_call | solution.py:163
  2.7 7.4 %all-to-all-start = ((bf16[16,72,256]{2,1,0:T(8,128)(2,1)}), bf16[16,72,256]{2,1,0:T(8,128)(2,1)S(1)}, u32[]{:S(2)}, u32[]{:S(2)}) async-start(bf16[16,72,256]{2,1,0:T(8,128)(2,1)} %bitcast.10), calls=%async_computation | async-start | bytes 1179648 | tf_op jit(solution)/shard_map/all_to_all | solution.py:168
  10.1 1.4 %shard_map.74 = bf16[4,1536]{1,0:T(4,128)(2,1)} custom-call(bf16[16,384]{1,0:T(8,128)(2,1)} %x_ref.1), custom_call_target="tpu_custom_call" | custom-call | tf_op jit(solution)/shard_map/pallas_call | solution.py:156
  11.5 25.4 %all-gather = bf16[16,4,1536]{2,1,0:T(4,128)(2,1)S(1)} all-gather(bf16[1,4,1536]{2,1,0:T(4,128)(2,1)} %bitcast.14), channel_id=1, replica_groups=mesh['groups'=2,'tm'=16] {'tm'}, dimensions={0}, use_global_device_ids=true | all-gather | bytes 208896 | tf_op jit(solution)/shard_map/all_gather | solution.py:161
  36.8 0.7 reshape.29.lat_ref
  37.6 1.5 %reshape.30.bias_ref = f32[384,1]{1,0:T(8,128)} reshape(f32[384]{0:T(512)} %param.10) | data formatting | bytes 3072 | tf_op jit(solution)/shard_map/reshape | solution.py:183
  39.0 1.5 %reshape.31.gain_ref = f32[384,1]{1,0:T(8,128)} reshape(f32[384]{0:T(512)} %param.11) | data formatting | bytes 3072 | tf_op jit(solution)/shard_map/reshape | solution.py:184
  40.5 0.0 copy-done
  40.5 0.1 dynamic-slice_bitcast_fusion
  40.6 0.7 copy.14.bias_ref
  41.3 8.6 %shard_map.75 = (bf16[3072,768]{1,0:T(8,128)(2,1)}, f32[8,24,768]{2,1,0:T(8,128)}) custom-call(bf16[64,1536]{1,0:T(8,128)(2,1)} %reshape.29.lat_ref, bf16[432,384]{1,0:T(8,128)(2,1)} %bitcast.15, f32[384,1]{1,0:T(8,128)} %reshape.30.bias_ref, f32[384,1]{1,0:T(8,128)} %reshape.31.gain_ref, s32[1]{0:T(128)} %bitcast.4.first_ref), custom_call_target="tpu_custom_call" | custom-call | flops 2038431744 | bytes 20000000 | tf_op jit(solution)/shard_map/pallas_call | solution.py:169
  49.9 0.0 all-to-all-done
  49.9 0.0 copy-start.1
  49.9 0.8 %copy-done.1 = bf16[16,72,256]{2,1,0:T(8,128)(2,1)} copy-done((bf16[16,72,256]{2,1,0:T(8,128)(2,1)}, bf16[16,72,256]{2,1,0:T(8,128)(2,1)S(1)}, u32[]{:S(2)}) %copy-start.1) | copy-done | bytes 589848
  50.7 7.5 %shard_map.76 = bf16[384,384]{1,0:T(8,128)(2,1)} custom-call(bf16[1152,256]{1,0:T(8,128)(2,1)} %bitcast.12, bf16[3072,768]{1,0:T(8,128)(2,1)} %get-tuple-element.7.x_ref, f32[8,24,768]{2,1,0:T(8,128)} %get-tuple-element.8.stream_ref, f32[24,1]{1,0:T(8,128)} %copy.14.bias_ref, s32[8]{0:T(128)} %count_ref.1), custom_call_target="tpu_custom_call" | custom-call | flops 3057647616 | bytes 20000000 | tf_op jit(solution)/shard_map/pallas_call | solution.py:188
  58.2 14.8 %all_to_all.22 = bf16[16,24,384]{2,1,0:T(8,128)(2,1)} all-to-all(bf16[16,24,384]{2,1,0:T(8,128)(2,1)} %bitcast.13), channel_id=1, replica_groups=mesh['groups'=2,'tm'=16] {'tm'}, dimensions={0} | all-to-all | bytes 589824 | tf_op jit(solution)/shard_map/all_to_all | solution.py:196
  72.9 1.8 %shard_map.77 = bf16[384,384]{1,0:T(8,128)(2,1)} custom-call(bf16[384,384]{1,0:T(8,128)(2,1)} %bitcast.11), custom_call_target="tpu_custom_call" | custom-call | tf_op jit(solution)/shard_map/pallas_call | solution.py:197
Async XLA Ops:
  0.0 40.5 %copy-start = (f32[384]{0:T(512)S(1)}, f32[384]{0:T(512)}, u32[]{:S(2)}) copy-start(f32[384]{0:T(512)} %param.13) | copy-start | bytes 4612
  2.7 47.2 %all-to-all-start = ((bf16[16,72,256]{2,1,0:T(8,128)(2,1)}), bf16[16,72,256]{2,1,0:T(8,128)(2,1)S(1)}, u32[]{:S(2)}, u32[]{:S(2)}) async-start(bf16[16,72,256]{2,1,0:T(8,128)(2,1)} %bitcast.10), calls=%async_computation | async-start | bytes 1179648 | tf_op jit(solution)/shard_map/all_to_all | solution.py:168
  49.9 0.8 %copy-start.1 = (bf16[16,72,256]{2,1,0:T(8,128)(2,1)}, bf16[16,72,256]{2,1,0:T(8,128)(2,1)S(1)}, u32[]{:S(2)}) copy-start(bf16[16,72,256]{2,1,0:T(8,128)(2,1)S(1)} %all-to-all-done) | copy-start | bytes 1769476

commit v2 on v1

--- a/solution.py
+++ b/solution.py
@@ -17,7 +17,7 @@
 LANES = PROMPT_SAMPLES * HW
 VMEM = pl.BlockSpec(memory_space=pltpu.VMEM)
 SMEM = pl.BlockSpec(memory_space=pltpu.SMEM)
-LIMIT = 56 * 1024 * 1024
+ANY = pl.BlockSpec(memory_space=pl.ANY)
 
 
 def shift_mask(j, k):
@@ -40,13 +40,16 @@
     return x if delta == 0 else pltpu.roll(x, (-delta) % x.shape[1], 1)
 
 
-def latent_rows_kernel(x_ref, o_ref):
+def latent_rows_kernel(n, x_ref, o_ref):
     x = x_ref[...].astype(jnp.float32)
     rows = []
-    for c in range(x.shape[1] // HW):
-        pieces = [x[r : r + 1, c * HW : (c + 1) * HW] for r in range(x.shape[0])]
-        rows.append(jnp.concatenate(pieces, axis=1))
-    o_ref[...] = jnp.concatenate(rows, axis=0).astype(jnp.bfloat16)
+    for b in range(x.shape[0] // PROMPT_SAMPLES):
+        for c in range(x.shape[1] // HW):
+            at = b * PROMPT_SAMPLES
+            pieces = [x[r : r + 1, c * HW : (c + 1) * HW] for r in range(at, at + PROMPT_SAMPLES)]
+            rows.append(jnp.concatenate(pieces, axis=1))
+    rows = jnp.concatenate(rows, axis=0)
+    o_ref[...] = jnp.concatenate([rows] * n, axis=0).astype(jnp.bfloat16)
 
 
 def kernel_chunks_kernel(n, w_ref, o_ref):
@@ -63,54 +66,88 @@
         o_ref[d * 3 * own : (d + 2) * 3 * own, :] = jnp.concatenate(both, axis=0).astype(jnp.bfloat16)
 
 
-def active_kernel(frames, own, lat_ref, entry_ref, bias_ref, gain_ref, first_ref, x_ref, stream_ref, col_ref, s0_ref, s1_ref):
-    weight = jnp.transpose(entry_ref[...])
+def column(row_ref, width):
+    tile = jnp.transpose(jnp.broadcast_to(row_ref[...], (128, row_ref.shape[1])))
+    return jnp.concatenate([tile] * (width // 128), axis=1)
+
+
+def active_kernel(n, lat_ref, entry_ref, bias_ref, gain_ref, first_ref, x_hbm, stream_ref, col_ref, row_ref, x_ref, sem):
+    own = C // n
+    frames = n // PROMPT_SAMPLES * BLOCK_FRAMES
+    each = LATENT_CHANNELS * BLOCK_FRAMES // n
     taps = 9 * LATENT_CHANNELS
+    ahead = -(-own // 16) * 16
+    first = pl.multiple_of(first_ref[0], 8)
+    bias = column(bias_ref, LANES)
+    half_gain = (column(gain_ref, LANES) * 0.5).astype(jnp.bfloat16)
+    full = jnp.transpose(entry_ref[...].astype(jnp.float32))
+    row_ref[:, 0 : 3 * taps] = full
+    row_ref[:, 3 * taps : 3 * taps + 128] = bias[:, 0:128]
+    mine = row_ref[pl.ds(first, own), :]
+    mine_bias = mine[:, 3 * taps : 3 * taps + 128]
+    mine_bias = jnp.concatenate([mine_bias] * (LANES // 128), axis=1)
+    spare = jnp.zeros((ahead - own, 3 * taps), jnp.float32)
+    weight = jnp.concatenate([mine[:, : 3 * taps], spare, full], axis=0).astype(jnp.bfloat16)
+    per_frame = LATENT_CHANNELS // each
+    blocks = n // PROMPT_SAMPLES
+    lats = lat_ref[...].astype(jnp.float32).reshape(BLOCK_FRAMES, per_frame, blocks, each, LANES)
+    copies = []
     for f in range(frames):
         b, g = divmod(f, BLOCK_FRAMES)
-        lat = lat_ref[g * LATENT_CHANNELS : (g + 1) * LATENT_CHANNELS, b * LANES : (b + 1) * LANES].astype(jnp.float32)
+        lat = lats[g, :, b].reshape(LATENT_CHANNELS, LANES)
         for j in range(3):
             for k in range(3):
                 moved = shifted(lat, LATENT_COLUMNS * (j - 1) + k - 1)
                 moved = jnp.where(shift_mask(j, k), moved, 0.0)
                 at = f * taps + (3 * j + k) * LATENT_CHANNELS
                 col_ref[at : at + LATENT_CHANNELS, :] = moved.astype(jnp.bfloat16)
-    bias = bias_ref[...]
-    gain = gain_ref[...]
-    first = pl.multiple_of(first_ref[0], 8)
-    for f in range(frames):
-        s_ref = (s0_ref, s1_ref)[f % 2]
         least = max(f - 2, 0)
-        s = jnp.dot(
+        z = jnp.dot(
             weight[:, (2 - (f - least)) * taps :],
             col_ref[least * taps : (f + 1) * taps, :],
             preferred_element_type=jnp.float32,
         )
-        s = (s + bias).astype(jnp.bfloat16).astype(jnp.float32)
-        s_ref[...] = s
+        stream_ref[f] = (z[:own] + mine_bias).astype(jnp.bfloat16).astype(jnp.float32)
+        s = z[ahead:] + bias
         scale = lax.rsqrt(jnp.sum(s * s, axis=0, keepdims=True) * (1.0 / C) + 1e-06)
-        half = s_ref[...] * (scale * 0.5) * gain
-        x_ref[f * C : (f + 1) * C, :] = (half + half * jnp.tanh(half)).astype(jnp.bfloat16)
-        stream_ref[f] = s_ref[pl.ds(first, own), :]
-
-
-def branch_kernel(frames, n, w_ref, x_ref, stream_ref, bias_ref, count_ref, o_ref, out_ref):
+        half = s.astype(jnp.bfloat16) * half_gain * scale.astype(jnp.bfloat16)
+        x_ref[f * C : (f + 1) * C, :] = half + half * jnp.tanh(half)
+        rows = pl.ds(f * C, C)
+        copy = pltpu.make_async_copy(x_ref.at[rows], x_hbm.at[rows], sem.at[f])
+        copy.start()
+        copies.append(copy)
+    for copy in copies:
+        copy.wait()
+
+
+def branch_kernel(n, w_ref, x_hbm, stream_ref, bias_ref, first_ref, count_ref, o_ref, x_ref, bias_col_ref, out_ref, sem):
     own = C // n
+    frames = n // PROMPT_SAMPLES * BLOCK_FRAMES
+    copies = []
+    for f in range(frames):
+        rows = pl.ds(f * C, C)
+        copy = pltpu.make_async_copy(x_hbm.at[rows], x_ref.at[rows], sem.at[f])
+        copy.start()
+        copies.append(copy)
     w = w_ref[...].astype(jnp.float32).reshape(n, 3, own, w_ref.shape[1])
     w = jnp.transpose(w, (1, 0, 2, 3)).reshape(3 * C, w_ref.shape[1])
-    weight = jnp.transpose(w.astype(jnp.bfloat16))
+    weight = jnp.transpose(w.astype(jnp.bfloat16))[: -(-9 * own // 16) * 16]
+    bias_col_ref[...] = column(bias_ref, 128)
+    bias = bias_col_ref[pl.ds(pl.multiple_of(first_ref[0], 8), own), :]
+    bias = jnp.concatenate([bias] * (LANES // 128), axis=1)
     lane = lax.broadcasted_iota(jnp.int32, (1, LANES), 1)
     count = jnp.zeros((1, LANES), jnp.int32)
     for s in range(PROMPT_SAMPLES):
         count = jnp.where(lane // HW == s, count_ref[s], count)
     for f in range(frames):
+        copies[f].wait()
         least = max(f - 2, 0)
         z = jnp.dot(
             weight[:, (2 - (f - least)) * C :],
             x_ref[least * C : (f + 1) * C, :],
             preferred_element_type=jnp.float32,
         )
-        total = stream_ref[f] + bias_ref[...]
+        total = stream_ref[f] + bias
         for k in range(3):
             part = None
             for j in range(3):
@@ -122,28 +159,29 @@
                 part = jnp.where(shift_mask(1, k), shifted(part, k - 1), 0.0)
             total = total + part
         out_ref[f] = jnp.where(count > f, total, 0.0)
-    for b in range(frames // BLOCK_FRAMES):
-        parts = [out_ref[b * BLOCK_FRAMES + g] for g in range(BLOCK_FRAMES)]
-        for s in range(0, PROMPT_SAMPLES, 2):
-            both = [
-                jnp.concatenate([p[:, t * HW : (t + 1) * HW] for p in parts], axis=1) for t in (s, s + 1)
-            ]
-            at = (b * PROMPT_SAMPLES + s) * own
-            o_ref[at : at + 2 * own, :] = jnp.concatenate(both, axis=0).astype(jnp.bfloat16)
+        b, g = divmod(f, BLOCK_FRAMES)
+        if g == BLOCK_FRAMES - 1:
+            parts = [out_ref[b * BLOCK_FRAMES + t] for t in range(BLOCK_FRAMES)]
+            for s in range(0, PROMPT_SAMPLES, 2):
+                both = [
+                    jnp.concatenate([p[:, t * HW : (t + 1) * HW] for p in parts], axis=1) for t in (s, s + 1)
+                ]
+                at = (b * PROMPT_SAMPLES + s) * own
+                o_ref[at : at + 2 * own, :] = jnp.concatenate(both, axis=0).astype(jnp.bfloat16)
 
 
 def transpose_kernel(x_ref, o_ref):
     o_ref[...] = jnp.transpose(x_ref[...])
 
 
-def call(body, out, specs, scratch=(), flops=0, moved=0):
+def call(body, out, ins, outs, scratch=(), flops=0, moved=0, limit=8):
     return pl.pallas_call(
         body,
         out_shape=out,
-        in_specs=specs,
-        out_specs=jax.tree.map(lambda _: VMEM, out),
+        in_specs=ins,
+        out_specs=outs,
         scratch_shapes=list(scratch),
-        compiler_params=pltpu.CompilerParams(vmem_limit_bytes=LIMIT),
+        compiler_params=pltpu.CompilerParams(vmem_limit_bytes=limit * 1024 * 1024),
         cost_estimate=pl.CostEstimate(flops=flops, bytes_accessed=moved, transcendentals=0),
     )
 
@@ -151,50 +189,57 @@
 def by_channel(n, latents, counts, entry_kernel, entry_bias, gain, kernel, bias):
     own = C // n
     frames = n // PROMPT_SAMPLES * BLOCK_FRAMES
-    first = (lax.axis_index("tm") * own).astype(jnp.int32)
+    first = (lax.axis_index("tm") * own).astype(jnp.int32).reshape(1)
     shape = jax.ShapeDtypeStruct
+    bf16, f32 = jnp.bfloat16, jnp.float32
+    each = latents.shape[1] // HW * (n // PROMPT_SAMPLES)
     rows = call(
-        latent_rows_kernel,
-        shape((latents.shape[1] // HW, n * HW), jnp.bfloat16),
-        [VMEM],
+        functools.partial(latent_rows_kernel, n), shape((n * each, LANES), bf16), [VMEM], VMEM
     )(latents)
-    rows = lax.all_gather(rows, "tm", axis=0, tiled=True)
+    rows = lax.all_to_all(rows, "tm", split_axis=0, concat_axis=0, tiled=True)
     width = -(-9 * own // 128) * 128
     chunks = call(
-        functools.partial(kernel_chunks_kernel, n),
-        shape((n * 3 * own, width), jnp.bfloat16),
-        [VMEM],
+        functools.partial(kernel_chunks_kernel, n), shape((n * 3 * own, width), bf16), [VMEM], VMEM
     )(kernel)
     chunks = lax.all_to_all(chunks, "tm", split_axis=0, concat_axis=0, tiled=True)
     active, stream = call(
-        functools.partial(active_kernel, frames, own),
-        (shape((frames * C, LANES), jnp.bfloat16), shape((frames, own, LANES), jnp.float32)),
+        functools.partial(active_kernel, n),
+        (shape((frames * C, LANES), bf16), shape((frames, own, LANES), f32)),
         [VMEM, VMEM, VMEM, VMEM, SMEM],
+        (ANY, VMEM),
         [
-            pltpu.VMEM((frames * 9 * LATENT_CHANNELS, LANES), jnp.bfloat16),
-            pltpu.VMEM((C, LANES), jnp.float32),
-            pltpu.VMEM((C, LANES), jnp.float32),
+            pltpu.VMEM((frames * 9 * LATENT_CHANNELS, LANES), bf16),
+            pltpu.VMEM((C, 27 * LATENT_CHANNELS + 128), f32),
+            pltpu.VMEM((frames * C, LANES), bf16),
+            pltpu.SemaphoreType.DMA((frames,)),
         ],
         flops=2 * frames * LANES * 432 * C,
         moved=20_000_000,
+        limit=32,
     )(
         rows,
         entry_kernel.reshape(27 * LATENT_CHANNELS, C),
-        entry_bias.reshape(C, 1),
-        gain.reshape(C, 1),
-        first.reshape(1),
-    )
-    own_bias = lax.dynamic_slice(bias, (first,), (own,)).reshape(own, 1)
+        entry_bias.reshape(1, C),
+        gain.reshape(1, C),
+        first,
+    )
     out = call(
-        functools.partial(branch_kernel, frames, n),
-        shape((n * own, BLOCK_FRAMES * HW), jnp.bfloat16),
-        [VMEM, VMEM, VMEM, VMEM, SMEM],
-        [pltpu.VMEM((frames, own, LANES), jnp.float32)],
+        functools.partial(branch_kernel, n),
+        shape((n * own, BLOCK_FRAMES * HW), bf16),
+        [VMEM, ANY, VMEM, VMEM, SMEM, SMEM],
+        VMEM,
+        [
+            pltpu.VMEM((frames * C, LANES), bf16),
+            pltpu.VMEM((C, 128), f32),
+            pltpu.VMEM((frames, own, LANES), f32),
+            pltpu.SemaphoreType.DMA((frames,)),
+        ],
         flops=2 * frames * LANES * 27 * C * own,
         moved=20_000_000,
-    )(chunks, active, stream, own_bias, counts)
+        limit=32,
+    )(chunks, active, stream, bias.reshape(1, C), first, counts)
     out = lax.all_to_all(out, "tm", split_axis=0, concat_axis=0, tiled=True)
-    out = call(transpose_kernel, shape((BLOCK_FRAMES * HW, C), jnp.bfloat16), [VMEM])(out)
+    out = call(transpose_kernel, shape((BLOCK_FRAMES * HW, C), bf16), [VMEM], VMEM)(out)
     return out.reshape(BLOCK_FRAMES, LATENT_ROWS, LATENT_COLUMNS, C)
 
 

time: 75.2 us -> 64.1 us (0.85)
  blocking collectives: 40.1 us -> 14.7 us
  waiting for transfers between devices: 0.01 us -> 9.25 us
  local copies, waits for them, and re-layouts: 5.23 us -> 9.24 us
  starting transfers between devices: 7.39 us -> 11 us
  Pallas kernels: 22 us -> 19.3 us
    all_gather x1 -> x0, blocking collectives: 25.4 us -> none  [by_channel(): rows = lax.all_gather(rows, 'tm', axis=0, tiled=True)]
    all_to_all x0 -> x1, starting transfers between devices: none -> 7.39 us  [by_channel(): rows = lax.all_to_all(rows, 'tm', split_axis=0, concat_axis=0, tiled=True)]
    all_to_all x0 -> x1, waiting for transfers between devices: none -> 6.32 us  [by_channel(): rows = lax.all_to_all(rows, 'tm', split_axis=0, concat_axis=0, tiled=True)]
    unnamed x5 -> x12, local copies, waits for them, and re-layouts: 1.54 us -> 7.18 us
    all_to_all x1, starting transfers between devices: 7.39 us -> 3.58 us  [by_channel(): lax.all_to_all(chunks, 'tm', split_axis=0, concat_axis=0, tiled=True)]
    all_to_all x1, waiting for transfers between devices: 0.01 us -> 2.93 us  [by_channel(): lax.all_to_all(chunks, 'tm', split_axis=0, concat_axis=0, tiled=True)]
    pallas_call x4, Pallas kernels: 19.3 us -> 17.7 us  [the longest x1 8.63 us: by_channel(): call(functools.partial(branch_kernel, n), shape((n * own, BLOCK_FRAMES *...]
    reshape x4 -> x3, local copies, waits for them, and re-layouts: 3.69 us -> 2.05 us  [the longest x1 0.69 us: by_channel(): entry_bias.reshape(1, C)]
  transfers between devices with their start and end apart: 1 -> 2, of which waited for: 0 -> 2; matrix products, arithmetic and copies ran while one was open for 6% -> 3% of each run, Pallas kernels for 13% -> 14%
where the time goes in v2:
time: 64.1 us; the launch traced here: 63.6 us
  Pallas kernels  19.3 us (30%)
  blocking collectives  14.7 us (23%)
  starting transfers between devices  11 us (17%)
  waiting for transfers between devices  9.25 us (14%)
  local copies, waits for them, and re-layouts  9.24 us (14%)
    all_to_all x1, blocking collectives, by_channel(): out = lax.all_to_all(out, 'tm', split_axis=0, concat_axis=0, tiled=True)  14.7 us
    pallas_call x1, Pallas kernels, by_channel(): call(functools.partial(branch_kernel, n), shape((n * own, BLOCK_FRAMES *...  8.63 us
    pallas_call x1, Pallas kernels, by_channel(): call(functools.partial(active_kernel, n), (shape((frames * C, LANES), bf1...  7.4 us
    all_to_all x1, starting transfers between devices, by_channel(): rows = lax.all_to_all(rows, 'tm', split_axis=0, concat_axis=0, tiled=True)  7.39 us
    unnamed x12, local copies, waits for them, and re-layouts  7.18 us
    all_to_all x1, waiting for transfers between devices, by_channel(): rows = lax.all_to_all(rows, 'tm', split_axis=0, concat_axis=0, tiled=True)  6.32 us
    all_to_all x1, starting transfers between devices, by_channel(): lax.all_to_all(chunks, 'tm', split_axis=0, concat_axis=0, tiled=True)  3.58 us
    all_to_all x1, waiting for transfers between devices, by_channel(): lax.all_to_all(chunks, 'tm', split_axis=0, concat_axis=0, tiled=True)  2.93 us
  transfers between devices with their start and end apart: 2, of which 2 were waited for; matrix products, arithmetic and copies ran while one was open for 3% of the time, Pallas kernels for 14%

profile of v2, /device:TPU:0, one launch (start us, length us, event | category | flops | bytes accessed | tf_op | source)
XLA Modules:
  0.0 63.6 jit_solution(2567506282234333989)
XLA Ops:
  0.0 0.0 copy-start.1
  0.0 0.7 %copy-done.1 = bf16[16,384]{1,0:T(8,128)(2,1)S(1)} copy-done((bf16[16,384]{1,0:T(8,128)(2,1)S(1)}, bf16[16,384]{1,0:T(8,128)(2,1)}, u32[]{:S(2)}) %copy-start.1) | copy-done | bytes 12312
  0.7 0.8 %shard_map.74 = bf16[128,768]{1,0:T(8,128)(2,1)} custom-call(bf16[16,384]{1,0:T(8,128)(2,1)S(1)} %copy-done.1), custom_call_target="tpu_custom_call" | custom-call | tf_op jit(solution)/shard_map/pallas_call | solution.py:196
  1.5 7.4 %all-to-all-start.1 = ((bf16[16,8,768]{2,1,0:T(8,128)(2,1)}), bf16[16,8,768]{2,1,0:T(8,128)(2,1)S(1)}, u32[]{:S(2)}, u32[]{:S(2)}) async-start(bf16[16,8,768]{2,1,0:T(8,128)(2,1)} %bitcast.2), calls=%async_computation.1 | async-start | bytes 393216 | tf_op jit(solution)/shard_map/all_to_all | solution.py:199
  8.9 0.0 copy-start
  8.9 1.0 %copy-done = bf16[27,24,384]{2,1,0:T(8,128)(2,1)S(1)} copy-done((bf16[27,24,384]{2,1,0:T(8,128)(2,1)S(1)}, bf16[27,24,384]{2,1,0:T(8,128)(2,1)}, u32[]{:S(2)}) %copy-start) | copy-done | bytes 497688
  9.9 0.0 copy-start.3
  9.9 1.6 %shard_map.73 = bf16[1152,256]{1,0:T(8,128)(2,1)} custom-call(bf16[27,24,384]{2,1,0:T(8,128)(2,1)S(1)} %copy-done), custom_call_target="tpu_custom_call" | custom-call | tf_op jit(solution)/shard_map/pallas_call | solution.py:201
  11.6 6.3 %all-to-all-done.1 = bf16[16,8,768]{2,1,0:T(8,128)(2,1)S(1)} async-done(((bf16[16,8,768]{2,1,0:T(8,128)(2,1)}), bf16[16,8,768]{2,1,0:T(8,128)(2,1)S(1)}, u32[]{:S(2)}, u32[]{:S(2)}) %all-to-all-start.1) | async-done | bytes 196640 | tf_op jit(solution)/shard_map/all_to_all | solution.py:199
  17.9 3.6 %all-to-all-start = ((bf16[16,72,256]{2,1,0:T(8,128)(2,1)}), bf16[16,72,256]{2,1,0:T(8,128)(2,1)S(1)}, u32[]{:S(2)}, u32[]{:S(2)}) async-start(bf16[16,72,256]{2,1,0:T(8,128)(2,1)} %bitcast), calls=%async_computation | async-start | bytes 1179648 | tf_op jit(solution)/shard_map/all_to_all | solution.py:204
  21.5 0.7 %reshape.25.bias_ref = f32[1,384]{1,0:T(1,128)S(1)} reshape(f32[384]{0:T(512)} %param.10) | data formatting | bytes 3072 | tf_op jit(solution)/shard_map/reshape | solution.py:222
  22.2 0.7 %reshape.26.gain_ref = f32[1,384]{1,0:T(1,128)S(1)} reshape(f32[384]{0:T(512)} %param.11) | data formatting | bytes 3072 | tf_op jit(solution)/shard_map/reshape | solution.py:223
  22.9 0.7 %reshape.28.bias_ref = f32[1,384]{1,0:T(1,128)S(1)} reshape(f32[384]{0:T(512)} %param.13) | data formatting | bytes 3072 | tf_op jit(solution)/shard_map/reshape | solution.py:240
  23.5 0.0 copy-start.2
  23.5 1.0 %copy-done.2 = bf16[27,16,384]{2,1,0:T(8,128)(2,1)S(1)} copy-done((bf16[27,16,384]{2,1,0:T(8,128)(2,1)S(1)}, bf16[27,16,384]{2,1,0:T(8,128)(2,1)}, u32[]{:S(2)}) %copy-start.2) | copy-done | bytes 331800
  24.5 7.4 %shard_map.75 = (bf16[3072,768]{1,0:T(8,128)(2,1)S(1)}, f32[8,24,768]{2,1,0:T(8,128)S(1)}) custom-call(bf16[128,768]{1,0:T(8,128)(2,1)S(1)} %bitcast.12, bf16[432,384]{1,0:T(8,128)(2,1)S(1)} %bitcast.13, f32[1,384]{1,0:T(1,128)S(1)} %reshape.25.bias_ref, f32[1,384]{1,0:T(1,128)S(1)} %reshape.26.gain_ref, s32[1]{0:T(128)} %bitcast.5.first_ref), custom_call_target="tpu_custom_call" | custom-call | flops 2038431744 | bytes 20000000 | tf_op jit(solution)/shard_map/pallas_call | solution.py:205
  31.9 0.0 copy-start.4
  31.9 2.1 %copy-done.4 = bf16[3072,768]{1,0:T(8,128)(2,1)} copy-done((bf16[3072,768]{1,0:T(8,128)(2,1)}, bf16[3072,768]{1,0:T(8,128)(2,1)S(1)}, u32[]{:S(2)}) %copy-start.4) | copy-done | bytes 4718616
  34.1 2.9 %all-to-all-done = bf16[16,72,256]{2,1,0:T(8,128)(2,1)S(1)} async-done(((bf16[16,72,256]{2,1,0:T(8,128)(2,1)}), bf16[16,72,256]{2,1,0:T(8,128)(2,1)S(1)}, u32[]{:S(2)}, u32[]{:S(2)}) %all-to-all-start) | async-done | bytes 589856 | tf_op jit(solution)/shard_map/all_to_all | solution.py:204
  37.0 0.0 copy-done.3
  37.0 2.3 %copy-done.5 = bf16[3072,768]{1,0:T(8,128)(2,1)S(1)} copy-done((bf16[3072,768]{1,0:T(8,128)(2,1)S(1)}, bf16[3072,768]{1,0:T(8,128)(2,1)}, u32[]{:S(2)}) %copy-start.5) | copy-done | bytes 4718616
  39.3 8.6 %shard_map.76 = bf16[384,384]{1,0:T(8,128)(2,1)S(1)} custom-call(bf16[1152,256]{1,0:T(8,128)(2,1)S(1)} %bitcast.10, bf16[3072,768]{1,0:T(8,128)(2,1)S(1)} %copy-done.5, f32[8,24,768]{2,1,0:T(8,128)S(1)} %get-tuple-element.8.stream_ref, f32[1,384]{1,0:T(1,128)S(1)} %reshape.28.bias_ref, s32[1]{0:T(128)} %bitcast.5.first_ref, s32[8]{0:T(128)S(1)} %copy-done.3), custom_call_target="tpu_custom_call" | custom-call | flops 3057647616 | bytes 20000000 | tf_op jit(solution)/shard_map/pallas_call | solution.py:226
  48.0 14.7 %all_to_all.33 = bf16[16,24,384]{2,1,0:T(8,128)(2,1)S(1)} all-to-all(bf16[16,24,384]{2,1,0:T(8,128)(2,1)S(1)} %bitcast.11), channel_id=1, replica_groups=mesh['groups'=2,'tm'=16] {'tm'}, dimensions={0} | all-to-all | bytes 589824 | tf_op jit(solution)/shard_map/all_to_all | solution.py:241
  62.7 0.9 %shard_map.77 = bf16[384,384]{1,0:T(8,128)(2,1)} custom-call(bf16[384,384]{1,0:T(8,128)(2,1)S(1)} %bitcast.9), custom_call_target="tpu_custom_call" | custom-call | tf_op jit(solution)/shard_map/pallas_call | solution.py:242
  (1 shorter events, 0.0 us)
Async XLA Ops:
  0.0 0.7 %copy-start.1 = (bf16[16,384]{1,0:T(8,128)(2,1)S(1)}, bf16[16,384]{1,0:T(8,128)(2,1)}, u32[]{:S(2)}) copy-start(bf16[16,384]{1,0:T(8,128)(2,1)} %x_ref.1) | copy-start | bytes 36868
  1.5 16.4 %all-to-all-start.1 = ((bf16[16,8,768]{2,1,0:T(8,128)(2,1)}), bf16[16,8,768]{2,1,0:T(8,128)(2,1)S(1)}, u32[]{:S(2)}, u32[]{:S(2)}) async-start(bf16[16,8,768]{2,1,0:T(8,128)(2,1)} %bitcast.2), calls=%async_computation.1 | async-start | bytes 393216 | tf_op jit(solution)/shard_map/all_to_all | solution.py:199
  8.9 1.0 %copy-start = (bf16[27,24,384]{2,1,0:T(8,128)(2,1)S(1)}, bf16[27,24,384]{2,1,0:T(8,128)(2,1)}, u32[]{:S(2)}) copy-start(bf16[27,24,384]{2,1,0:T(8,128)(2,1)} %w_ref.1) | copy-start | bytes 1492996
  9.9 27.1 %copy-start.3 = (s32[8]{0:T(128)S(1)}, s32[8]{0:T(128)}, u32[]{:S(2)}) copy-start(s32[8]{0:T(128)} %count_ref.1) | copy-start | bytes 100
  17.9 19.1 %all-to-all-start = ((bf16[16,72,256]{2,1,0:T(8,128)(2,1)}), bf16[16,72,256]{2,1,0:T(8,128)(2,1)S(1)}, u32[]{:S(2)}, u32[]{:S(2)}) async-start(bf16[16,72,256]{2,1,0:T(8,128)(2,1)} %bitcast), calls=%async_computation | async-start | bytes 1179648 | tf_op jit(solution)/shard_map/all_to_all | solution.py:204
  23.5 1.0 %copy-start.2 = (bf16[27,16,384]{2,1,0:T(8,128)(2,1)S(1)}, bf16[27,16,384]{2,1,0:T(8,128)(2,1)}, u32[]{:S(2)}) copy-start(bf16[27,16,384]{2,1,0:T(8,128)(2,1)} %param.9) | copy-start | bytes 995332
  31.9 2.1 %copy-start.4 = (bf16[3072,768]{1,0:T(8,128)(2,1)}, bf16[3072,768]{1,0:T(8,128)(2,1)S(1)}, u32[]{:S(2)}) copy-start(bf16[3072,768]{1,0:T(8,128)(2,1)S(1)} %get-tuple-element.7.x_hbm) | copy-start | bytes 14155780
  37.0 2.3 %copy-start.5 = (bf16[3072,768]{1,0:T(8,128)(2,1)S(1)}, bf16[3072,768]{1,0:T(8,128)(2,1)}, u32[]{:S(2)}) copy-start(bf16[3072,768]{1,0:T(8,128)(2,1)} %copy-done.4) | copy-start | bytes 14155780

commit v3 on v2

--- a/solution.py
+++ b/solution.py
@@ -40,7 +40,8 @@
     return x if delta == 0 else pltpu.roll(x, (-delta) % x.shape[1], 1)
 
 
-def latent_rows_kernel(n, x_ref, o_ref):
+def parcels_kernel(n, x_ref, w_ref, side_ref, o_ref):
+    own = C // n
     x = x_ref[...].astype(jnp.float32)
     rows = []
     for b in range(x.shape[0] // PROMPT_SAMPLES):
@@ -49,21 +50,19 @@
             pieces = [x[r : r + 1, c * HW : (c + 1) * HW] for r in range(at, at + PROMPT_SAMPLES)]
             rows.append(jnp.concatenate(pieces, axis=1))
     rows = jnp.concatenate(rows, axis=0)
-    o_ref[...] = jnp.concatenate([rows] * n, axis=0).astype(jnp.bfloat16)
-
-
-def kernel_chunks_kernel(n, w_ref, o_ref):
-    own = C // n
+    tiles = [rows[:, t * 128 : (t + 1) * 128] for t in range(LANES // 128)]
     w = w_ref[...].astype(jnp.float32).reshape(3, 9, own, C)
     taps = [w[:, t].reshape(3 * own, C) for t in range(9)]
-    pad = o_ref.shape[1] - 9 * own
+    left = jnp.broadcast_to(side_ref[0] == 0, (3 * own, 128))
     for d in range(0, n, 2):
         both = []
         for e in (d, d + 1):
             pieces = [tap[:, e * own : (e + 1) * own] for tap in taps]
-            pieces.append(jnp.zeros((3 * own, pad), jnp.float32))
-            both.append(jnp.concatenate(pieces, axis=1))
-        o_ref[d * 3 * own : (d + 2) * 3 * own, :] = jnp.concatenate(both, axis=0).astype(jnp.bfloat16)
+            pieces.append(jnp.zeros((3 * own, 256 - 9 * own), jnp.float32))
+            share = jnp.concatenate(pieces, axis=1)
+            both += [jnp.where(left, share[:, :128], share[:, 128:])] + tiles
+        both = jnp.concatenate(both, axis=0).astype(jnp.bfloat16)
+        o_ref[d // 2 * both.shape[0] : (d // 2 + 1) * both.shape[0], :] = both
 
 
 def column(row_ref, width):
@@ -71,7 +70,7 @@
     return jnp.concatenate([tile] * (width // 128), axis=1)
 
 
-def active_kernel(n, lat_ref, entry_ref, bias_ref, gain_ref, first_ref, x_hbm, stream_ref, col_ref, row_ref, x_ref, sem):
+def active_kernel(n, got_ref, entry_ref, bias_ref, gain_ref, first_ref, x_hbm, stream_ref, col_ref, row_ref, x_ref, sem):
     own = C // n
     frames = n // PROMPT_SAMPLES * BLOCK_FRAMES
     each = LATENT_CHANNELS * BLOCK_FRAMES // n
@@ -90,7 +89,10 @@
     weight = jnp.concatenate([mine[:, : 3 * taps], spare, full], axis=0).astype(jnp.bfloat16)
     per_frame = LATENT_CHANNELS // each
     blocks = n // PROMPT_SAMPLES
-    lats = lat_ref[...].astype(jnp.float32).reshape(BLOCK_FRAMES, per_frame, blocks, each, LANES)
+    lats = got_ref[...].astype(jnp.float32).reshape(n, -1, 128)[:, 3 * own :]
+    lats = lats.reshape(n, LANES // 128, blocks * each, 128)
+    lats = jnp.concatenate([lats[:, t] for t in range(LANES // 128)], axis=2)
+    lats = lats.reshape(BLOCK_FRAMES, per_frame, blocks, each, LANES)
     copies = []
     for f in range(frames):
         b, g = divmod(f, BLOCK_FRAMES)
@@ -120,7 +122,7 @@
         copy.wait()
 
 
-def branch_kernel(n, w_ref, x_hbm, stream_ref, bias_ref, first_ref, count_ref, o_ref, x_ref, bias_col_ref, out_ref, sem):
+def branch_kernel(n, got_ref, w_ref, x_hbm, stream_ref, bias_ref, first_ref, side_ref, count_ref, o_ref, x_ref, bias_col_ref, out_ref, sem):
     own = C // n
     frames = n // PROMPT_SAMPLES * BLOCK_FRAMES
     copies = []
@@ -129,8 +131,11 @@
         copy = pltpu.make_async_copy(x_hbm.at[rows], x_ref.at[rows], sem.at[f])
         copy.start()
         copies.append(copy)
-    w = w_ref[...].astype(jnp.float32).reshape(n, 3, own, w_ref.shape[1])
-    w = jnp.transpose(w, (1, 0, 2, 3)).reshape(3 * C, w_ref.shape[1])
+    mine = got_ref[...].astype(jnp.float32).reshape(n, -1, 128)[:, : 3 * own].reshape(n, 3, own, 128)
+    other = w_ref[...].astype(jnp.float32).reshape(n, 3, own, 128)
+    left = jnp.broadcast_to(side_ref[0] == 0, other.shape)
+    w = jnp.concatenate([jnp.where(left, mine, other), jnp.where(left, other, mine)], axis=3)
+    w = jnp.transpose(w, (1, 0, 2, 3)).reshape(3 * C, 256)
     weight = jnp.transpose(w.astype(jnp.bfloat16))[: -(-9 * own // 16) * 16]
     bias_col_ref[...] = column(bias_ref, 128)
     bias = bias_col_ref[pl.ds(pl.multiple_of(first_ref[0], 8), own), :]
@@ -192,16 +197,15 @@
     first = (lax.axis_index("tm") * own).astype(jnp.int32).reshape(1)
     shape = jax.ShapeDtypeStruct
     bf16, f32 = jnp.bfloat16, jnp.float32
+    side = lax.axis_index("groups").astype(jnp.int32).reshape(1)
     each = latents.shape[1] // HW * (n // PROMPT_SAMPLES)
-    rows = call(
-        functools.partial(latent_rows_kernel, n), shape((n * each, LANES), bf16), [VMEM], VMEM
-    )(latents)
-    rows = lax.all_to_all(rows, "tm", split_axis=0, concat_axis=0, tiled=True)
-    width = -(-9 * own // 128) * 128
-    chunks = call(
-        functools.partial(kernel_chunks_kernel, n), shape((n * 3 * own, width), bf16), [VMEM], VMEM
-    )(kernel)
-    chunks = lax.all_to_all(chunks, "tm", split_axis=0, concat_axis=0, tiled=True)
+    height = 3 * own + each * LANES // 128
+    parcels = call(
+        functools.partial(parcels_kernel, n), shape((n * height, 128), bf16), [VMEM, VMEM, SMEM], VMEM
+    )(latents, kernel, side)
+    got = lax.all_to_all(parcels, "tm", split_axis=0, concat_axis=0, tiled=True)
+    other = got.reshape(n, height, 128)[:, : 3 * own].reshape(n * 3 * own, 128)
+    other = lax.ppermute(other, "groups", [(0, 1), (1, 0)])
     active, stream = call(
         functools.partial(active_kernel, n),
         (shape((frames * C, LANES), bf16), shape((frames, own, LANES), f32)),
@@ -217,7 +221,7 @@
         moved=20_000_000,
         limit=32,
     )(
-        rows,
+        got,
         entry_kernel.reshape(27 * LATENT_CHANNELS, C),
         entry_bias.reshape(1, C),
         gain.reshape(1, C),
@@ -226,7 +230,7 @@
     out = call(
         functools.partial(branch_kernel, n),
         shape((n * own, BLOCK_FRAMES * HW), bf16),
-        [VMEM, ANY, VMEM, VMEM, SMEM, SMEM],
+        [VMEM, VMEM, ANY, VMEM, VMEM, SMEM, SMEM, SMEM],
         VMEM,
         [
             pltpu.VMEM((frames * C, LANES), bf16),
@@ -237,7 +241,7 @@
         flops=2 * frames * LANES * 27 * C * own,
         moved=20_000_000,
         limit=32,
-    )(chunks, active, stream, bias.reshape(1, C), first, counts)
+    )(got, other, active, stream, bias.reshape(1, C), first, side, counts)
     out = lax.all_to_all(out, "tm", split_axis=0, concat_axis=0, tiled=True)
     out = call(transpose_kernel, shape((BLOCK_FRAMES * HW, C), bf16), [VMEM], VMEM)(out)
     return out.reshape(BLOCK_FRAMES, LATENT_ROWS, LATENT_COLUMNS, C)
@@ -324,7 +328,8 @@
 def solution(mesh):
     n = mesh.shape["tm"]
     cells = BLOCK_FRAMES * LATENT_CHANNELS * HW
-    whole_rows = cells % (n * HW) == 0 and C % n == 0 and (C // n) % 8 == 0 and n % PROMPT_SAMPLES == 0
+    fits = mesh.shape["groups"] == 2 and 9 * (C // n) <= 256 and n * HW % 128 == 0
+    whole_rows = fits and cells % (n * HW) == 0 and C % n == 0 and (C // n) % 8 == 0 and n % PROMPT_SAMPLES == 0
     body = functools.partial(by_channel, n) if whole_rows else by_block
     in_specs = (P("groups", "tm"), P("groups"), P(), P(), P(), P(None, "tm", None), P())
     out_specs = P(("groups", "tm"), None, None, None)

time: 64.1 us -> 60 us (0.936)
  blocking collectives: 14.7 us -> 35.4 us
  starting transfers between devices: 11 us -> 1.56 us
  waiting for transfers between devices: 9.25 us -> 0.01 us
  local copies, waits for them, and re-layouts: 9.24 us -> 4.79 us
  Pallas kernels: 19.3 us -> 17.7 us
    all_to_all x0 -> x1, blocking collectives: none -> 21 us  [by_channel(): got = lax.all_to_all(parcels, 'tm', split_axis=0, concat_axis=0, tiled=True)]
    all_to_all x2 -> x0, starting transfers between devices: 11 us -> none  [the longest x1 7.39 us: by_channel(): rows = lax.all_to_all(rows, 'tm', split_axis=0, concat_axis=0, tiled=True)]
    all_to_all x2 -> x0, waiting for transfers between devices: 9.25 us -> none  [the longest x1 6.32 us: by_channel(): rows = lax.all_to_all(rows, 'tm', split_axis=0, concat_axis=0, tiled=True)]
    unnamed x12 -> x8, local copies, waits for them, and re-layouts: 7.18 us -> 2.72 us
    pallas_call x2 -> x1, Pallas kernels: 2.43 us -> 0.85 us  [by_channel(): call(functools.partial(parcels_kernel, n), shape((n * height, 128), bf16)...]
    ppermute x0 -> x1, starting transfers between devices: none -> 1.56 us  [by_channel(): other = lax.ppermute(other, 'groups', [(0, 1), (1, 0)])]
  transfers between devices with their start and end apart: 2 -> 1, of which waited for: 2 -> 0; matrix products, arithmetic and copies ran while one was open for 3% -> 3% of each run, Pallas kernels for 14% -> 12%
where the time goes in v3:
time: 60 us; the launch traced here: 59.6 us
  blocking collectives  35.4 us (59%)
  Pallas kernels  17.7 us (30%)
  local copies, waits for them, and re-layouts  4.79 us (8%)
  starting transfers between devices  1.56 us (3%)
    all_to_all x1, blocking collectives, by_channel(): got = lax.all_to_all(parcels, 'tm', split_axis=0, concat_axis=0, tiled=True)  21 us
    all_to_all x1, blocking collectives, by_channel(): out = lax.all_to_all(out, 'tm', split_axis=0, concat_axis=0, tiled=True)  14.5 us
    pallas_call x1, Pallas kernels, by_channel(): call(functools.partial(branch_kernel, n), shape((n * own, BLOCK_FRAMES *...  8.66 us
    pallas_call x1, Pallas kernels, by_channel(): call(functools.partial(active_kernel, n), (shape((frames * C, LANES), bf1...  7.39 us
    unnamed x8, local copies, waits for them, and re-layouts  2.72 us
    ppermute x1, starting transfers between devices, by_channel(): other = lax.ppermute(other, 'groups', [(0, 1), (1, 0)])  1.56 us
  transfers between devices with their start and end apart: 1, of which 0 were waited for; matrix products, arithmetic and copies ran while one was open for 3% of the time, Pallas kernels for 12%

profile of v3, /device:TPU:0, one launch (start us, length us, event | category | flops | bytes accessed | tf_op | source)
XLA Modules:
  0.0 59.6 jit_solution(12230945577274031226)
XLA Ops:
  0.0 0.0 copy-start
  0.0 1.0 %copy-done = bf16[27,24,384]{2,1,0:T(8,128)(2,1)S(1)} copy-done((bf16[27,24,384]{2,1,0:T(8,128)(2,1)S(1)}, bf16[27,24,384]{2,1,0:T(8,128)(2,1)}, u32[]{:S(2)}) %copy-start) | copy-done | bytes 497688
  1.0 0.0 copy-start.1
  1.0 0.7 %copy-done.1 = bf16[16,384]{1,0:T(8,128)(2,1)S(1)} copy-done((bf16[16,384]{1,0:T(8,128)(2,1)S(1)}, bf16[16,384]{1,0:T(8,128)(2,1)}, u32[]{:S(2)}) %copy-start.1) | copy-done | bytes 12312
  1.7 0.9 %shard_map.73 = bf16[1920,128]{1,0:T(8,128)(2,1)S(1)} custom-call(bf16[16,384]{1,0:T(8,128)(2,1)S(1)} %copy-done.1, bf16[27,24,384]{2,1,0:T(8,128)(2,1)S(1)} %copy-done, s32[1]{0:T(128)} %bitcast.side_ref), custom_call_target="tpu_custom_call" | custom-call | tf_op jit(solution)/shard_map/pallas_call | solution.py:203
  2.6 0.0 copy-start.3
  2.6 21.0 %all_to_all.22 = bf16[16,120,128]{2,1,0:T(8,128)(2,1)S(1)} all-to-all(bf16[16,120,128]{2,1,0:T(8,128)(2,1)S(1)} %bitcast.9), channel_id=1, replica_groups=mesh['groups'=2,'tm'=16] {'tm'}, dimensions={0} | all-to-all | bytes 983040 | tf_op jit(solution)/shard_map/all_to_all | solution.py:206
  23.6 1.6 %collective-permute-start = (bf16[1152,128]{1,0:T(8,128)(2,1)S(1)}, bf16[1152,128]{1,0:T(8,128)(2,1)S(1)}, u32[]{:S(2)}, u32[]{:S(2)}) collective-permute-start(bf16[1152,128]{1,0:T(8,128)(2,1)S(1)} %bitcast.15), channel_id=1, source_target_pairs={{0,16},{16,0},{1,17},{17,1},{2,18},{18,2},{3,19},{19,3},{4,20},{20... | collective-permute-start | bytes 884744 | tf_op jit(solution)/shard_map/ppermute | solution.py:208
  25.2 0.7 %reshape.33.bias_ref = f32[1,384]{1,0:T(1,128)S(1)} reshape(f32[384]{0:T(512)} %param.10) | data formatting | bytes 3072 | tf_op jit(solution)/shard_map/reshape | solution.py:226
  25.8 0.7 %reshape.34.gain_ref = f32[1,384]{1,0:T(1,128)S(1)} reshape(f32[384]{0:T(512)} %param.11) | data formatting | bytes 3072 | tf_op jit(solution)/shard_map/reshape | solution.py:227
  26.5 0.7 %reshape.36.bias_ref = f32[1,384]{1,0:T(1,128)S(1)} reshape(f32[384]{0:T(512)} %param.13) | data formatting | bytes 3072 | tf_op jit(solution)/shard_map/reshape | solution.py:244
  27.2 0.0 copy-start.2
  27.2 1.0 %copy-done.2 = bf16[27,16,384]{2,1,0:T(8,128)(2,1)S(1)} copy-done((bf16[27,16,384]{2,1,0:T(8,128)(2,1)S(1)}, bf16[27,16,384]{2,1,0:T(8,128)(2,1)}, u32[]{:S(2)}) %copy-start.2) | copy-done | bytes 331800
  28.2 7.4 %shard_map.74 = (bf16[3072,768]{1,0:T(8,128)(2,1)S(1)}, f32[8,24,768]{2,1,0:T(8,128)S(1)}) custom-call(bf16[1920,128]{1,0:T(8,128)(2,1)S(1)} %bitcast.10, bf16[432,384]{1,0:T(8,128)(2,1)S(1)} %bitcast.14, f32[1,384]{1,0:T(1,128)S(1)} %reshape.33.bias_ref, f32[1,384]{1,0:T(1,128)S(1)} %reshape.34.gain_ref, s32[1]{0:T(128)} %bitcast.5.first_ref), custom_call_target="tpu_custom_call" | custom-call | flops 2038431744 | bytes 20000000 | tf_op jit(solution)/shard_map/pallas_call | solution.py:209
  35.6 0.0 collective-permute-done.w_ref
  35.6 0.0 copy-done.3
  35.6 8.7 %shard_map.75 = bf16[384,384]{1,0:T(8,128)(2,1)S(1)} custom-call(bf16[1920,128]{1,0:T(8,128)(2,1)S(1)} %bitcast.11, bf16[1152,128]{1,0:T(8,128)(2,1)S(1)} %collective-permute-done.w_ref, bf16[3072,768]{1,0:T(8,128)(2,1)S(1)} %get-tuple-element.7.x_hbm, f32[8,24,768]{2,1,0:T(8,128)S(1)} %get-tuple-element.8.stream_ref, f32[1,384]{1,0:T(1,128)S(1)} %reshape.36.bias_ref, ...), custom_call_target="tpu_custom_call" | custom-call | flops 3057647616 | bytes 20000000 | tf_op jit(solution)/shard_map/pallas_call | solution.py:230
  44.3 14.5 %all_to_all.23 = bf16[16,24,384]{2,1,0:T(8,128)(2,1)S(1)} all-to-all(bf16[16,24,384]{2,1,0:T(8,128)(2,1)S(1)} %bitcast.13), channel_id=1, replica_groups=mesh['groups'=2,'tm'=16] {'tm'}, dimensions={0} | all-to-all | bytes 589824 | tf_op jit(solution)/shard_map/all_to_all | solution.py:245
  58.7 0.9 %shard_map.76 = bf16[384,384]{1,0:T(8,128)(2,1)} custom-call(bf16[384,384]{1,0:T(8,128)(2,1)S(1)} %bitcast.12), custom_call_target="tpu_custom_call" | custom-call | tf_op jit(solution)/shard_map/pallas_call | solution.py:246
  (1 shorter events, 0.0 us)
Async XLA Ops:
  0.0 1.0 %copy-start = (bf16[27,24,384]{2,1,0:T(8,128)(2,1)S(1)}, bf16[27,24,384]{2,1,0:T(8,128)(2,1)}, u32[]{:S(2)}) copy-start(bf16[27,24,384]{2,1,0:T(8,128)(2,1)} %w_ref.1) | copy-start | bytes 1492996
  1.0 0.7 %copy-start.1 = (bf16[16,384]{1,0:T(8,128)(2,1)S(1)}, bf16[16,384]{1,0:T(8,128)(2,1)}, u32[]{:S(2)}) copy-start(bf16[16,384]{1,0:T(8,128)(2,1)} %x_ref.1) | copy-start | bytes 36868
  2.6 33.0 %copy-start.3 = (s32[8]{0:T(128)S(1)}, s32[8]{0:T(128)}, u32[]{:S(2)}) copy-start(s32[8]{0:T(128)} %count_ref.1) | copy-start | bytes 100
  23.6 12.0 %collective-permute-start = (bf16[1152,128]{1,0:T(8,128)(2,1)S(1)}, bf16[1152,128]{1,0:T(8,128)(2,1)S(1)}, u32[]{:S(2)}, u32[]{:S(2)}) collective-permute-start(bf16[1152,128]{1,0:T(8,128)(2,1)S(1)} %bitcast.15), channel_id=1, source_target_pairs={{0,16},{16,0},{1,17},{17,1},{2,18},{18,2},{3,19},{19,3},{4,20},{20... | collective-permute-start | bytes 884744 | tf_op jit(solution)/shard_map/ppermute | solution.py:208
  27.2 1.0 %copy-start.2 = (bf16[27,16,384]{2,1,0:T(8,128)(2,1)S(1)}, bf16[27,16,384]{2,1,0:T(8,128)(2,1)}, u32[]{:S(2)}) copy-start(bf16[27,16,384]{2,1,0:T(8,128)(2,1)} %param.9) | copy-start | bytes 995332

commit v4 on v3

--- a/solution.py
+++ b/solution.py
@@ -17,7 +17,6 @@
 LANES = PROMPT_SAMPLES * HW
 VMEM = pl.BlockSpec(memory_space=pltpu.VMEM)
 SMEM = pl.BlockSpec(memory_space=pltpu.SMEM)
-ANY = pl.BlockSpec(memory_space=pl.ANY)
 
 
 def shift_mask(j, k):
@@ -70,30 +69,53 @@
     return jnp.concatenate([tile] * (width // 128), axis=1)
 
 
-def active_kernel(n, got_ref, entry_ref, bias_ref, gain_ref, first_ref, x_hbm, stream_ref, col_ref, row_ref, x_ref, sem):
+def thirds(x):
+    parts = []
+    for _ in range(3):
+        part = x.astype(jnp.bfloat16).astype(jnp.float32)
+        parts.append(part)
+        x = x - part
+    return parts
+
+
+def params_kernel(n, entry_ref, bias_ref, gain_ref, after_ref, first_ref, o_ref, row_ref):
+    own = C // n
+    depth = 27 * LATENT_CHANNELS
+    first = pl.multiple_of(first_ref[0], 8)
+    lane = lax.broadcasted_iota(jnp.int32, (C, 16), 1)
+
+    def spread(ref):
+        tile = column(ref, 128)[:, :16]
+        out = jnp.zeros((C, 16), jnp.float32)
+        for t, part in enumerate(thirds(tile)):
+            out = jnp.where(lane == t, part, out)
+        return out
+
+    half_gain = column(gain_ref, 128) * 0.5
+    gap = jnp.zeros((C, 512 - depth - 16), jnp.float32)
+    weight = jnp.transpose(entry_ref[...].astype(jnp.float32))
+    full = jnp.concatenate([weight, spread(bias_ref), gap, half_gain], axis=1)
+    row_ref[0:C, :] = full
+    row_ref[C : 2 * C, :] = jnp.concatenate([jnp.zeros_like(weight), spread(after_ref), gap, half_gain], axis=1)
+    mine = row_ref[pl.ds(first, own), :]
+    after = row_ref[pl.ds(first + C, own), :]
+    o_ref[...] = jnp.concatenate([mine, after, full], axis=0).astype(jnp.bfloat16)
+
+
+def active_kernel(n, got_ref, params_ref, x_ref, stream_ref, col_ref):
     own = C // n
     frames = n // PROMPT_SAMPLES * BLOCK_FRAMES
     each = LATENT_CHANNELS * BLOCK_FRAMES // n
     taps = 9 * LATENT_CHANNELS
-    ahead = -(-own // 16) * 16
-    first = pl.multiple_of(first_ref[0], 8)
-    bias = column(bias_ref, LANES)
-    half_gain = (column(gain_ref, LANES) * 0.5).astype(jnp.bfloat16)
-    full = jnp.transpose(entry_ref[...].astype(jnp.float32))
-    row_ref[:, 0 : 3 * taps] = full
-    row_ref[:, 3 * taps : 3 * taps + 128] = bias[:, 0:128]
-    mine = row_ref[pl.ds(first, own), :]
-    mine_bias = mine[:, 3 * taps : 3 * taps + 128]
-    mine_bias = jnp.concatenate([mine_bias] * (LANES // 128), axis=1)
-    spare = jnp.zeros((ahead - own, 3 * taps), jnp.float32)
-    weight = jnp.concatenate([mine[:, : 3 * taps], spare, full], axis=0).astype(jnp.bfloat16)
+    weight = params_ref[:, : 3 * taps + 16]
+    half_gain = jnp.concatenate([params_ref[2 * own :, 512:]] * (LANES // 128), axis=1)
+    ones = (lax.broadcasted_iota(jnp.int32, (16, LANES), 0) < 3).astype(jnp.float32).astype(jnp.bfloat16)
     per_frame = LATENT_CHANNELS // each
     blocks = n // PROMPT_SAMPLES
     lats = got_ref[...].astype(jnp.float32).reshape(n, -1, 128)[:, 3 * own :]
     lats = lats.reshape(n, LANES // 128, blocks * each, 128)
     lats = jnp.concatenate([lats[:, t] for t in range(LANES // 128)], axis=2)
     lats = lats.reshape(BLOCK_FRAMES, per_frame, blocks, each, LANES)
-    copies = []
     for f in range(frames):
         b, g = divmod(f, BLOCK_FRAMES)
         lat = lats[g, :, b].reshape(LATENT_CHANNELS, LANES)
@@ -106,53 +128,37 @@
         least = max(f - 2, 0)
         z = jnp.dot(
             weight[:, (2 - (f - least)) * taps :],
-            col_ref[least * taps : (f + 1) * taps, :],
+            jnp.concatenate([col_ref[least * taps : (f + 1) * taps, :], ones], axis=0),
             preferred_element_type=jnp.float32,
         )
-        stream_ref[f] = (z[:own] + mine_bias).astype(jnp.bfloat16).astype(jnp.float32)
-        s = z[ahead:] + bias
+        stream_ref[f] = z[:own].astype(jnp.bfloat16).astype(jnp.float32) + z[own : 2 * own]
+        s = z[2 * own :]
         scale = lax.rsqrt(jnp.sum(s * s, axis=0, keepdims=True) * (1.0 / C) + 1e-06)
         half = s.astype(jnp.bfloat16) * half_gain * scale.astype(jnp.bfloat16)
         x_ref[f * C : (f + 1) * C, :] = half + half * jnp.tanh(half)
-        rows = pl.ds(f * C, C)
-        copy = pltpu.make_async_copy(x_ref.at[rows], x_hbm.at[rows], sem.at[f])
-        copy.start()
-        copies.append(copy)
-    for copy in copies:
-        copy.wait()
-
-
-def branch_kernel(n, got_ref, w_ref, x_hbm, stream_ref, bias_ref, first_ref, side_ref, count_ref, o_ref, x_ref, bias_col_ref, out_ref, sem):
+
+
+def branch_kernel(n, got_ref, w_ref, x_ref, stream_ref, side_ref, count_ref, o_ref, out_ref):
     own = C // n
     frames = n // PROMPT_SAMPLES * BLOCK_FRAMES
-    copies = []
-    for f in range(frames):
-        rows = pl.ds(f * C, C)
-        copy = pltpu.make_async_copy(x_hbm.at[rows], x_ref.at[rows], sem.at[f])
-        copy.start()
-        copies.append(copy)
     mine = got_ref[...].astype(jnp.float32).reshape(n, -1, 128)[:, : 3 * own].reshape(n, 3, own, 128)
     other = w_ref[...].astype(jnp.float32).reshape(n, 3, own, 128)
     left = jnp.broadcast_to(side_ref[0] == 0, other.shape)
     w = jnp.concatenate([jnp.where(left, mine, other), jnp.where(left, other, mine)], axis=3)
     w = jnp.transpose(w, (1, 0, 2, 3)).reshape(3 * C, 256)
     weight = jnp.transpose(w.astype(jnp.bfloat16))[: -(-9 * own // 16) * 16]
-    bias_col_ref[...] = column(bias_ref, 128)
-    bias = bias_col_ref[pl.ds(pl.multiple_of(first_ref[0], 8), own), :]
-    bias = jnp.concatenate([bias] * (LANES // 128), axis=1)
     lane = lax.broadcasted_iota(jnp.int32, (1, LANES), 1)
     count = jnp.zeros((1, LANES), jnp.int32)
     for s in range(PROMPT_SAMPLES):
         count = jnp.where(lane // HW == s, count_ref[s], count)
     for f in range(frames):
-        copies[f].wait()
         least = max(f - 2, 0)
         z = jnp.dot(
             weight[:, (2 - (f - least)) * C :],
             x_ref[least * C : (f + 1) * C, :],
             preferred_element_type=jnp.float32,
         )
-        total = stream_ref[f] + bias
+        total = stream_ref[f]
         for k in range(3):
             part = None
             for j in range(3):
@@ -206,42 +212,41 @@
     got = lax.all_to_all(parcels, "tm", split_axis=0, concat_axis=0, tiled=True)
     other = got.reshape(n, height, 128)[:, : 3 * own].reshape(n * 3 * own, 128)
     other = lax.ppermute(other, "groups", [(0, 1), (1, 0)])
+    params = call(
+        functools.partial(params_kernel, n),
+        shape((2 * own + C, 640), bf16),
+        [VMEM, VMEM, VMEM, VMEM, SMEM],
+        VMEM,
+        [pltpu.VMEM((2 * C, 640), f32)],
+        flops=500_000_000,
+        moved=2_000_000,
+    )(
+        entry_kernel.reshape(27 * LATENT_CHANNELS, C),
+        entry_bias.reshape(1, C),
+        gain.reshape(1, C),
+        bias.reshape(1, C),
+        first,
+    )
     active, stream = call(
         functools.partial(active_kernel, n),
         (shape((frames * C, LANES), bf16), shape((frames, own, LANES), f32)),
-        [VMEM, VMEM, VMEM, VMEM, SMEM],
-        (ANY, VMEM),
-        [
-            pltpu.VMEM((frames * 9 * LATENT_CHANNELS, LANES), bf16),
-            pltpu.VMEM((C, 27 * LATENT_CHANNELS + 128), f32),
-            pltpu.VMEM((frames * C, LANES), bf16),
-            pltpu.SemaphoreType.DMA((frames,)),
-        ],
+        [VMEM, VMEM],
+        (VMEM, VMEM),
+        [pltpu.VMEM((frames * 9 * LATENT_CHANNELS, LANES), bf16)],
         flops=2 * frames * LANES * 432 * C,
         moved=20_000_000,
-        limit=32,
-    )(
-        got,
-        entry_kernel.reshape(27 * LATENT_CHANNELS, C),
-        entry_bias.reshape(1, C),
-        gain.reshape(1, C),
-        first,
-    )
+        limit=24,
+    )(got, params)
     out = call(
         functools.partial(branch_kernel, n),
         shape((n * own, BLOCK_FRAMES * HW), bf16),
-        [VMEM, VMEM, ANY, VMEM, VMEM, SMEM, SMEM, SMEM],
+        [VMEM, VMEM, VMEM, VMEM, SMEM, SMEM],
         VMEM,
-        [
-            pltpu.VMEM((frames * C, LANES), bf16),
-            pltpu.VMEM((C, 128), f32),
-            pltpu.VMEM((frames, own, LANES), f32),
-            pltpu.SemaphoreType.DMA((frames,)),
-        ],
+        [pltpu.VMEM((frames, own, LANES), f32)],
         flops=2 * frames * LANES * 27 * C * own,
         moved=20_000_000,
-        limit=32,
-    )(got, other, active, stream, bias.reshape(1, C), first, side, counts)
+        limit=24,
+    )(got, other, active, stream, side, counts)
     out = lax.all_to_all(out, "tm", split_axis=0, concat_axis=0, tiled=True)
     out = call(transpose_kernel, shape((BLOCK_FRAMES * HW, C), bf16), [VMEM], VMEM)(out)
     return out.reshape(BLOCK_FRAMES, LATENT_ROWS, LATENT_COLUMNS, C)

time: 60 us -> 52.9 us (0.88)
  Pallas kernels: 17.7 us -> 10.4 us
    pallas_call x1, Pallas kernels: 8.66 us -> 4.32 us  [by_channel(): call(functools.partial(branch_kernel, n), shape((n * own, BLOCK_FRAMES *...]
    pallas_call x1, Pallas kernels: 7.39 us -> 3.89 us  [by_channel(): call(functools.partial(active_kernel, n), (shape((frames * C, LANES), bf1...]
  transfers between devices with their start and end apart: 1 -> 1, of which waited for: 0 -> 1; matrix products, arithmetic and copies ran while one was open for 3% -> 4% of each run, Pallas kernels for 12% -> 8%
where the time goes in v4:
time: 52.9 us; the launch traced here: 52.5 us
  blocking collectives  35.6 us (67%)
  Pallas kernels  10.4 us (20%)
  local copies, waits for them, and re-layouts  4.79 us (9%)
  starting transfers between devices  1.56 us (3%)
    all_to_all x1, blocking collectives, by_channel(): got = lax.all_to_all(parcels, 'tm', split_axis=0, concat_axis=0, tiled=True)  21 us
    all_to_all x1, blocking collectives, by_channel(): out = lax.all_to_all(out, 'tm', split_axis=0, concat_axis=0, tiled=True)  14.6 us
    pallas_call x1, Pallas kernels, by_channel(): call(functools.partial(branch_kernel, n), shape((n * own, BLOCK_FRAMES *...  4.32 us
    pallas_call x1, Pallas kernels, by_channel(): call(functools.partial(active_kernel, n), (shape((frames * C, LANES), bf1...  3.89 us
    unnamed x8, local copies, waits for them, and re-layouts  2.72 us
    ppermute x1, starting transfers between devices, by_channel(): other = lax.ppermute(other, 'groups', [(0, 1), (1, 0)])  1.56 us
  transfers between devices with their start and end apart: 1, of which 1 were waited for; matrix products, arithmetic and copies ran while one was open for 4% of the time, Pallas kernels for 8%

profile of v4, /device:TPU:0, one launch (start us, length us, event | category | flops | bytes accessed | tf_op | source)
XLA Modules:
  0.0 52.5 jit_solution(214195691553768301)
XLA Ops:
  0.0 0.0 copy-start
  0.0 1.0 %copy-done = bf16[27,24,384]{2,1,0:T(8,128)(2,1)S(1)} copy-done((bf16[27,24,384]{2,1,0:T(8,128)(2,1)S(1)}, bf16[27,24,384]{2,1,0:T(8,128)(2,1)}, u32[]{:S(2)}) %copy-start) | copy-done | bytes 497688
  1.0 0.0 copy-start.1
  1.0 0.7 %copy-done.1 = bf16[16,384]{1,0:T(8,128)(2,1)S(1)} copy-done((bf16[16,384]{1,0:T(8,128)(2,1)S(1)}, bf16[16,384]{1,0:T(8,128)(2,1)}, u32[]{:S(2)}) %copy-start.1) | copy-done | bytes 12312
  1.7 0.9 %shard_map.73 = bf16[1920,128]{1,0:T(8,128)(2,1)S(1)} custom-call(bf16[16,384]{1,0:T(8,128)(2,1)S(1)} %copy-done.1, bf16[27,24,384]{2,1,0:T(8,128)(2,1)S(1)} %copy-done, s32[1]{0:T(128)} %bitcast.side_ref), custom_call_target="tpu_custom_call" | custom-call | tf_op jit(solution)/shard_map/pallas_call | solution.py:209
  2.6 21.0 %all_to_all.22 = bf16[16,120,128]{2,1,0:T(8,128)(2,1)S(1)} all-to-all(bf16[16,120,128]{2,1,0:T(8,128)(2,1)S(1)} %bitcast.9), channel_id=1, replica_groups=mesh['groups'=2,'tm'=16] {'tm'}, dimensions={0} | all-to-all | bytes 983040 | tf_op jit(solution)/shard_map/all_to_all | solution.py:212
  23.6 0.0 copy-start.3
  23.6 1.6 %collective-permute-start = (bf16[1152,128]{1,0:T(8,128)(2,1)S(1)}, bf16[1152,128]{1,0:T(8,128)(2,1)S(1)}, u32[]{:S(2)}, u32[]{:S(2)}) collective-permute-start(bf16[1152,128]{1,0:T(8,128)(2,1)S(1)} %bitcast.15), channel_id=1, source_target_pairs={{0,16},{16,0},{1,17},{17,1},{2,18},{18,2},{3,19},{19,3},{4,20},{20... | collective-permute-start | bytes 884744 | tf_op jit(solution)/shard_map/ppermute | solution.py:214
  25.2 0.7 %reshape.33.bias_ref = f32[1,384]{1,0:T(1,128)S(1)} reshape(f32[384]{0:T(512)} %param.10) | data formatting | bytes 3072 | tf_op jit(solution)/shard_map/reshape | solution.py:225
  25.8 0.7 %reshape.34.gain_ref = f32[1,384]{1,0:T(1,128)S(1)} reshape(f32[384]{0:T(512)} %param.11) | data formatting | bytes 3072 | tf_op jit(solution)/shard_map/reshape | solution.py:226
  26.5 0.7 %reshape.35.after_ref = f32[1,384]{1,0:T(1,128)S(1)} reshape(f32[384]{0:T(512)} %param.13) | data formatting | bytes 3072 | tf_op jit(solution)/shard_map/reshape | solution.py:227
  27.2 0.0 copy-start.2
  27.2 1.0 %copy-done.2 = bf16[27,16,384]{2,1,0:T(8,128)(2,1)S(1)} copy-done((bf16[27,16,384]{2,1,0:T(8,128)(2,1)S(1)}, bf16[27,16,384]{2,1,0:T(8,128)(2,1)}, u32[]{:S(2)}) %copy-start.2) | copy-done | bytes 331800
  28.2 0.5 shard_map.74.params_ref
  28.7 3.9 %shard_map.75 = (bf16[3072,768]{1,0:T(8,128)(2,1)S(1)}, f32[8,24,768]{2,1,0:T(8,128)S(1)}) custom-call(bf16[1920,128]{1,0:T(8,128)(2,1)S(1)} %bitcast.10, bf16[432,640]{1,0:T(8,128)(2,1)S(1)} %shard_map.74.params_ref), custom_call_target="tpu_custom_call" | custom-call | flops 2038431744 | bytes 20000000 | tf_op jit(solution)/shard_map/pallas_call | solution.py:230
  32.6 0.1 collective-permute-done.w_ref
  32.7 0.0 copy-done.3
  32.7 4.3 %shard_map.76 = bf16[384,384]{1,0:T(8,128)(2,1)S(1)} custom-call(bf16[1920,128]{1,0:T(8,128)(2,1)S(1)} %bitcast.11, bf16[1152,128]{1,0:T(8,128)(2,1)S(1)} %collective-permute-done.w_ref, bf16[3072,768]{1,0:T(8,128)(2,1)S(1)} %get-tuple-element.7.x_ref, f32[8,24,768]{2,1,0:T(8,128)S(1)} %get-tuple-element.8.stream_ref, s32[1]{0:T(128)} %bitcast.side_ref, ...), custom_call_target="tpu_custom_call" | custom-call | flops 3057647616 | bytes 20000000 | tf_op jit(solution)/shard_map/pallas_call | solution.py:240
  37.0 14.6 %all_to_all.23 = bf16[16,24,384]{2,1,0:T(8,128)(2,1)S(1)} all-to-all(bf16[16,24,384]{2,1,0:T(8,128)(2,1)S(1)} %bitcast.13), channel_id=1, replica_groups=mesh['groups'=2,'tm'=16] {'tm'}, dimensions={0} | all-to-all | bytes 589824 | tf_op jit(solution)/shard_map/all_to_all | solution.py:250
  51.7 0.9 %shard_map.77 = bf16[384,384]{1,0:T(8,128)(2,1)} custom-call(bf16[384,384]{1,0:T(8,128)(2,1)S(1)} %bitcast.12), custom_call_target="tpu_custom_call" | custom-call | tf_op jit(solution)/shard_map/pallas_call | solution.py:251
  (1 shorter events, 0.0 us)
Async XLA Ops:
  0.0 1.0 %copy-start = (bf16[27,24,384]{2,1,0:T(8,128)(2,1)S(1)}, bf16[27,24,384]{2,1,0:T(8,128)(2,1)}, u32[]{:S(2)}) copy-start(bf16[27,24,384]{2,1,0:T(8,128)(2,1)} %w_ref.1) | copy-start | bytes 1492996
  1.0 0.7 %copy-start.1 = (bf16[16,384]{1,0:T(8,128)(2,1)S(1)}, bf16[16,384]{1,0:T(8,128)(2,1)}, u32[]{:S(2)}) copy-start(bf16[16,384]{1,0:T(8,128)(2,1)} %x_ref.1) | copy-start | bytes 36868
  23.6 9.1 %copy-start.3 = (s32[8]{0:T(128)S(1)}, s32[8]{0:T(128)}, u32[]{:S(2)}) copy-start(s32[8]{0:T(128)} %count_ref.1) | copy-start | bytes 100
  23.6 9.1 %collective-permute-start = (bf16[1152,128]{1,0:T(8,128)(2,1)S(1)}, bf16[1152,128]{1,0:T(8,128)(2,1)S(1)}, u32[]{:S(2)}, u32[]{:S(2)}) collective-permute-start(bf16[1152,128]{1,0:T(8,128)(2,1)S(1)} %bitcast.15), channel_id=1, source_target_pairs={{0,16},{16,0},{1,17},{17,1},{2,18},{18,2},{3,19},{19,3},{4,20},{20... | collective-permute-start | bytes 884744 | tf_op jit(solution)/shard_map/ppermute | solution.py:214
  27.2 1.0 %copy-start.2 = (bf16[27,16,384]{2,1,0:T(8,128)(2,1)S(1)}, bf16[27,16,384]{2,1,0:T(8,128)(2,1)}, u32[]{:S(2)}) copy-start(bf16[27,16,384]{2,1,0:T(8,128)(2,1)} %param.9) | copy-start | bytes 995332

commit v5 on v4

--- a/solution.py
+++ b/solution.py
@@ -59,14 +59,16 @@
             pieces = [tap[:, e * own : (e + 1) * own] for tap in taps]
             pieces.append(jnp.zeros((3 * own, 256 - 9 * own), jnp.float32))
             share = jnp.concatenate(pieces, axis=1)
-            both += [jnp.where(left, share[:, :128], share[:, 128:])] + tiles
+            half = len(tiles) // 2
+            own_tiles = tiles[half:] if e % 2 else tiles[:half]
+            both += [jnp.where(left, share[:, :128], share[:, 128:])] + own_tiles
         both = jnp.concatenate(both, axis=0).astype(jnp.bfloat16)
         o_ref[d // 2 * both.shape[0] : (d // 2 + 1) * both.shape[0], :] = both
 
 
-def column(row_ref, width):
-    tile = jnp.transpose(jnp.broadcast_to(row_ref[...], (128, row_ref.shape[1])))
-    return jnp.concatenate([tile] * (width // 128), axis=1)
+def column(rows):
+    parts = [jnp.transpose(jnp.broadcast_to(rows[t : t + 1], (128, 128))) for t in range(rows.shape[0])]
+    return jnp.concatenate(parts, axis=0)
 
 
 def thirds(x):
@@ -78,31 +80,32 @@
     return parts
 
 
-def params_kernel(n, entry_ref, bias_ref, gain_ref, after_ref, first_ref, o_ref, row_ref):
+def params_kernel(n, entry_ref, vectors_ref, first_ref, o_ref, row_ref):
     own = C // n
     depth = 27 * LATENT_CHANNELS
+    tall = C // 128
     first = pl.multiple_of(first_ref[0], 8)
     lane = lax.broadcasted_iota(jnp.int32, (C, 16), 1)
 
-    def spread(ref):
-        tile = column(ref, 128)[:, :16]
+    def spread(t):
+        tile = column(vectors_ref[t * tall : (t + 1) * tall])[:, :16]
         out = jnp.zeros((C, 16), jnp.float32)
         for t, part in enumerate(thirds(tile)):
             out = jnp.where(lane == t, part, out)
         return out
 
-    half_gain = column(gain_ref, 128) * 0.5
+    half_gain = column(vectors_ref[tall : 2 * tall]) * 0.5
     gap = jnp.zeros((C, 512 - depth - 16), jnp.float32)
     weight = jnp.transpose(entry_ref[...].astype(jnp.float32))
-    full = jnp.concatenate([weight, spread(bias_ref), gap, half_gain], axis=1)
+    full = jnp.concatenate([weight, spread(0), gap, half_gain], axis=1)
     row_ref[0:C, :] = full
-    row_ref[C : 2 * C, :] = jnp.concatenate([jnp.zeros_like(weight), spread(after_ref), gap, half_gain], axis=1)
+    row_ref[C : 2 * C, :] = jnp.concatenate([jnp.zeros_like(weight), spread(2), gap, half_gain], axis=1)
     mine = row_ref[pl.ds(first, own), :]
     after = row_ref[pl.ds(first + C, own), :]
     o_ref[...] = jnp.concatenate([mine, after, full], axis=0).astype(jnp.bfloat16)
 
 
-def active_kernel(n, got_ref, params_ref, x_ref, stream_ref, col_ref):
+def active_kernel(n, got_ref, lat_ref, params_ref, odd_ref, x_ref, stream_ref, col_ref):
     own = C // n
     frames = n // PROMPT_SAMPLES * BLOCK_FRAMES
     each = LATENT_CHANNELS * BLOCK_FRAMES // n
@@ -112,7 +115,10 @@
     ones = (lax.broadcasted_iota(jnp.int32, (16, LANES), 0) < 3).astype(jnp.float32).astype(jnp.bfloat16)
     per_frame = LATENT_CHANNELS // each
     blocks = n // PROMPT_SAMPLES
-    lats = got_ref[...].astype(jnp.float32).reshape(n, -1, 128)[:, 3 * own :]
+    mine = got_ref[...].astype(jnp.float32).reshape(n, -1, 128)[:, 3 * own :]
+    other = lat_ref[...].astype(jnp.float32).reshape(mine.shape)
+    even = jnp.broadcast_to(odd_ref[0] == 0, mine.shape)
+    lats = jnp.concatenate([jnp.where(even, mine, other), jnp.where(even, other, mine)], axis=1)
     lats = lats.reshape(n, LANES // 128, blocks * each, 128)
     lats = jnp.concatenate([lats[:, t] for t in range(LANES // 128)], axis=2)
     lats = lats.reshape(BLOCK_FRAMES, per_frame, blocks, each, LANES)
@@ -205,38 +211,40 @@
     bf16, f32 = jnp.bfloat16, jnp.float32
     side = lax.axis_index("groups").astype(jnp.int32).reshape(1)
     each = latents.shape[1] // HW * (n // PROMPT_SAMPLES)
-    height = 3 * own + each * LANES // 128
+    odd = (lax.axis_index("tm") % 2).astype(jnp.int32).reshape(1)
+    height = 3 * own + each * LANES // 256
     parcels = call(
         functools.partial(parcels_kernel, n), shape((n * height, 128), bf16), [VMEM, VMEM, SMEM], VMEM
     )(latents, kernel, side)
     got = lax.all_to_all(parcels, "tm", split_axis=0, concat_axis=0, tiled=True)
-    other = got.reshape(n, height, 128)[:, : 3 * own].reshape(n * 3 * own, 128)
-    other = lax.ppermute(other, "groups", [(0, 1), (1, 0)])
     params = call(
         functools.partial(params_kernel, n),
         shape((2 * own + C, 640), bf16),
-        [VMEM, VMEM, VMEM, VMEM, SMEM],
+        [VMEM, VMEM, SMEM],
         VMEM,
         [pltpu.VMEM((2 * C, 640), f32)],
         flops=500_000_000,
         moved=2_000_000,
     )(
         entry_kernel.reshape(27 * LATENT_CHANNELS, C),
-        entry_bias.reshape(1, C),
-        gain.reshape(1, C),
-        bias.reshape(1, C),
+        jnp.concatenate([entry_bias, gain, bias]).reshape(-1, 128),
         first,
     )
+    split = got.reshape(n, height, 128)
+    other, params = lax.optimization_barrier((split[:, : 3 * own].reshape(n * 3 * own, 128), params))
+    other = lax.ppermute(other, "groups", [(0, 1), (1, 0)])
+    lats = split[:, 3 * own :].reshape(-1, 128)
+    lats = lax.ppermute(lats, "tm", [(i, i ^ 1) for i in range(n)])
     active, stream = call(
         functools.partial(active_kernel, n),
         (shape((frames * C, LANES), bf16), shape((frames, own, LANES), f32)),
-        [VMEM, VMEM],
+        [VMEM, VMEM, VMEM, SMEM],
         (VMEM, VMEM),
         [pltpu.VMEM((frames * 9 * LATENT_CHANNELS, LANES), bf16)],
         flops=2 * frames * LANES * 432 * C,
         moved=20_000_000,
         limit=24,
-    )(got, params)
+    )(got, lats, params, odd)
     out = call(
         functools.partial(branch_kernel, n),
         shape((n * own, BLOCK_FRAMES * HW), bf16),
@@ -333,7 +341,7 @@
 def solution(mesh):
     n = mesh.shape["tm"]
     cells = BLOCK_FRAMES * LATENT_CHANNELS * HW
-    fits = mesh.shape["groups"] == 2 and 9 * (C // n) <= 256 and n * HW % 128 == 0
+    fits = mesh.shape["groups"] == 2 and 9 * (C // n) <= 256 and n % 2 == 0 and LANES % 256 == 0
     whole_rows = fits and cells % (n * HW) == 0 and C % n == 0 and (C // n) % 8 == 0 and n % PROMPT_SAMPLES == 0
     body = functools.partial(by_channel, n) if whole_rows else by_block
     in_specs = (P("groups", "tm"), P("groups"), P(), P(), P(), P(None, "tm", None), P())

time: 52.9 us -> 51.6 us (0.975)
  blocking collectives: 35.6 us -> 14.1 us
  waiting for transfers between devices: 0.14 us -> 13.3 us
  starting transfers between devices: 1.56 us -> 9.01 us
  local copies, waits for them, and re-layouts: 4.79 us -> 2.75 us
  Pallas kernels: 10.4 us -> 11.2 us
  other arithmetic: 0 us -> 0.73 us
    all_to_all x1 -> x0, blocking collectives: 21 us -> none  [by_channel(): got = lax.all_to_all(parcels, 'tm', split_axis=0, concat_axis=0, tiled=True)]
    all_to_all x0 -> x1, waiting for transfers between devices: none -> 10 us  [by_channel(): got = lax.all_to_all(parcels, 'tm', split_axis=0, concat_axis=0, tiled=True)]
    all_to_all x0 -> x1, starting transfers between devices: none -> 7.39 us  [by_channel(): got = lax.all_to_all(parcels, 'tm', split_axis=0, concat_axis=0, tiled=True)]
    reshape x3 -> x0, local copies, waits for them, and re-layouts: 2.05 us -> none  [the longest x1 0.68 us: by_channel(): entry_bias.reshape(1, C)]
    ppermute x1, waiting for transfers between devices: 0.14 us -> 2.05 us  [by_channel(): other = lax.ppermute(other, 'groups', [(0, 1), (1, 0)])]
    ppermute x0 -> x1, waiting for transfers between devices: none -> 1.28 us  [by_channel(): lats = lax.ppermute(lats, 'tm', [(i, i ^ 1) for i in range(n)])]
    pallas_call x1, Pallas kernels: 0.85 us -> 1.6 us  [by_channel(): call(functools.partial(parcels_kernel, n), shape((n * height, 128), bf16)...]
    concatenate x0 -> x1, other arithmetic: none -> 0.73 us  [by_channel(): jnp.concatenate([entry_bias, gain, bias]).reshape(-1, 128)]
  transfers between devices with their start and end apart: 1 -> 3, of which waited for: 1 -> 3; matrix products, arithmetic and copies ran while one was open for 4% -> 1% of each run, Pallas kernels for 8% -> 9%
where the time goes in v5:
time: 51.6 us; the launch traced here: 51.2 us
  blocking collectives  14.1 us (27%)
  waiting for transfers between devices  13.3 us (26%)
  Pallas kernels  11.2 us (22%)
  starting transfers between devices  9.01 us (17%)
  local copies, waits for them, and re-layouts  2.75 us (5%)
  other arithmetic  0.73 us (1%)
    all_to_all x1, blocking collectives, by_channel(): out = lax.all_to_all(out, 'tm', split_axis=0, concat_axis=0, tiled=True)  14.1 us
    all_to_all x1, waiting for transfers between devices, by_channel(): got = lax.all_to_all(parcels, 'tm', split_axis=0, concat_axis=0, tiled=True)  10 us
    all_to_all x1, starting transfers between devices, by_channel(): got = lax.all_to_all(parcels, 'tm', split_axis=0, concat_axis=0, tiled=True)  7.39 us
    pallas_call x1, Pallas kernels, by_channel(): call(functools.partial(branch_kernel, n), shape((n * own, BLOCK_FRAMES *...  4.16 us
    pallas_call x1, Pallas kernels, by_channel(): call(functools.partial(active_kernel, n), (shape((frames * C, LANES), bf1...  4.1 us
    unnamed x8, local copies, waits for them, and re-layouts  2.71 us
    ppermute x1, waiting for transfers between devices, by_channel(): other = lax.ppermute(other, 'groups', [(0, 1), (1, 0)])  2.05 us
    pallas_call x1, Pallas kernels, by_channel(): call(functools.partial(parcels_kernel, n), shape((n * height, 128), bf16)...  1.6 us
  transfers between devices with their start and end apart: 3, of which 3 were waited for; matrix products, arithmetic and copies ran while one was open for 1% of the time, Pallas kernels for 9%

profile of v5, /device:TPU:0, one launch (start us, length us, event | category | flops | bytes accessed | tf_op | source)
XLA Modules:
  0.0 51.2 jit_solution(4920361647309393310)
XLA Ops:
  0.0 0.0 copy-start
  0.0 1.0 %copy-done = bf16[27,24,384]{2,1,0:T(8,128)(2,1)S(1)} copy-done((bf16[27,24,384]{2,1,0:T(8,128)(2,1)S(1)}, bf16[27,24,384]{2,1,0:T(8,128)(2,1)}, u32[]{:S(2)}) %copy-start) | copy-done | bytes 497688
  1.0 0.0 copy-start.1
  1.0 0.7 %copy-done.1 = bf16[16,384]{1,0:T(8,128)(2,1)S(1)} copy-done((bf16[16,384]{1,0:T(8,128)(2,1)S(1)}, bf16[16,384]{1,0:T(8,128)(2,1)}, u32[]{:S(2)}) %copy-start.1) | copy-done | bytes 12312
  1.7 1.6 %shard_map.73 = bf16[1536,128]{1,0:T(8,128)(2,1)} custom-call(bf16[16,384]{1,0:T(8,128)(2,1)S(1)} %copy-done.1, bf16[27,24,384]{2,1,0:T(8,128)(2,1)S(1)} %copy-done, s32[1]{0:T(128)} %bitcast.side_ref), custom_call_target="tpu_custom_call" | custom-call | tf_op jit(solution)/shard_map/pallas_call | solution.py:216
  3.3 7.4 %all-to-all-start = ((bf16[16,96,128]{2,1,0:T(8,128)(2,1)}), bf16[16,96,128]{2,1,0:T(8,128)(2,1)S(1)}, u32[]{:S(2)}, u32[]{:S(2)}) async-start(bf16[16,96,128]{2,1,0:T(8,128)(2,1)} %bitcast.1), calls=%async_computation | async-start | bytes 786432 | tf_op jit(solution)/shard_map/all_to_all | solution.py:219
  10.7 0.7 %pad_maximum_fusion.vectors_ref = f32[9,128]{1,0:T(8,128)S(1)} fusion(f32[3,128]{1,0:T(4,128)} %bitcast.21, f32[3,128]{1,0:T(4,128)} %bitcast.22, f32[3,128]{1,0:T(4,128)} %bitcast.23), kind=kLoop, calls=%fused_computation | loop fusion | flops 2304 | bytes 9216 | tf_op jit(solution)/shard_map/concatenate | solution.py:230
  11.5 0.0 copy-start.2
  11.5 1.0 %copy-done.2 = bf16[27,16,384]{2,1,0:T(8,128)(2,1)S(1)} copy-done((bf16[27,16,384]{2,1,0:T(8,128)(2,1)S(1)}, bf16[27,16,384]{2,1,0:T(8,128)(2,1)}, u32[]{:S(2)}) %copy-start.2) | copy-done | bytes 331800
  12.4 0.0 copy-start.3
  12.4 0.5 shard_map.74.params_ref
  12.9 10.0 %all-to-all-done = bf16[16,96,128]{2,1,0:T(8,128)(2,1)S(1)} async-done(((bf16[16,96,128]{2,1,0:T(8,128)(2,1)}), bf16[16,96,128]{2,1,0:T(8,128)(2,1)S(1)}, u32[]{:S(2)}, u32[]{:S(2)}) %all-to-all-start) | async-done | bytes 393248 | tf_op jit(solution)/shard_map/all_to_all | solution.py:219
  23.0 1.6 %collective-permute-start = (bf16[1152,128]{1,0:T(8,128)(2,1)S(1)}, bf16[1152,128]{1,0:T(8,128)(2,1)S(1)}, u32[]{:S(2)}, u32[]{:S(2)}) collective-permute-start(bf16[1152,128]{1,0:T(8,128)(2,1)S(1)} %bitcast.19), channel_id=1, source_target_pairs={{0,16},{16,0},{1,17},{17,1},{2,18},{18,2},{3,19},{19,3},{4,20},{20... | collective-permute-start | bytes 884744 | tf_op jit(solution)/shard_map/ppermute | solution.py:235
  24.5 0.1 collective-permute-start.1
  24.6 1.3 %collective-permute-done.1.lat_ref = bf16[384,128]{1,0:T(8,128)(2,1)S(1)} collective-permute-done((bf16[384,128]{1,0:T(8,128)(2,1)S(1)}, bf16[384,128]{1,0:T(8,128)(2,1)S(1)}, u32[]{:S(2)}, u32[]{:S(2)}) %collective-permute-start.1) | collective-permute-done | bytes 98336 | tf_op jit(solution)/shard_map/ppermute | solution.py:237
  25.9 4.1 %shard_map.75 = (bf16[3072,768]{1,0:T(8,128)(2,1)S(1)}, f32[8,24,768]{2,1,0:T(8,128)S(1)}) custom-call(bf16[1536,128]{1,0:T(8,128)(2,1)S(1)} %bitcast.14, bf16[384,128]{1,0:T(8,128)(2,1)S(1)} %collective-permute-done.1.lat_ref, bf16[432,640]{1,0:T(8,128)(2,1)S(1)} %shard_map.74.params_ref, s32[1]{0:T(128)} %bitcast.10.odd_ref), custom_call_target="tpu_custom_call" | custom-call | flops 2038431744 | bytes 20000000 | tf_op jit(solution)/shard_map/pallas_call | solution.py:238
  30.0 2.0 %collective-permute-done.w_ref = bf16[1152,128]{1,0:T(8,128)(2,1)S(1)} collective-permute-done((bf16[1152,128]{1,0:T(8,128)(2,1)S(1)}, bf16[1152,128]{1,0:T(8,128)(2,1)S(1)}, u32[]{:S(2)}, u32[]{:S(2)}) %collective-permute-start) | collective-permute-done | bytes 294944 | tf_op jit(solution)/shard_map/ppermute | solution.py:235
  32.1 0.0 copy-done.3
  32.1 4.2 %shard_map.76 = bf16[384,384]{1,0:T(8,128)(2,1)S(1)} custom-call(bf16[1536,128]{1,0:T(8,128)(2,1)S(1)} %bitcast.15, bf16[1152,128]{1,0:T(8,128)(2,1)S(1)} %collective-permute-done.w_ref, bf16[3072,768]{1,0:T(8,128)(2,1)S(1)} %get-tuple-element.11.x_ref, f32[8,24,768]{2,1,0:T(8,128)S(1)} %get-tuple-element.12.stream_ref, s32[1]{0:T(128)} %bitcast.side_ref, ...), custom_call_target="tpu_custom_call" | custom-call | flops 3057647616 | bytes 20000000 | tf_op jit(solution)/shard_map/pallas_call | solution.py:248
  36.2 14.1 %all_to_all.22 = bf16[16,24,384]{2,1,0:T(8,128)(2,1)S(1)} all-to-all(bf16[16,24,384]{2,1,0:T(8,128)(2,1)S(1)} %bitcast.17), channel_id=1, replica_groups=mesh['groups'=2,'tm'=16] {'tm'}, dimensions={0} | all-to-all | bytes 589824 | tf_op jit(solution)/shard_map/all_to_all | solution.py:258
  50.3 0.9 %shard_map.77 = bf16[384,384]{1,0:T(8,128)(2,1)} custom-call(bf16[384,384]{1,0:T(8,128)(2,1)S(1)} %bitcast.16), custom_call_target="tpu_custom_call" | custom-call | tf_op jit(solution)/shard_map/pallas_call | solution.py:259
  (2 shorter events, 0.0 us)
Async XLA Ops:
  0.0 1.0 %copy-start = (bf16[27,24,384]{2,1,0:T(8,128)(2,1)S(1)}, bf16[27,24,384]{2,1,0:T(8,128)(2,1)}, u32[]{:S(2)}) copy-start(bf16[27,24,384]{2,1,0:T(8,128)(2,1)} %w_ref.1) | copy-start | bytes 1492996
  1.0 0.7 %copy-start.1 = (bf16[16,384]{1,0:T(8,128)(2,1)S(1)}, bf16[16,384]{1,0:T(8,128)(2,1)}, u32[]{:S(2)}) copy-start(bf16[16,384]{1,0:T(8,128)(2,1)} %x_ref.1) | copy-start | bytes 36868
  3.3 19.6 %all-to-all-start = ((bf16[16,96,128]{2,1,0:T(8,128)(2,1)}), bf16[16,96,128]{2,1,0:T(8,128)(2,1)S(1)}, u32[]{:S(2)}, u32[]{:S(2)}) async-start(bf16[16,96,128]{2,1,0:T(8,128)(2,1)} %bitcast.1), calls=%async_computation | async-start | bytes 786432 | tf_op jit(solution)/shard_map/all_to_all | solution.py:219
  11.5 1.0 %copy-start.2 = (bf16[27,16,384]{2,1,0:T(8,128)(2,1)S(1)}, bf16[27,16,384]{2,1,0:T(8,128)(2,1)}, u32[]{:S(2)}) copy-start(bf16[27,16,384]{2,1,0:T(8,128)(2,1)} %param.9) | copy-start | bytes 995332
  12.4 19.6 %copy-start.3 = (s32[8]{0:T(128)S(1)}, s32[8]{0:T(128)}, u32[]{:S(2)}) copy-start(s32[8]{0:T(128)} %count_ref.1) | copy-start | bytes 100
  23.0 9.1 %collective-permute-start = (bf16[1152,128]{1,0:T(8,128)(2,1)S(1)}, bf16[1152,128]{1,0:T(8,128)(2,1)S(1)}, u32[]{:S(2)}, u32[]{:S(2)}) collective-permute-start(bf16[1152,128]{1,0:T(8,128)(2,1)S(1)} %bitcast.19), channel_id=1, source_target_pairs={{0,16},{16,0},{1,17},{17,1},{2,18},{18,2},{3,19},{19,3},{4,20},{20... | collective-permute-start | bytes 884744 | tf_op jit(solution)/shard_map/ppermute | solution.py:235
  24.5 1.4 %collective-permute-start.1 = (bf16[384,128]{1,0:T(8,128)(2,1)S(1)}, bf16[384,128]{1,0:T(8,128)(2,1)S(1)}, u32[]{:S(2)}, u32[]{:S(2)}) collective-permute-start(bf16[384,128]{1,0:T(8,128)(2,1)S(1)} %bitcast.20), channel_id=1, source_target_pairs={{0,1},{1,0},{2,3},{3,2},{4,5},{5,4},{6,7},{7,6},{8,9},{9,8},{10,11... | collective-permute-start | bytes 294920 | tf_op jit(solution)/shard_map/ppermute | solution.py:237

commit v6 on v5

--- a/solution.py
+++ b/solution.py
@@ -39,6 +39,20 @@
     return x if delta == 0 else pltpu.roll(x, (-delta) % x.shape[1], 1)
 
 
+def packing(own):
+    runs = 3 * (own // 8)
+    places = {}
+    for run in range(runs):
+        for t in range(9):
+            if run < runs // 2 * 2:
+                place = (run // (runs // 2), (run % (runs // 2) * 9 + t) * own)
+            else:
+                place = (0 if t < 5 else 1, (runs // 2 * 9 + (t if t < 5 else t - 5)) * own)
+            places[run // (own // 8), run % (own // 8), t] = place
+    longest = max(lane for _, lane in places.values()) + own
+    return places, -(-longest // 128) * 128
+
+
 def parcels_kernel(n, x_ref, w_ref, side_ref, o_ref):
     own = C // n
     x = x_ref[...].astype(jnp.float32)
@@ -50,18 +64,27 @@
             rows.append(jnp.concatenate(pieces, axis=1))
     rows = jnp.concatenate(rows, axis=0)
     tiles = [rows[:, t * 128 : (t + 1) * 128] for t in range(LANES // 128)]
-    w = w_ref[...].astype(jnp.float32).reshape(3, 9, own, C)
-    taps = [w[:, t].reshape(3 * own, C) for t in range(9)]
-    left = jnp.broadcast_to(side_ref[0] == 0, (3 * own, 128))
+    w = w_ref[...].astype(jnp.float32).reshape(3, 9, own // 8, 8, C)
+    places, width = packing(own)
+    left = jnp.broadcast_to(side_ref[0] == 0, (8, width))
+    half = len(tiles) // 2
     for d in range(0, n, 2):
         both = []
         for e in (d, d + 1):
-            pieces = [tap[:, e * own : (e + 1) * own] for tap in taps]
-            pieces.append(jnp.zeros((3 * own, 256 - 9 * own), jnp.float32))
-            share = jnp.concatenate(pieces, axis=1)
-            half = len(tiles) // 2
-            own_tiles = tiles[half:] if e % 2 else tiles[:half]
-            both += [jnp.where(left, share[:, :128], share[:, 128:])] + own_tiles
+            halves = []
+            for side in range(2):
+                pieces = [
+                    w[i, t, c, :, e * own : (e + 1) * own]
+                    for i in range(3)
+                    for c in range(own // 8)
+                    for t in range(9)
+                    if places[i, c, t][0] == side
+                ]
+                pieces.append(jnp.zeros((8, width - len(pieces) * own), jnp.float32))
+                halves.append(jnp.concatenate(pieces, axis=1))
+            share = jnp.where(left, halves[0], halves[1])
+            both += [share[:, t * 128 : (t + 1) * 128] for t in range(width // 128)]
+            both += tiles[half:] if e % 2 else tiles[:half]
         both = jnp.concatenate(both, axis=0).astype(jnp.bfloat16)
         o_ref[d // 2 * both.shape[0] : (d // 2 + 1) * both.shape[0], :] = both
 
@@ -115,7 +138,7 @@
     ones = (lax.broadcasted_iota(jnp.int32, (16, LANES), 0) < 3).astype(jnp.float32).astype(jnp.bfloat16)
     per_frame = LATENT_CHANNELS // each
     blocks = n // PROMPT_SAMPLES
-    mine = got_ref[...].astype(jnp.float32).reshape(n, -1, 128)[:, 3 * own :]
+    mine = got_ref[...].astype(jnp.float32).reshape(n, -1, 128)[:, packing(own)[1] // 16 :]
     other = lat_ref[...].astype(jnp.float32).reshape(mine.shape)
     even = jnp.broadcast_to(odd_ref[0] == 0, mine.shape)
     lats = jnp.concatenate([jnp.where(even, mine, other), jnp.where(even, other, mine)], axis=1)
@@ -147,11 +170,30 @@
 def branch_kernel(n, got_ref, w_ref, x_ref, stream_ref, side_ref, count_ref, o_ref, out_ref):
     own = C // n
     frames = n // PROMPT_SAMPLES * BLOCK_FRAMES
-    mine = got_ref[...].astype(jnp.float32).reshape(n, -1, 128)[:, : 3 * own].reshape(n, 3, own, 128)
-    other = w_ref[...].astype(jnp.float32).reshape(n, 3, own, 128)
+    places, width = packing(own)
+
+    def lanes(x):
+        x = x.reshape(n, width // 128, 8, 128)
+        return jnp.concatenate([x[:, t] for t in range(width // 128)], axis=2).reshape(n * 8, width)
+
+    mine = lanes(got_ref[...].astype(jnp.float32).reshape(n, -1, 128)[:, : width // 16])
+    other = lanes(w_ref[...].astype(jnp.float32))
     left = jnp.broadcast_to(side_ref[0] == 0, other.shape)
-    w = jnp.concatenate([jnp.where(left, mine, other), jnp.where(left, other, mine)], axis=3)
-    w = jnp.transpose(w, (1, 0, 2, 3)).reshape(3 * C, 256)
+    halves = (jnp.where(left, mine, other), jnp.where(left, other, mine))
+    pad = jnp.zeros((n * 8, 256 - 9 * own), jnp.float32)
+    depths = []
+    for i in range(3):
+        runs = []
+        for c in range(own // 8):
+            side, lane = places[i, c, 0]
+            if places[i, c, 8][0] == side:
+                parts = [halves[side][:, lane : lane + 9 * own]]
+            else:
+                end = places[i, c, 5][1]
+                parts = [halves[0][:, lane : lane + 5 * own], halves[1][:, end : end + 4 * own]]
+            runs.append(jnp.concatenate(parts + [pad], axis=1).reshape(n, 1, 8, 256))
+        depths.append(jnp.concatenate(runs, axis=1).reshape(C, 256))
+    w = jnp.concatenate(depths, axis=0)
     weight = jnp.transpose(w.astype(jnp.bfloat16))[: -(-9 * own // 16) * 16]
     lane = lax.broadcasted_iota(jnp.int32, (1, LANES), 1)
     count = jnp.zeros((1, LANES), jnp.int32)
@@ -212,9 +254,10 @@
     side = lax.axis_index("groups").astype(jnp.int32).reshape(1)
     each = latents.shape[1] // HW * (n // PROMPT_SAMPLES)
     odd = (lax.axis_index("tm") % 2).astype(jnp.int32).reshape(1)
-    height = 3 * own + each * LANES // 256
+    height = packing(own)[1] // 16
+    extra = each * LANES // 256
     parcels = call(
-        functools.partial(parcels_kernel, n), shape((n * height, 128), bf16), [VMEM, VMEM, SMEM], VMEM
+        functools.partial(parcels_kernel, n), shape((n * (height + extra), 128), bf16), [VMEM, VMEM, SMEM], VMEM, limit=58
     )(latents, kernel, side)
     got = lax.all_to_all(parcels, "tm", split_axis=0, concat_axis=0, tiled=True)
     params = call(
@@ -230,10 +273,10 @@
         jnp.concatenate([entry_bias, gain, bias]).reshape(-1, 128),
         first,
     )
-    split = got.reshape(n, height, 128)
-    other, params = lax.optimization_barrier((split[:, : 3 * own].reshape(n * 3 * own, 128), params))
+    split = got.reshape(n, height + extra, 128)
+    other, params = lax.optimization_barrier((split[:, :height].reshape(n * height, 128), params))
     other = lax.ppermute(other, "groups", [(0, 1), (1, 0)])
-    lats = split[:, 3 * own :].reshape(-1, 128)
+    lats = split[:, height:].reshape(-1, 128)
     lats = lax.ppermute(lats, "tm", [(i, i ^ 1) for i in range(n)])
     active, stream = call(
         functools.partial(active_kernel, n),

time: 51.6 us -> 51.4 us (level)
  local copies, waits for them, and re-layouts: 2.75 us -> 1.01 us
  Pallas kernels: 11.2 us -> 12.5 us
  waiting for transfers between devices: 13.3 us -> 14 us
    unnamed x8 -> x4, local copies, waits for them, and re-layouts: 2.71 us -> 0.98 us
    ppermute x1, waiting for transfers between devices: 1.28 us -> 0.01 us  [by_channel(): lats = lax.ppermute(lats, 'tm', [(i, i ^ 1) for i in range(n)])]
    pallas_call x1, Pallas kernels: 1.6 us -> 2.63 us  [by_channel(): call(functools.partial(parcels_kernel, n), shape((n * (height + extra), 1...]
    ppermute x1, waiting for transfers between devices: 2.05 us -> 3.04 us  [by_channel(): other = lax.ppermute(other, 'groups', [(0, 1), (1, 0)])]
    all_to_all x1, waiting for transfers between devices: 10 us -> 10.9 us  [by_channel(): got = lax.all_to_all(parcels, 'tm', split_axis=0, concat_axis=0, tiled=True)]
  transfers between devices with their start and end apart: 3 -> 3, of which waited for: 3 -> 2; matrix products, arithmetic and copies ran while one was open for 1% -> 1% of each run, Pallas kernels for 9% -> 9%
where the time goes in v6:
time: 51.4 us; the launch traced here: 51 us
  waiting for transfers between devices  14 us (27%)
  blocking collectives  13.7 us (27%)
  Pallas kernels  12.5 us (24%)
  starting transfers between devices  9.12 us (18%)
  local copies, waits for them, and re-layouts  1.01 us (2%)
  other arithmetic  0.73 us (1%)
    all_to_all x1, blocking collectives, by_channel(): out = lax.all_to_all(out, 'tm', split_axis=0, concat_axis=0, tiled=True)  13.7 us
    all_to_all x1, waiting for transfers between devices, by_channel(): got = lax.all_to_all(parcels, 'tm', split_axis=0, concat_axis=0, tiled=True)  10.9 us
    all_to_all x1, starting transfers between devices, by_channel(): got = lax.all_to_all(parcels, 'tm', split_axis=0, concat_axis=0, tiled=True)  7.39 us
    pallas_call x1, Pallas kernels, by_channel(): call(functools.partial(branch_kernel, n), shape((n * own, BLOCK_FRAMES *...  4.44 us
    pallas_call x1, Pallas kernels, by_channel(): call(functools.partial(active_kernel, n), (shape((frames * C, LANES), bf1...  4.1 us
    ppermute x1, waiting for transfers between devices, by_channel(): other = lax.ppermute(other, 'groups', [(0, 1), (1, 0)])  3.04 us
    pallas_call x1, Pallas kernels, by_channel(): call(functools.partial(parcels_kernel, n), shape((n * (height + extra), 1...  2.63 us
    ppermute x1, starting transfers between devices, by_channel(): other = lax.ppermute(other, 'groups', [(0, 1), (1, 0)])  1.56 us
  transfers between devices with their start and end apart: 3, of which 2 were waited for; matrix products, arithmetic and copies ran while one was open for 1% of the time, Pallas kernels for 9%

profile of v6, /device:TPU:0, one launch (start us, length us, event | category | flops | bytes accessed | tf_op | source)
XLA Modules:
  0.0 51.0 jit_solution(4218187581245625996)
XLA Ops:
  0.0 2.6 %shard_map.73 = bf16[1408,128]{1,0:T(8,128)(2,1)} custom-call(bf16[16,384]{1,0:T(8,128)(2,1)} %x_ref.1, bf16[27,24,384]{2,1,0:T(8,128)(2,1)} %w_ref.1, s32[1]{0:T(128)} %bitcast.side_ref), custom_call_target="tpu_custom_call" | custom-call | tf_op jit(solution)/shard_map/pallas_call | solution.py:259
  2.6 7.4 %all-to-all-start = ((bf16[16,88,128]{2,1,0:T(8,128)(2,1)}), bf16[16,88,128]{2,1,0:T(8,128)(2,1)S(1)}, u32[]{:S(2)}, u32[]{:S(2)}) async-start(bf16[16,88,128]{2,1,0:T(8,128)(2,1)} %bitcast.19), calls=%async_computation | async-start | bytes 720896 | tf_op jit(solution)/shard_map/all_to_all | solution.py:262
  10.0 0.7 %pad_maximum_fusion.vectors_ref = f32[9,128]{1,0:T(8,128)S(1)} fusion(f32[3,128]{1,0:T(4,128)} %bitcast.22, f32[3,128]{1,0:T(4,128)} %bitcast.23, f32[3,128]{1,0:T(4,128)} %bitcast.24), kind=kLoop, calls=%fused_computation | loop fusion | flops 2304 | bytes 9216 | tf_op jit(solution)/shard_map/concatenate | solution.py:273
  10.8 10.9 %all-to-all-done = bf16[16,88,128]{2,1,0:T(8,128)(2,1)S(1)} async-done(((bf16[16,88,128]{2,1,0:T(8,128)(2,1)}), bf16[16,88,128]{2,1,0:T(8,128)(2,1)S(1)}, u32[]{:S(2)}, u32[]{:S(2)}) %all-to-all-start) | async-done | bytes 360480 | tf_op jit(solution)/shard_map/all_to_all | solution.py:262
  21.7 0.2 collective-permute-start.1
  21.9 0.0 copy-start
  21.9 1.0 %copy-done = bf16[27,16,384]{2,1,0:T(8,128)(2,1)S(1)} copy-done((bf16[27,16,384]{2,1,0:T(8,128)(2,1)S(1)}, bf16[27,16,384]{2,1,0:T(8,128)(2,1)}, u32[]{:S(2)}) %copy-start) | copy-done | bytes 331800
  22.9 0.0 copy-start.1
  22.9 0.5 shard_map.74.params_ref
  23.4 1.6 %collective-permute-start = (bf16[1024,128]{1,0:T(8,128)(2,1)S(1)}, bf16[1024,128]{1,0:T(8,128)(2,1)S(1)}, u32[]{:S(2)}, u32[]{:S(2)}) collective-permute-start(bf16[1024,128]{1,0:T(8,128)(2,1)S(1)} %bitcast.20), channel_id=1, source_target_pairs={{0,16},{16,0},{1,17},{17,1},{2,18},{18,2},{3,19},{19,3},{4,20},{20... | collective-permute-start | bytes 786440 | tf_op jit(solution)/shard_map/ppermute | solution.py:278
  24.9 0.0 collective-permute-done.1.lat_ref
  24.9 4.1 %shard_map.75 = (bf16[3072,768]{1,0:T(8,128)(2,1)S(1)}, f32[8,24,768]{2,1,0:T(8,128)S(1)}) custom-call(bf16[1408,128]{1,0:T(8,128)(2,1)S(1)} %bitcast.14, bf16[384,128]{1,0:T(8,128)(2,1)S(1)} %collective-permute-done.1.lat_ref, bf16[432,640]{1,0:T(8,128)(2,1)S(1)} %shard_map.74.params_ref, s32[1]{0:T(128)} %bitcast.10.odd_ref), custom_call_target="tpu_custom_call" | custom-call | flops 2038431744 | bytes 20000000 | tf_op jit(solution)/shard_map/pallas_call | solution.py:281
  29.0 3.0 %collective-permute-done.w_ref = bf16[1024,128]{1,0:T(8,128)(2,1)S(1)} collective-permute-done((bf16[1024,128]{1,0:T(8,128)(2,1)S(1)}, bf16[1024,128]{1,0:T(8,128)(2,1)S(1)}, u32[]{:S(2)}, u32[]{:S(2)}) %collective-permute-start) | collective-permute-done | bytes 262176 | tf_op jit(solution)/shard_map/ppermute | solution.py:278
  32.1 0.0 copy-done.1
  32.1 4.4 %shard_map.76 = bf16[384,384]{1,0:T(8,128)(2,1)S(1)} custom-call(bf16[1408,128]{1,0:T(8,128)(2,1)S(1)} %bitcast.15, bf16[1024,128]{1,0:T(8,128)(2,1)S(1)} %collective-permute-done.w_ref, bf16[3072,768]{1,0:T(8,128)(2,1)S(1)} %get-tuple-element.11.x_ref, f32[8,24,768]{2,1,0:T(8,128)S(1)} %get-tuple-element.12.stream_ref, s32[1]{0:T(128)} %bitcast.side_ref, ...), custom_call_target="tpu_custom_call" | custom-call | flops 3057647616 | bytes 20000000 | tf_op jit(solution)/shard_map/pallas_call | solution.py:291
  36.5 13.7 %all_to_all.22 = bf16[16,24,384]{2,1,0:T(8,128)(2,1)S(1)} all-to-all(bf16[16,24,384]{2,1,0:T(8,128)(2,1)S(1)} %bitcast.17), channel_id=1, replica_groups=mesh['groups'=2,'tm'=16] {'tm'}, dimensions={0} | all-to-all | bytes 589824 | tf_op jit(solution)/shard_map/all_to_all | solution.py:301
  50.2 0.9 %shard_map.77 = bf16[384,384]{1,0:T(8,128)(2,1)} custom-call(bf16[384,384]{1,0:T(8,128)(2,1)S(1)} %bitcast.16), custom_call_target="tpu_custom_call" | custom-call | tf_op jit(solution)/shard_map/pallas_call | solution.py:302
  (2 shorter events, 0.0 us)
Async XLA Ops:
  2.6 19.1 %all-to-all-start = ((bf16[16,88,128]{2,1,0:T(8,128)(2,1)}), bf16[16,88,128]{2,1,0:T(8,128)(2,1)S(1)}, u32[]{:S(2)}, u32[]{:S(2)}) async-start(bf16[16,88,128]{2,1,0:T(8,128)(2,1)} %bitcast.19), calls=%async_computation | async-start | bytes 720896 | tf_op jit(solution)/shard_map/all_to_all | solution.py:262
  21.7 3.2 %collective-permute-start.1 = (bf16[384,128]{1,0:T(8,128)(2,1)S(1)}, bf16[384,128]{1,0:T(8,128)(2,1)S(1)}, u32[]{:S(2)}, u32[]{:S(2)}) collective-permute-start(bf16[384,128]{1,0:T(8,128)(2,1)S(1)} %bitcast.21), channel_id=1, source_target_pairs={{0,1},{1,0},{2,3},{3,2},{4,5},{5,4},{6,7},{7,6},{8,9},{9,8},{10,11... | collective-permute-start | bytes 294920 | tf_op jit(solution)/shard_map/ppermute | solution.py:280
  21.9 1.0 %copy-start = (bf16[27,16,384]{2,1,0:T(8,128)(2,1)S(1)}, bf16[27,16,384]{2,1,0:T(8,128)(2,1)}, u32[]{:S(2)}) copy-start(bf16[27,16,384]{2,1,0:T(8,128)(2,1)} %param.9) | copy-start | bytes 995332
  22.9 9.2 %copy-start.1 = (s32[8]{0:T(128)S(1)}, s32[8]{0:T(128)}, u32[]{:S(2)}) copy-start(s32[8]{0:T(128)} %count_ref.1) | copy-start | bytes 100
  23.4 8.7 %collective-permute-start = (bf16[1024,128]{1,0:T(8,128)(2,1)S(1)}, bf16[1024,128]{1,0:T(8,128)(2,1)S(1)}, u32[]{:S(2)}, u32[]{:S(2)}) collective-permute-start(bf16[1024,128]{1,0:T(8,128)(2,1)S(1)} %bitcast.20), channel_id=1, source_target_pairs={{0,16},{16,0},{1,17},{17,1},{2,18},{18,2},{3,19},{19,3},{4,20},{20... | collective-permute-start | bytes 786440 | tf_op jit(solution)/shard_map/ppermute | solution.py:278

commit v7 on v6

--- a/solution.py
+++ b/solution.py
@@ -17,6 +17,7 @@
 LANES = PROMPT_SAMPLES * HW
 VMEM = pl.BlockSpec(memory_space=pltpu.VMEM)
 SMEM = pl.BlockSpec(memory_space=pltpu.SMEM)
+ANY = pl.BlockSpec(memory_space=pl.ANY)
 
 
 def shift_mask(j, k):
@@ -53,8 +54,13 @@
     return places, -(-longest // 128) * 128
 
 
-def parcels_kernel(n, x_ref, w_ref, side_ref, o_ref):
+def parcels_kernel(n, x_hbm, w_hbm, side_ref, o_hbm, x_ref, w_ref, o_ref, in_sem, out_sem):
     own = C // n
+    get_x = pltpu.make_async_copy(x_hbm, x_ref, in_sem.at[0])
+    get_w = pltpu.make_async_copy(w_hbm, w_ref, in_sem.at[1])
+    get_x.start()
+    get_w.start()
+    get_x.wait()
     x = x_ref[...].astype(jnp.float32)
     rows = []
     for b in range(x.shape[0] // PROMPT_SAMPLES):
@@ -64,7 +70,9 @@
             rows.append(jnp.concatenate(pieces, axis=1))
     rows = jnp.concatenate(rows, axis=0)
     tiles = [rows[:, t * 128 : (t + 1) * 128] for t in range(LANES // 128)]
+    get_w.wait()
     w = w_ref[...].astype(jnp.float32).reshape(3, 9, own // 8, 8, C)
+    puts = []
     places, width = packing(own)
     left = jnp.broadcast_to(side_ref[0] == 0, (8, width))
     half = len(tiles) // 2
@@ -87,6 +95,12 @@
             both += tiles[half:] if e % 2 else tiles[:half]
         both = jnp.concatenate(both, axis=0).astype(jnp.bfloat16)
         o_ref[d // 2 * both.shape[0] : (d // 2 + 1) * both.shape[0], :] = both
+        if d % 4 == 2:
+            rows = pl.ds((d // 4) * 2 * both.shape[0], 2 * both.shape[0])
+            puts.append(pltpu.make_async_copy(o_ref.at[rows], o_hbm.at[rows], out_sem.at[d // 4]))
+            puts[-1].start()
+    for put in puts:
+        put.wait()
 
 
 def column(rows):
@@ -257,7 +271,18 @@
     height = packing(own)[1] // 16
     extra = each * LANES // 256
     parcels = call(
-        functools.partial(parcels_kernel, n), shape((n * (height + extra), 128), bf16), [VMEM, VMEM, SMEM], VMEM, limit=58
+        functools.partial(parcels_kernel, n),
+        shape((n * (height + extra), 128), bf16),
+        [ANY, ANY, SMEM],
+        ANY,
+        [
+            pltpu.VMEM(latents.shape, bf16),
+            pltpu.VMEM(kernel.shape, bf16),
+            pltpu.VMEM((n * (height + extra), 128), bf16),
+            pltpu.SemaphoreType.DMA((2,)),
+            pltpu.SemaphoreType.DMA((n // 4,)),
+        ],
+        limit=58,
     )(latents, kernel, side)
     got = lax.all_to_all(parcels, "tm", split_axis=0, concat_axis=0, tiled=True)
     params = call(
@@ -274,8 +299,7 @@
         first,
     )
     split = got.reshape(n, height + extra, 128)
-    other, params = lax.optimization_barrier((split[:, :height].reshape(n * height, 128), params))
-    other = lax.ppermute(other, "groups", [(0, 1), (1, 0)])
+    other = lax.ppermute(split[:, :height].reshape(n * height, 128), "groups", [(0, 1), (1, 0)])
     lats = split[:, height:].reshape(-1, 128)
     lats = lax.ppermute(lats, "tm", [(i, i ^ 1) for i in range(n)])
     active, stream = call(
@@ -384,7 +408,7 @@
 def solution(mesh):
     n = mesh.shape["tm"]
     cells = BLOCK_FRAMES * LATENT_CHANNELS * HW
-    fits = mesh.shape["groups"] == 2 and 9 * (C // n) <= 256 and n % 2 == 0 and LANES % 256 == 0
+    fits = mesh.shape["groups"] == 2 and 9 * (C // n) <= 256 and n % 4 == 0 and LANES % 256 == 0
     whole_rows = fits and cells % (n * HW) == 0 and C % n == 0 and (C // n) % 8 == 0 and n % PROMPT_SAMPLES == 0
     body = functools.partial(by_channel, n) if whole_rows else by_block
     in_specs = (P("groups", "tm"), P("groups"), P(), P(), P(), P(None, "tm", None), P())

time: 51.4 us -> 49.9 us (0.971)
  blocking collectives: 13.7 us -> 32.8 us
  waiting for transfers between devices: 14 us -> 1.06 us
  starting transfers between devices: 9.12 us -> 1.74 us
    all_to_all x0 -> x1, blocking collectives: none -> 19.1 us  [by_channel(): got = lax.all_to_all(parcels, 'tm', split_axis=0, concat_axis=0, tiled=True)]
    all_to_all x1 -> x0, waiting for transfers between devices: 10.9 us -> none  [by_channel(): got = lax.all_to_all(parcels, 'tm', split_axis=0, concat_axis=0, tiled=True)]
    all_to_all x1 -> x0, starting transfers between devices: 7.39 us -> none  [by_channel(): got = lax.all_to_all(parcels, 'tm', split_axis=0, concat_axis=0, tiled=True)]
    ppermute x1, waiting for transfers between devices: 3.04 us -> 1.06 us  [by_channel(): lax.ppermute(split[:, :height].reshape(n * height, 128), 'groups', [(0, 1...]
  transfers between devices with their start and end apart: 3 -> 2, of which waited for: 2 -> 1; matrix products, arithmetic and copies ran while one was open for 1% -> 1% of each run, Pallas kernels for 9% -> 9%
where the time goes in v7:
time: 49.9 us; the launch traced here: 49.5 us
  blocking collectives  32.8 us (66%)
  Pallas kernels  12.2 us (24%)
  starting transfers between devices  1.74 us (3%)
  waiting for transfers between devices  1.06 us (2%)
  local copies, waits for them, and re-layouts  1 us (2%)
  other arithmetic  0.72 us (1%)
    all_to_all x1, blocking collectives, by_channel(): got = lax.all_to_all(parcels, 'tm', split_axis=0, concat_axis=0, tiled=True)  19.1 us
    all_to_all x1, blocking collectives, by_channel(): out = lax.all_to_all(out, 'tm', split_axis=0, concat_axis=0, tiled=True)  13.7 us
    pallas_call x1, Pallas kernels, by_channel(): call(functools.partial(branch_kernel, n), shape((n * own, BLOCK_FRAMES *...  4.44 us
    pallas_call x1, Pallas kernels, by_channel(): call(functools.partial(active_kernel, n), (shape((frames * C, LANES), bf1...  3.89 us
    pallas_call x1, Pallas kernels, by_channel(): call(functools.partial(parcels_kernel, n), shape((n * (height + extra), 1...  2.54 us
    ppermute x1, starting transfers between devices, by_channel(): lax.ppermute(split[:, :height].reshape(n * height, 128), 'groups', [(0, 1...  1.56 us
    ppermute x1, waiting for transfers between devices, by_channel(): lax.ppermute(split[:, :height].reshape(n * height, 128), 'groups', [(0, 1...  1.06 us
  transfers between devices with their start and end apart: 2, of which 1 were waited for; matrix products, arithmetic and copies ran while one was open for 1% of the time, Pallas kernels for 9%

profile of v7, /device:TPU:0, one launch (start us, length us, event | category | flops | bytes accessed | tf_op | source)
XLA Modules:
  0.0 49.5 jit_solution(14873129777779760859)
XLA Ops:
  0.0 2.5 %shard_map.73 = bf16[1408,128]{1,0:T(8,128)(2,1)} custom-call(bf16[16,384]{1,0:T(8,128)(2,1)} %x_hbm.1, bf16[27,24,384]{2,1,0:T(8,128)(2,1)} %w_hbm.1, s32[1]{0:T(128)} %bitcast.side_ref), custom_call_target="tpu_custom_call" | custom-call | tf_op jit(solution)/shard_map/pallas_call | solution.py:273
  2.6 19.1 %all_to_all.22 = bf16[16,88,128]{2,1,0:T(8,128)(2,1)S(1)} all-to-all(bf16[16,88,128]{2,1,0:T(8,128)(2,1)} %bitcast.19), channel_id=1, replica_groups=mesh['groups'=2,'tm'=16] {'tm'}, dimensions={0} | all-to-all | bytes 720896 | tf_op jit(solution)/shard_map/all_to_all | solution.py:287
  21.6 0.2 collective-permute-start.1
  21.8 1.6 %collective-permute-start = (bf16[1024,128]{1,0:T(8,128)(2,1)S(1)}, bf16[1024,128]{1,0:T(8,128)(2,1)S(1)}, u32[]{:S(2)}, u32[]{:S(2)}) collective-permute-start(bf16[1024,128]{1,0:T(8,128)(2,1)S(1)} %bitcast.20), channel_id=1, source_target_pairs={{0,16},{16,0},{1,17},{17,1},{2,18},{18,2},{3,19},{19,3},{4,20},{20... | collective-permute-start | bytes 786440 | tf_op jit(solution)/shard_map/ppermute | solution.py:302
  23.4 0.7 %pad_maximum_fusion.vectors_ref = f32[9,128]{1,0:T(8,128)S(1)} fusion(f32[3,128]{1,0:T(4,128)} %bitcast.22, f32[3,128]{1,0:T(4,128)} %bitcast.23, f32[3,128]{1,0:T(4,128)} %bitcast.24), kind=kLoop, calls=%fused_computation | loop fusion | flops 2304 | bytes 9216 | tf_op jit(solution)/shard_map/concatenate | solution.py:298
  24.1 0.0 copy-start.1
  24.1 0.0 copy-start
  24.1 1.0 %copy-done = bf16[27,16,384]{2,1,0:T(8,128)(2,1)S(1)} copy-done((bf16[27,16,384]{2,1,0:T(8,128)(2,1)S(1)}, bf16[27,16,384]{2,1,0:T(8,128)(2,1)}, u32[]{:S(2)}) %copy-start) | copy-done | bytes 331800
  25.1 0.5 shard_map.74.params_ref
  25.6 0.0 collective-permute-done.1.lat_ref
  25.6 3.9 %shard_map.75 = (bf16[3072,768]{1,0:T(8,128)(2,1)S(1)}, f32[8,24,768]{2,1,0:T(8,128)S(1)}) custom-call(bf16[1408,128]{1,0:T(8,128)(2,1)S(1)} %bitcast.14, bf16[384,128]{1,0:T(8,128)(2,1)S(1)} %collective-permute-done.1.lat_ref, bf16[432,640]{1,0:T(8,128)(2,1)S(1)} %shard_map.74.params_ref, s32[1]{0:T(128)} %bitcast.10.odd_ref), custom_call_target="tpu_custom_call" | custom-call | flops 2038431744 | bytes 20000000 | tf_op jit(solution)/shard_map/pallas_call | solution.py:305
  29.5 1.1 %collective-permute-done.w_ref = bf16[1024,128]{1,0:T(8,128)(2,1)S(1)} collective-permute-done((bf16[1024,128]{1,0:T(8,128)(2,1)S(1)}, bf16[1024,128]{1,0:T(8,128)(2,1)S(1)}, u32[]{:S(2)}, u32[]{:S(2)}) %collective-permute-start) | collective-permute-done | bytes 262176 | tf_op jit(solution)/shard_map/ppermute | solution.py:302
  30.5 0.0 copy-done.1
  30.5 4.4 %shard_map.76 = bf16[384,384]{1,0:T(8,128)(2,1)S(1)} custom-call(bf16[1408,128]{1,0:T(8,128)(2,1)S(1)} %bitcast.15, bf16[1024,128]{1,0:T(8,128)(2,1)S(1)} %collective-permute-done.w_ref, bf16[3072,768]{1,0:T(8,128)(2,1)S(1)} %get-tuple-element.7.x_ref, f32[8,24,768]{2,1,0:T(8,128)S(1)} %get-tuple-element.8.stream_ref, s32[1]{0:T(128)} %bitcast.side_ref, ...), custom_call_target="tpu_custom_call" | custom-call | flops 3057647616 | bytes 20000000 | tf_op jit(solution)/shard_map/pallas_call | solution.py:315
  35.0 13.7 %all_to_all.23 = bf16[16,24,384]{2,1,0:T(8,128)(2,1)S(1)} all-to-all(bf16[16,24,384]{2,1,0:T(8,128)(2,1)S(1)} %bitcast.17), channel_id=1, replica_groups=mesh['groups'=2,'tm'=16] {'tm'}, dimensions={0} | all-to-all | bytes 589824 | tf_op jit(solution)/shard_map/all_to_all | solution.py:325
  48.7 0.9 %shard_map.77 = bf16[384,384]{1,0:T(8,128)(2,1)} custom-call(bf16[384,384]{1,0:T(8,128)(2,1)S(1)} %bitcast.16), custom_call_target="tpu_custom_call" | custom-call | tf_op jit(solution)/shard_map/pallas_call | solution.py:326
  (2 shorter events, 0.0 us)
Async XLA Ops:
  21.6 3.9 %collective-permute-start.1 = (bf16[384,128]{1,0:T(8,128)(2,1)S(1)}, bf16[384,128]{1,0:T(8,128)(2,1)S(1)}, u32[]{:S(2)}, u32[]{:S(2)}) collective-permute-start(bf16[384,128]{1,0:T(8,128)(2,1)S(1)} %bitcast.21), channel_id=1, source_target_pairs={{0,1},{1,0},{2,3},{3,2},{4,5},{5,4},{6,7},{7,6},{8,9},{9,8},{10,11... | collective-permute-start | bytes 294920 | tf_op jit(solution)/shard_map/ppermute | solution.py:304
  21.8 8.7 %collective-permute-start = (bf16[1024,128]{1,0:T(8,128)(2,1)S(1)}, bf16[1024,128]{1,0:T(8,128)(2,1)S(1)}, u32[]{:S(2)}, u32[]{:S(2)}) collective-permute-start(bf16[1024,128]{1,0:T(8,128)(2,1)S(1)} %bitcast.20), channel_id=1, source_target_pairs={{0,16},{16,0},{1,17},{17,1},{2,18},{18,2},{3,19},{19,3},{4,20},{20... | collective-permute-start | bytes 786440 | tf_op jit(solution)/shard_map/ppermute | solution.py:302
  24.1 6.4 %copy-start.1 = (s32[8]{0:T(128)S(1)}, s32[8]{0:T(128)}, u32[]{:S(2)}) copy-start(s32[8]{0:T(128)} %count_ref.1) | copy-start | bytes 100
  24.1 1.0 %copy-start = (bf16[27,16,384]{2,1,0:T(8,128)(2,1)S(1)}, bf16[27,16,384]{2,1,0:T(8,128)(2,1)}, u32[]{:S(2)}) copy-start(bf16[27,16,384]{2,1,0:T(8,128)(2,1)} %param.9) | copy-start | bytes 995332

commit v8 on v7

--- a/solution.py
+++ b/solution.py
@@ -54,7 +54,7 @@
     return places, -(-longest // 128) * 128
 
 
-def parcels_kernel(n, x_hbm, w_hbm, side_ref, o_hbm, x_ref, w_ref, o_ref, in_sem, out_sem):
+def parcels_kernel(n, x_hbm, w_hbm, side_ref, o_hbm, lat_ref, x_ref, w_ref, o_ref, in_sem, out_sem):
     own = C // n
     get_x = pltpu.make_async_copy(x_hbm, x_ref, in_sem.at[0])
     get_w = pltpu.make_async_copy(w_hbm, w_ref, in_sem.at[1])
@@ -68,14 +68,12 @@
             at = b * PROMPT_SAMPLES
             pieces = [x[r : r + 1, c * HW : (c + 1) * HW] for r in range(at, at + PROMPT_SAMPLES)]
             rows.append(jnp.concatenate(pieces, axis=1))
-    rows = jnp.concatenate(rows, axis=0)
-    tiles = [rows[:, t * 128 : (t + 1) * 128] for t in range(LANES // 128)]
+    lat_ref[...] = jnp.concatenate(rows, axis=0).astype(jnp.bfloat16)
     get_w.wait()
     w = w_ref[...].astype(jnp.float32).reshape(3, 9, own // 8, 8, C)
     puts = []
     places, width = packing(own)
     left = jnp.broadcast_to(side_ref[0] == 0, (8, width))
-    half = len(tiles) // 2
     for d in range(0, n, 2):
         both = []
         for e in (d, d + 1):
@@ -92,7 +90,6 @@
                 halves.append(jnp.concatenate(pieces, axis=1))
             share = jnp.where(left, halves[0], halves[1])
             both += [share[:, t * 128 : (t + 1) * 128] for t in range(width // 128)]
-            both += tiles[half:] if e % 2 else tiles[:half]
         both = jnp.concatenate(both, axis=0).astype(jnp.bfloat16)
         o_ref[d // 2 * both.shape[0] : (d // 2 + 1) * both.shape[0], :] = both
         if d % 4 == 2:
@@ -142,7 +139,7 @@
     o_ref[...] = jnp.concatenate([mine, after, full], axis=0).astype(jnp.bfloat16)
 
 
-def active_kernel(n, got_ref, lat_ref, params_ref, odd_ref, x_ref, stream_ref, col_ref):
+def active_kernel(n, near_ref, far_ref, params_ref, me_ref, x_ref, stream_ref, col_ref, lat_ref):
     own = C // n
     frames = n // PROMPT_SAMPLES * BLOCK_FRAMES
     each = LATENT_CHANNELS * BLOCK_FRAMES // n
@@ -152,12 +149,17 @@
     ones = (lax.broadcasted_iota(jnp.int32, (16, LANES), 0) < 3).astype(jnp.float32).astype(jnp.bfloat16)
     per_frame = LATENT_CHANNELS // each
     blocks = n // PROMPT_SAMPLES
-    mine = got_ref[...].astype(jnp.float32).reshape(n, -1, 128)[:, packing(own)[1] // 16 :]
-    other = lat_ref[...].astype(jnp.float32).reshape(mine.shape)
-    even = jnp.broadcast_to(odd_ref[0] == 0, mine.shape)
-    lats = jnp.concatenate([jnp.where(even, mine, other), jnp.where(even, other, mine)], axis=1)
-    lats = lats.reshape(n, LANES // 128, blocks * each, 128)
-    lats = jnp.concatenate([lats[:, t] for t in range(LANES // 128)], axis=2)
+    rows = blocks * each
+    lat_ref[: n // 2 * rows] = near_ref[...].astype(jnp.float32)
+    lat_ref[n // 2 * rows :] = far_ref[...].astype(jnp.float32)
+    lats = []
+    for p in range(n):
+        apart = jnp.bitwise_xor(me_ref[0], p)
+        slot, bits = 0, n.bit_length() - 1
+        for bit in range(bits):
+            slot = slot + ((apart >> bit) & 1) * (1 << (bits - 1 - bit))
+        lats.append(lat_ref[pl.ds(pl.multiple_of(slot * rows, 8), rows), :])
+    lats = jnp.stack(lats)
     lats = lats.reshape(BLOCK_FRAMES, per_frame, blocks, each, LANES)
     for f in range(frames):
         b, g = divmod(f, BLOCK_FRAMES)
@@ -190,7 +192,7 @@
         x = x.reshape(n, width // 128, 8, 128)
         return jnp.concatenate([x[:, t] for t in range(width // 128)], axis=2).reshape(n * 8, width)
 
-    mine = lanes(got_ref[...].astype(jnp.float32).reshape(n, -1, 128)[:, : width // 16])
+    mine = lanes(got_ref[...].astype(jnp.float32))
     other = lanes(w_ref[...].astype(jnp.float32))
     left = jnp.broadcast_to(side_ref[0] == 0, other.shape)
     halves = (jnp.where(left, mine, other), jnp.where(left, other, mine))
@@ -267,18 +269,17 @@
     bf16, f32 = jnp.bfloat16, jnp.float32
     side = lax.axis_index("groups").astype(jnp.int32).reshape(1)
     each = latents.shape[1] // HW * (n // PROMPT_SAMPLES)
-    odd = (lax.axis_index("tm") % 2).astype(jnp.int32).reshape(1)
+    me = lax.axis_index("tm").astype(jnp.int32).reshape(1)
     height = packing(own)[1] // 16
-    extra = each * LANES // 256
-    parcels = call(
+    parcels, lats = call(
         functools.partial(parcels_kernel, n),
-        shape((n * (height + extra), 128), bf16),
+        (shape((n * height, 128), bf16), shape((each, LANES), bf16)),
         [ANY, ANY, SMEM],
-        ANY,
+        (ANY, VMEM),
         [
             pltpu.VMEM(latents.shape, bf16),
             pltpu.VMEM(kernel.shape, bf16),
-            pltpu.VMEM((n * (height + extra), 128), bf16),
+            pltpu.VMEM((n * height, 128), bf16),
             pltpu.SemaphoreType.DMA((2,)),
             pltpu.SemaphoreType.DMA((n // 4,)),
         ],
@@ -298,20 +299,25 @@
         jnp.concatenate([entry_bias, gain, bias]).reshape(-1, 128),
         first,
     )
-    split = got.reshape(n, height + extra, 128)
-    other = lax.ppermute(split[:, :height].reshape(n * height, 128), "groups", [(0, 1), (1, 0)])
-    lats = split[:, height:].reshape(-1, 128)
-    lats = lax.ppermute(lats, "tm", [(i, i ^ 1) for i in range(n)])
+    bit = n // 2
+    while True:
+        far = lax.ppermute(lats, "tm", [(i, i ^ bit) for i in range(n)])
+        if bit == 1:
+            break
+        lats = jnp.concatenate([lats, far], axis=0)
+        bit //= 2
+    got, far = lax.optimization_barrier((got, far))
+    other = lax.ppermute(got, "groups", [(0, 1), (1, 0)])
     active, stream = call(
         functools.partial(active_kernel, n),
         (shape((frames * C, LANES), bf16), shape((frames, own, LANES), f32)),
         [VMEM, VMEM, VMEM, SMEM],
         (VMEM, VMEM),
-        [pltpu.VMEM((frames * 9 * LATENT_CHANNELS, LANES), bf16)],
+        [pltpu.VMEM((frames * 9 * LATENT_CHANNELS, LANES), bf16), pltpu.VMEM((n * each, LANES), f32)],
         flops=2 * frames * LANES * 432 * C,
         moved=20_000_000,
         limit=24,
-    )(got, lats, params, odd)
+    )(lats, far, params, me)
     out = call(
         functools.partial(branch_kernel, n),
         shape((n * own, BLOCK_FRAMES * HW), bf16),
@@ -408,7 +414,7 @@
 def solution(mesh):
     n = mesh.shape["tm"]
     cells = BLOCK_FRAMES * LATENT_CHANNELS * HW
-    fits = mesh.shape["groups"] == 2 and 9 * (C // n) <= 256 and n % 4 == 0 and LANES % 256 == 0
+    fits = mesh.shape["groups"] == 2 and 9 * (C // n) <= 256 and n % 4 == 0 and n & (n - 1) == 0
     whole_rows = fits and cells % (n * HW) == 0 and C % n == 0 and (C // n) % 8 == 0 and n % PROMPT_SAMPLES == 0
     body = functools.partial(by_channel, n) if whole_rows else by_block
     in_specs = (P("groups", "tm"), P("groups"), P(), P(), P(), P(None, "tm", None), P())

time: 49.9 us -> 54.4 us (1.090)
  blocking collectives: 32.8 us -> 16.2 us
  starting transfers between devices: 1.74 us -> 12.6 us
  waiting for transfers between devices: 1.06 us -> 8.37 us
  other arithmetic: 0.72 us -> 2.14 us
  local copies, waits for them, and re-layouts: 1 us -> 1.7 us
  Pallas kernels: 12.2 us -> 12.8 us
    all_to_all x1 -> x0, blocking collectives: 19.1 us -> none  [by_channel(): got = lax.all_to_all(parcels, 'tm', split_axis=0, concat_axis=0, tiled=True)]
    ppermute x2 -> x5, waiting for transfers between devices: 1.06 us -> 8.37 us  [the longest x4 7.59 us: by_channel(): far = lax.ppermute(lats, 'tm', [(i, i ^ bit) for i in range(n)])]
    ppermute x2 -> x5, starting transfers between devices: 1.74 us -> 8.64 us  [the longest x4 7.15 us: by_channel(): far = lax.ppermute(lats, 'tm', [(i, i ^ bit) for i in range(n)])]
    all_to_all x0 -> x1, starting transfers between devices: none -> 3.91 us  [by_channel(): got = lax.all_to_all(parcels, 'tm', split_axis=0, concat_axis=0, tiled=True)]
    all_to_all x1, blocking collectives: 13.7 us -> 16.2 us  [by_channel(): out = lax.all_to_all(out, 'tm', split_axis=0, concat_axis=0, tiled=True)]
    concatenate x0 -> x2, other arithmetic: none -> 1.42 us  [by_channel(): lats = jnp.concatenate([lats, far], axis=0)]
    unnamed x4 -> x7, local copies, waits for them, and re-layouts: 0.97 us -> 1.69 us
    pallas_call x1, Pallas kernels: 2.54 us -> 3.13 us  [by_channel(): call(functools.partial(parcels_kernel, n), (shape((n * height, 128), bf16...]
  transfers between devices with their start and end apart: 2 -> 6, of which waited for: 1 -> 4; matrix products, arithmetic and copies ran while one was open for 1% -> 5% of each run, Pallas kernels for 9% -> 8%
where the time goes in v8:
time: 54.4 us; the launch traced here: 53.8 us
  blocking collectives  16.2 us (30%)
  Pallas kernels  12.8 us (24%)
  starting transfers between devices  12.6 us (23%)
  waiting for transfers between devices  8.37 us (15%)
  other arithmetic  2.14 us (4%)
  local copies, waits for them, and re-layouts  1.7 us (3%)
    all_to_all x1, blocking collectives, by_channel(): out = lax.all_to_all(out, 'tm', split_axis=0, concat_axis=0, tiled=True)  16.2 us
    ppermute x4, waiting for transfers between devices, by_channel(): far = lax.ppermute(lats, 'tm', [(i, i ^ bit) for i in range(n)])  7.59 us
    ppermute x4, starting transfers between devices, by_channel(): far = lax.ppermute(lats, 'tm', [(i, i ^ bit) for i in range(n)])  7.15 us
    pallas_call x1, Pallas kernels, by_channel(): call(functools.partial(branch_kernel, n), shape((n * own, BLOCK_FRAMES *...  4.43 us
    pallas_call x1, Pallas kernels, by_channel(): call(functools.partial(active_kernel, n), (shape((frames * C, LANES), bf1...  3.92 us
    all_to_all x1, starting transfers between devices, by_channel(): got = lax.all_to_all(parcels, 'tm', split_axis=0, concat_axis=0, tiled=True)  3.91 us
    pallas_call x1, Pallas kernels, by_channel(): call(functools.partial(parcels_kernel, n), (shape((n * height, 128), bf16...  3.13 us
    unnamed x7, local copies, waits for them, and re-layouts  1.69 us
  transfers between devices with their start and end apart: 6, of which 4 were waited for; matrix products, arithmetic and copies ran while one was open for 5% of the time, Pallas kernels for 8%

profile of v8, /device:TPU:0, one launch (start us, length us, event | category | flops | bytes accessed | tf_op | source)
XLA Modules:
  0.0 53.8 jit_solution(9074365977073030192)
XLA Ops:
  0.0 3.1 %shard_map.73 = (bf16[1024,128]{1,0:T(8,128)(2,1)}, bf16[8,768]{1,0:T(8,128)(2,1)}) custom-call(bf16[16,384]{1,0:T(8,128)(2,1)} %x_hbm.1, bf16[27,24,384]{2,1,0:T(8,128)(2,1)} %w_hbm.1, s32[1]{0:T(128)} %bitcast.side_ref), custom_call_target="tpu_custom_call" | custom-call | tf_op jit(solution)/shard_map/pallas_call | solution.py:274
  3.1 4.1 %collective-permute-start = (bf16[8,768]{1,0:T(8,128)(2,1)}, bf16[8,768]{1,0:T(8,128)(2,1)S(1)}, u32[]{:S(2)}, u32[]{:S(2)}) collective-permute-start(bf16[8,768]{1,0:T(8,128)(2,1)} %get-tuple-element.12), channel_id=1, source_target_pairs={{0,8},{1,9},{2,10},{3,11},{4,12},{5,13},{6,14},{7,15},{8,0},{9,1},... | collective-permute-start | bytes 36872 | tf_op jit(solution)/shard_map/ppermute | solution.py:304
  7.2 3.9 %all-to-all-start = ((bf16[16,64,128]{2,1,0:T(8,128)(2,1)}), bf16[16,64,128]{2,1,0:T(8,128)(2,1)S(1)}, u32[]{:S(2)}, u32[]{:S(2)}) async-start(bf16[16,64,128]{2,1,0:T(8,128)(2,1)} %bitcast.17), calls=%async_computation | async-start | bytes 524288 | tf_op jit(solution)/shard_map/all_to_all | solution.py:288
  11.2 0.7 %constant_dynamic-update-slice_fusion.3 = bf16[64,768]{1,0:T(8,128)(2,1)S(1)} fusion(bf16[8,768]{1,0:T(8,128)(2,1)} %get-tuple-element.12), kind=kLoop, calls=%fused_computation.5 | loop fusion | bytes 24576
  11.9 0.0 collective-permute-done
  11.9 0.7 %pad_maximum_fusion.1 = bf16[16,768]{1,0:T(8,128)(2,1)S(1)} fusion(bf16[8,768]{1,0:T(8,128)(2,1)S(1)} %collective-permute-done, bf16[8,768]{1,0:T(8,128)(2,1)} %get-tuple-element.12), kind=kLoop, calls=%fused_computation.1 | loop fusion | flops 49152 | bytes 49152 | tf_op jit(solution)/shard_map/concatenate | solution.py:307
  12.6 1.9 %collective-permute-start.1 = (bf16[16,768]{1,0:T(8,128)(2,1)S(1)}, bf16[16,768]{1,0:T(8,128)(2,1)S(1)}, u32[]{:S(2)}, u32[]{:S(2)}) collective-permute-start(bf16[16,768]{1,0:T(8,128)(2,1)S(1)} %pad_maximum_fusion.1), channel_id=1, source_target_pairs={{0,4},{1,5},{2,6},{3,7},{4,0},{5,1},{6,2},{7,3},{8,12},{9,13},{10,... | collective-permute-start | bytes 73736 | tf_op jit(solution)/shard_map/ppermute | solution.py:304
  14.5 3.3 %collective-permute-done.1 = bf16[16,768]{1,0:T(8,128)(2,1)S(1)} collective-permute-done((bf16[16,768]{1,0:T(8,128)(2,1)S(1)}, bf16[16,768]{1,0:T(8,128)(2,1)S(1)}, u32[]{:S(2)}, u32[]{:S(2)}) %collective-permute-start.1) | collective-permute-done | bytes 24608 | tf_op jit(solution)/shard_map/ppermute | solution.py:304
  17.8 0.7 %pad_maximum_fusion = bf16[32,768]{1,0:T(8,128)(2,1)S(1)} fusion(bf16[16,768]{1,0:T(8,128)(2,1)S(1)} %collective-permute-done.1, bf16[8,768]{1,0:T(8,128)(2,1)S(1)} %collective-permute-done, bf16[8,768]{1,0:T(8,128)(2,1)} %get-tuple-element.12), kind=kLoop, calls=%fused_computation | loop fusion | flops 147456 | bytes 98304 | tf_op jit(solution)/shard_map/concatenate | solution.py:307
  18.5 1.1 %collective-permute-start.2 = (bf16[32,768]{1,0:T(8,128)(2,1)S(1)}, bf16[32,768]{1,0:T(8,128)(2,1)S(1)}, u32[]{:S(2)}, u32[]{:S(2)}) collective-permute-start(bf16[32,768]{1,0:T(8,128)(2,1)S(1)} %pad_maximum_fusion), channel_id=1, source_target_pairs={{0,2},{1,3},{2,0},{3,1},{4,6},{5,7},{6,4},{7,5},{8,10},{9,11},{10,... | collective-permute-start | bytes 147464 | tf_op jit(solution)/shard_map/ppermute | solution.py:304
  19.7 3.0 %collective-permute-done.2 = bf16[32,768]{1,0:T(8,128)(2,1)S(1)} collective-permute-done((bf16[32,768]{1,0:T(8,128)(2,1)S(1)}, bf16[32,768]{1,0:T(8,128)(2,1)S(1)}, u32[]{:S(2)}, u32[]{:S(2)}) %collective-permute-start.2) | collective-permute-done | bytes 49184 | tf_op jit(solution)/shard_map/ppermute | solution.py:304
  22.6 0.0 collective-permute-start.3
  22.7 1.3 %collective-permute-done.3.far_ref = bf16[64,768]{1,0:T(8,128)(2,1)S(1)} collective-permute-done((bf16[64,768]{1,0:T(8,128)(2,1)S(1)}, bf16[64,768]{1,0:T(8,128)(2,1)S(1)}, u32[]{:S(2)}, u32[]{:S(2)}) %collective-permute-start.3) | collective-permute-done | bytes 98336 | tf_op jit(solution)/shard_map/ppermute | solution.py:304
  23.9 0.0 all-to-all-done
  24.0 1.5 %collective-permute-start.4 = (bf16[1024,128]{1,0:T(8,128)(2,1)S(1)}, bf16[1024,128]{1,0:T(8,128)(2,1)S(1)}, u32[]{:S(2)}, u32[]{:S(2)}) collective-permute-start(bf16[1024,128]{1,0:T(8,128)(2,1)S(1)} %bitcast.14), channel_id=1, source_target_pairs={{0,16},{16,0},{1,17},{17,1},{2,18},{18,2},{3,19},{19,3},{4,20},{20... | collective-permute-start | bytes 786440 | tf_op jit(solution)/shard_map/ppermute | solution.py:310
  25.4 0.7 %pad_maximum_fusion.2.vectors_ref = f32[9,128]{1,0:T(8,128)S(1)} fusion(f32[3,128]{1,0:T(4,128)} %bitcast.18, f32[3,128]{1,0:T(4,128)} %bitcast.19, f32[3,128]{1,0:T(4,128)} %bitcast.20), kind=kLoop, calls=%fused_computation.6 | loop fusion | flops 2304 | bytes 9216 | tf_op jit(solution)/shard_map/concatenate | solution.py:299
  26.2 1.0 %copy-done = bf16[27,16,384]{2,1,0:T(8,128)(2,1)S(1)} copy-done((bf16[27,16,384]{2,1,0:T(8,128)(2,1)S(1)}, bf16[27,16,384]{2,1,0:T(8,128)(2,1)}, u32[]{:S(2)}) %copy-start) | copy-done | bytes 331800
  27.1 0.5 shard_map.74.params_ref
  27.6 3.9 %shard_map.75 = (bf16[3072,768]{1,0:T(8,128)(2,1)S(1)}, f32[8,24,768]{2,1,0:T(8,128)S(1)}) custom-call(bf16[64,768]{1,0:T(8,128)(2,1)S(1)} %constant_dynamic-update-slice_fusion.near_ref, bf16[64,768]{1,0:T(8,128)(2,1)S(1)} %collective-permute-done.3.far_ref, bf16[432,640]{1,0:T(8,128)(2,1)S(1)} %shard_map.74.params_ref, s32[1]{0:T(128)} %bitcast.8.me_ref), custom_call_target="tpu_custom_call" | custom-call | flops 2038431744 | bytes 20000000 | tf_op jit(solution)/shard_map/pallas_call | solution.py:311
  31.5 0.8 %collective-permute-done.4.w_ref = bf16[1024,128]{1,0:T(8,128)(2,1)S(1)} collective-permute-done((bf16[1024,128]{1,0:T(8,128)(2,1)S(1)}, bf16[1024,128]{1,0:T(8,128)(2,1)S(1)}, u32[]{:S(2)}, u32[]{:S(2)}) %collective-permute-start.4) | collective-permute-done | bytes 262176 | tf_op jit(solution)/shard_map/ppermute | solution.py:310
  32.3 0.0 copy-done.1
  32.3 4.4 %shard_map.76 = bf16[384,384]{1,0:T(8,128)(2,1)S(1)} custom-call(bf16[1024,128]{1,0:T(8,128)(2,1)S(1)} %bitcast.15, bf16[1024,128]{1,0:T(8,128)(2,1)S(1)} %collective-permute-done.4.w_ref, bf16[3072,768]{1,0:T(8,128)(2,1)S(1)} %get-tuple-element.15.x_ref, f32[8,24,768]{2,1,0:T(8,128)S(1)} %get-tuple-element.16.stream_ref, s32[1]{0:T(128)} %bitcast.side_ref, ...), custom_call_target="tpu_custom_call" | custom-call | flops 3057647616 | bytes 20000000 | tf_op jit(solution)/shard_map/pallas_call | solution.py:321
  36.8 16.2 %all_to_all.23 = bf16[16,24,384]{2,1,0:T(8,128)(2,1)S(1)} all-to-all(bf16[16,24,384]{2,1,0:T(8,128)(2,1)S(1)} %bitcast.13), channel_id=1, replica_groups=mesh['groups'=2,'tm'=16] {'tm'}, dimensions={0} | all-to-all | bytes 589824 | tf_op jit(solution)/shard_map/all_to_all | solution.py:331
  53.0 0.9 %shard_map.77 = bf16[384,384]{1,0:T(8,128)(2,1)} custom-call(bf16[384,384]{1,0:T(8,128)(2,1)S(1)} %bitcast.12), custom_call_target="tpu_custom_call" | custom-call | tf_op jit(solution)/shard_map/pallas_call | solution.py:332
  (5 shorter events, 0.0 us)
Async XLA Ops:
  3.1 8.7 %collective-permute-start = (bf16[8,768]{1,0:T(8,128)(2,1)}, bf16[8,768]{1,0:T(8,128)(2,1)S(1)}, u32[]{:S(2)}, u32[]{:S(2)}) collective-permute-start(bf16[8,768]{1,0:T(8,128)(2,1)} %get-tuple-element.12), channel_id=1, source_target_pairs={{0,8},{1,9},{2,10},{3,11},{4,12},{5,13},{6,14},{7,15},{8,0},{9,1},... | collective-permute-start | bytes 36872 | tf_op jit(solution)/shard_map/ppermute | solution.py:304
  7.2 16.7 %all-to-all-start = ((bf16[16,64,128]{2,1,0:T(8,128)(2,1)}), bf16[16,64,128]{2,1,0:T(8,128)(2,1)S(1)}, u32[]{:S(2)}, u32[]{:S(2)}) async-start(bf16[16,64,128]{2,1,0:T(8,128)(2,1)} %bitcast.17), calls=%async_computation | async-start | bytes 524288 | tf_op jit(solution)/shard_map/all_to_all | solution.py:288
  12.6 5.3 %collective-permute-start.1 = (bf16[16,768]{1,0:T(8,128)(2,1)S(1)}, bf16[16,768]{1,0:T(8,128)(2,1)S(1)}, u32[]{:S(2)}, u32[]{:S(2)}) collective-permute-start(bf16[16,768]{1,0:T(8,128)(2,1)S(1)} %pad_maximum_fusion.1), channel_id=1, source_target_pairs={{0,4},{1,5},{2,6},{3,7},{4,0},{5,1},{6,2},{7,3},{8,12},{9,13},{10,... | collective-permute-start | bytes 73736 | tf_op jit(solution)/shard_map/ppermute | solution.py:304
  18.5 4.1 %collective-permute-start.2 = (bf16[32,768]{1,0:T(8,128)(2,1)S(1)}, bf16[32,768]{1,0:T(8,128)(2,1)S(1)}, u32[]{:S(2)}, u32[]{:S(2)}) collective-permute-start(bf16[32,768]{1,0:T(8,128)(2,1)S(1)} %pad_maximum_fusion), channel_id=1, source_target_pairs={{0,2},{1,3},{2,0},{3,1},{4,6},{5,7},{6,4},{7,5},{8,10},{9,11},{10,... | collective-permute-start | bytes 147464 | tf_op jit(solution)/shard_map/ppermute | solution.py:304
  22.6 9.7 %copy-start.1 = (s32[8]{0:T(128)S(1)}, s32[8]{0:T(128)}, u32[]{:S(2)}) copy-start(s32[8]{0:T(128)} %count_ref.1) | copy-start | bytes 100
  22.6 1.3 %collective-permute-start.3 = (bf16[64,768]{1,0:T(8,128)(2,1)S(1)}, bf16[64,768]{1,0:T(8,128)(2,1)S(1)}, u32[]{:S(2)}, u32[]{:S(2)}) collective-permute-start(bf16[64,768]{1,0:T(8,128)(2,1)S(1)} %constant_dynamic-update-slice_fusion.near_ref), channel_id=1, source_target_pairs={{0,1},{1,0},{2,3},{3,2},{4,5},{5,4},{6,7},{7,6},{8,9},{9,8},{10,11... | collective-permute-start | bytes 294920 | tf_op jit(solution)/shard_map/ppermute | solution.py:304
  24.0 8.4 %collective-permute-start.4 = (bf16[1024,128]{1,0:T(8,128)(2,1)S(1)}, bf16[1024,128]{1,0:T(8,128)(2,1)S(1)}, u32[]{:S(2)}, u32[]{:S(2)}) collective-permute-start(bf16[1024,128]{1,0:T(8,128)(2,1)S(1)} %bitcast.14), channel_id=1, source_target_pairs={{0,16},{16,0},{1,17},{17,1},{2,18},{18,2},{3,19},{19,3},{4,20},{20... | collective-permute-start | bytes 786440 | tf_op jit(solution)/shard_map/ppermute | solution.py:310
  26.2 1.0 %copy-start = (bf16[27,16,384]{2,1,0:T(8,128)(2,1)S(1)}, bf16[27,16,384]{2,1,0:T(8,128)(2,1)}, u32[]{:S(2)}) copy-start(bf16[27,16,384]{2,1,0:T(8,128)(2,1)} %param.9) | copy-start | bytes 995332

commit v9 on v7

--- a/solution.py
+++ b/solution.py
@@ -74,23 +74,18 @@
     w = w_ref[...].astype(jnp.float32).reshape(3, 9, own // 8, 8, C)
     puts = []
     places, width = packing(own)
-    left = jnp.broadcast_to(side_ref[0] == 0, (8, width))
+    left = jnp.broadcast_to(side_ref[0] == 0, (8, C))
+    by_lane = [{place[1]: w[i, t, c] for (i, c, t), place in places.items() if place[0] == side} for side in range(2)]
+    chosen = []
+    for lane in sorted(by_lane[0]):
+        first = by_lane[0][lane]
+        chosen.append(jnp.where(left, first, by_lane[1].get(lane, first)))
+    gap = jnp.zeros((8, width - len(chosen) * own), jnp.float32)
     half = len(tiles) // 2
     for d in range(0, n, 2):
         both = []
         for e in (d, d + 1):
-            halves = []
-            for side in range(2):
-                pieces = [
-                    w[i, t, c, :, e * own : (e + 1) * own]
-                    for i in range(3)
-                    for c in range(own // 8)
-                    for t in range(9)
-                    if places[i, c, t][0] == side
-                ]
-                pieces.append(jnp.zeros((8, width - len(pieces) * own), jnp.float32))
-                halves.append(jnp.concatenate(pieces, axis=1))
-            share = jnp.where(left, halves[0], halves[1])
+            share = jnp.concatenate([piece[:, e * own : (e + 1) * own] for piece in chosen] + [gap], axis=1)
             both += [share[:, t * 128 : (t + 1) * 128] for t in range(width // 128)]
             both += tiles[half:] if e % 2 else tiles[:half]
         both = jnp.concatenate(both, axis=0).astype(jnp.bfloat16)

time: 49.9 us -> 49.5 us (level)
  transfers between devices with their start and end apart: 2 -> 2, of which waited for: 1 -> 1; matrix products, arithmetic and copies ran while one was open for 1% -> 2% of each run, Pallas kernels for 9% -> 9%
where the time goes in v9:
time: 49.5 us; the launch traced here: 49.2 us
  blocking collectives  32.8 us (66%)
  Pallas kernels  11.8 us (24%)
  starting transfers between devices  1.74 us (4%)
  waiting for transfers between devices  1.06 us (2%)
  local copies, waits for them, and re-layouts  1 us (2%)
  other arithmetic  0.72 us (1%)
    all_to_all x1, blocking collectives, by_channel(): got = lax.all_to_all(parcels, 'tm', split_axis=0, concat_axis=0, tiled=True)  19.1 us
    all_to_all x1, blocking collectives, by_channel(): out = lax.all_to_all(out, 'tm', split_axis=0, concat_axis=0, tiled=True)  13.7 us
    pallas_call x1, Pallas kernels, by_channel(): call(functools.partial(branch_kernel, n), shape((n * own, BLOCK_FRAMES *...  4.44 us
    pallas_call x1, Pallas kernels, by_channel(): call(functools.partial(active_kernel, n), (shape((frames * C, LANES), bf1...  3.89 us
    pallas_call x1, Pallas kernels, by_channel(): call(functools.partial(parcels_kernel, n), shape((n * (height + extra), 1...  2.18 us
    ppermute x1, starting transfers between devices, by_channel(): lax.ppermute(split[:, :height].reshape(n * height, 128), 'groups', [(0, 1...  1.56 us
    ppermute x1, waiting for transfers between devices, by_channel(): lax.ppermute(split[:, :height].reshape(n * height, 128), 'groups', [(0, 1...  1.06 us
  transfers between devices with their start and end apart: 2, of which 1 were waited for; matrix products, arithmetic and copies ran while one was open for 2% of the time, Pallas kernels for 9%

profile of v9, /device:TPU:0, one launch (start us, length us, event | category | flops | bytes accessed | tf_op | source)
XLA Modules:
  0.0 49.2 jit_solution(15119139658120042862)
XLA Ops:
  0.0 2.2 %shard_map.73 = bf16[1408,128]{1,0:T(8,128)(2,1)} custom-call(bf16[16,384]{1,0:T(8,128)(2,1)} %x_hbm.1, bf16[27,24,384]{2,1,0:T(8,128)(2,1)} %w_hbm.1, s32[1]{0:T(128)} %bitcast.side_ref), custom_call_target="tpu_custom_call" | custom-call | tf_op jit(solution)/shard_map/pallas_call | solution.py:268
  2.2 19.1 %all_to_all.22 = bf16[16,88,128]{2,1,0:T(8,128)(2,1)S(1)} all-to-all(bf16[16,88,128]{2,1,0:T(8,128)(2,1)} %bitcast.19), channel_id=1, replica_groups=mesh['groups'=2,'tm'=16] {'tm'}, dimensions={0} | all-to-all | bytes 720896 | tf_op jit(solution)/shard_map/all_to_all | solution.py:282
  21.3 0.2 collective-permute-start.1
  21.5 1.6 %collective-permute-start = (bf16[1024,128]{1,0:T(8,128)(2,1)S(1)}, bf16[1024,128]{1,0:T(8,128)(2,1)S(1)}, u32[]{:S(2)}, u32[]{:S(2)}) collective-permute-start(bf16[1024,128]{1,0:T(8,128)(2,1)S(1)} %bitcast.20), channel_id=1, source_target_pairs={{0,16},{16,0},{1,17},{17,1},{2,18},{18,2},{3,19},{19,3},{4,20},{20... | collective-permute-start | bytes 786440 | tf_op jit(solution)/shard_map/ppermute | solution.py:297
  23.0 0.7 %pad_maximum_fusion.vectors_ref = f32[9,128]{1,0:T(8,128)S(1)} fusion(f32[3,128]{1,0:T(4,128)} %bitcast.22, f32[3,128]{1,0:T(4,128)} %bitcast.23, f32[3,128]{1,0:T(4,128)} %bitcast.24), kind=kLoop, calls=%fused_computation | loop fusion | flops 2304 | bytes 9216 | tf_op jit(solution)/shard_map/concatenate | solution.py:293
  23.8 0.0 copy-start.1
  23.8 0.0 copy-start
  23.8 1.0 %copy-done = bf16[27,16,384]{2,1,0:T(8,128)(2,1)S(1)} copy-done((bf16[27,16,384]{2,1,0:T(8,128)(2,1)S(1)}, bf16[27,16,384]{2,1,0:T(8,128)(2,1)}, u32[]{:S(2)}) %copy-start) | copy-done | bytes 331800
  24.7 0.5 shard_map.74.params_ref
  25.2 0.0 collective-permute-done.1.lat_ref
  25.2 3.9 %shard_map.75 = (bf16[3072,768]{1,0:T(8,128)(2,1)S(1)}, f32[8,24,768]{2,1,0:T(8,128)S(1)}) custom-call(bf16[1408,128]{1,0:T(8,128)(2,1)S(1)} %bitcast.14, bf16[384,128]{1,0:T(8,128)(2,1)S(1)} %collective-permute-done.1.lat_ref, bf16[432,640]{1,0:T(8,128)(2,1)S(1)} %shard_map.74.params_ref, s32[1]{0:T(128)} %bitcast.10.odd_ref), custom_call_target="tpu_custom_call" | custom-call | flops 2038431744 | bytes 20000000 | tf_op jit(solution)/shard_map/pallas_call | solution.py:300
  29.1 1.1 %collective-permute-done.w_ref = bf16[1024,128]{1,0:T(8,128)(2,1)S(1)} collective-permute-done((bf16[1024,128]{1,0:T(8,128)(2,1)S(1)}, bf16[1024,128]{1,0:T(8,128)(2,1)S(1)}, u32[]{:S(2)}, u32[]{:S(2)}) %collective-permute-start) | collective-permute-done | bytes 262176 | tf_op jit(solution)/shard_map/ppermute | solution.py:297
  30.2 0.0 copy-done.1
  30.2 4.4 %shard_map.76 = bf16[384,384]{1,0:T(8,128)(2,1)S(1)} custom-call(bf16[1408,128]{1,0:T(8,128)(2,1)S(1)} %bitcast.15, bf16[1024,128]{1,0:T(8,128)(2,1)S(1)} %collective-permute-done.w_ref, bf16[3072,768]{1,0:T(8,128)(2,1)S(1)} %get-tuple-element.7.x_ref, f32[8,24,768]{2,1,0:T(8,128)S(1)} %get-tuple-element.8.stream_ref, s32[1]{0:T(128)} %bitcast.side_ref, ...), custom_call_target="tpu_custom_call" | custom-call | flops 3057647616 | bytes 20000000 | tf_op jit(solution)/shard_map/pallas_call | solution.py:310
  34.6 13.7 %all_to_all.23 = bf16[16,24,384]{2,1,0:T(8,128)(2,1)S(1)} all-to-all(bf16[16,24,384]{2,1,0:T(8,128)(2,1)S(1)} %bitcast.17), channel_id=1, replica_groups=mesh['groups'=2,'tm'=16] {'tm'}, dimensions={0} | all-to-all | bytes 589824 | tf_op jit(solution)/shard_map/all_to_all | solution.py:320
  48.3 0.9 %shard_map.77 = bf16[384,384]{1,0:T(8,128)(2,1)} custom-call(bf16[384,384]{1,0:T(8,128)(2,1)S(1)} %bitcast.16), custom_call_target="tpu_custom_call" | custom-call | tf_op jit(solution)/shard_map/pallas_call | solution.py:321
  (2 shorter events, 0.0 us)
Async XLA Ops:
  21.3 3.9 %collective-permute-start.1 = (bf16[384,128]{1,0:T(8,128)(2,1)S(1)}, bf16[384,128]{1,0:T(8,128)(2,1)S(1)}, u32[]{:S(2)}, u32[]{:S(2)}) collective-permute-start(bf16[384,128]{1,0:T(8,128)(2,1)S(1)} %bitcast.21), channel_id=1, source_target_pairs={{0,1},{1,0},{2,3},{3,2},{4,5},{5,4},{6,7},{7,6},{8,9},{9,8},{10,11... | collective-permute-start | bytes 294920 | tf_op jit(solution)/shard_map/ppermute | solution.py:299
  21.5 8.7 %collective-permute-start = (bf16[1024,128]{1,0:T(8,128)(2,1)S(1)}, bf16[1024,128]{1,0:T(8,128)(2,1)S(1)}, u32[]{:S(2)}, u32[]{:S(2)}) collective-permute-start(bf16[1024,128]{1,0:T(8,128)(2,1)S(1)} %bitcast.20), channel_id=1, source_target_pairs={{0,16},{16,0},{1,17},{17,1},{2,18},{18,2},{3,19},{19,3},{4,20},{20... | collective-permute-start | bytes 786440 | tf_op jit(solution)/shard_map/ppermute | solution.py:297
  23.8 6.4 %copy-start.1 = (s32[8]{0:T(128)S(1)}, s32[8]{0:T(128)}, u32[]{:S(2)}) copy-start(s32[8]{0:T(128)} %count_ref.1) | copy-start | bytes 100
  23.8 1.0 %copy-start = (bf16[27,16,384]{2,1,0:T(8,128)(2,1)S(1)}, bf16[27,16,384]{2,1,0:T(8,128)(2,1)}, u32[]{:S(2)}) copy-start(bf16[27,16,384]{2,1,0:T(8,128)(2,1)} %param.9) | copy-start | bytes 995332

commit v10 on v9

--- a/solution.py
+++ b/solution.py
@@ -52,6 +52,18 @@
             places[run // (own // 8), run % (own // 8), t] = place
     longest = max(lane for _, lane in places.values()) + own
     return places, -(-longest // 128) * 128
+
+
+def unpacked(got, n, own):
+    width = packing(own)[1]
+    x = got.reshape(n, width // 128, 8, 128)
+    x = jnp.concatenate([x[:, t] for t in range(width // 128)], axis=2).reshape(n * 8, width)
+    runs = 3 * (own // 8)
+    ends = [(r * 9 * own, (r + 1) * 9 * own) for r in range(runs // 2)]
+    if runs % 2:
+        ends.append((runs // 2 * 9 * own, (runs // 2 * 9 + 5) * own))
+    pad = lambda a, b: jnp.zeros((n * 8, 256 - (b - a)), jnp.float32)
+    return [jnp.concatenate([x[:, a:b], pad(a, b)], axis=1) for a, b in ends]
 
 
 def parcels_kernel(n, x_hbm, w_hbm, side_ref, o_hbm, x_ref, w_ref, o_ref, in_sem, out_sem):
@@ -137,7 +149,7 @@
     o_ref[...] = jnp.concatenate([mine, after, full], axis=0).astype(jnp.bfloat16)
 
 
-def active_kernel(n, got_ref, lat_ref, params_ref, odd_ref, x_ref, stream_ref, col_ref):
+def active_kernel(n, got_ref, lat_ref, params_ref, odd_ref, x_ref, stream_ref, half_ref, col_ref):
     own = C // n
     frames = n // PROMPT_SAMPLES * BLOCK_FRAMES
     each = LATENT_CHANNELS * BLOCK_FRAMES // n
@@ -147,7 +159,11 @@
     ones = (lax.broadcasted_iota(jnp.int32, (16, LANES), 0) < 3).astype(jnp.float32).astype(jnp.bfloat16)
     per_frame = LATENT_CHANNELS // each
     blocks = n // PROMPT_SAMPLES
-    mine = got_ref[...].astype(jnp.float32).reshape(n, -1, 128)[:, packing(own)[1] // 16 :]
+    got = got_ref[...].astype(jnp.float32).reshape(n, -1, 128)
+    share = unpacked(got[:, : packing(own)[1] // 16], n, own)
+    for r, run in enumerate(share):
+        half_ref[r] = run
+    mine = got[:, packing(own)[1] // 16 :]
     other = lat_ref[...].astype(jnp.float32).reshape(mine.shape)
     even = jnp.broadcast_to(odd_ref[0] == 0, mine.shape)
     lats = jnp.concatenate([jnp.where(even, mine, other), jnp.where(even, other, mine)], axis=1)
@@ -176,32 +192,24 @@
         x_ref[f * C : (f + 1) * C, :] = half + half * jnp.tanh(half)
 
 
-def branch_kernel(n, got_ref, w_ref, x_ref, stream_ref, side_ref, count_ref, o_ref, out_ref):
+def branch_kernel(n, half_ref, w_ref, x_ref, stream_ref, side_ref, count_ref, o_ref, out_ref):
     own = C // n
     frames = n // PROMPT_SAMPLES * BLOCK_FRAMES
-    places, width = packing(own)
-
-    def lanes(x):
-        x = x.reshape(n, width // 128, 8, 128)
-        return jnp.concatenate([x[:, t] for t in range(width // 128)], axis=2).reshape(n * 8, width)
-
-    mine = lanes(got_ref[...].astype(jnp.float32).reshape(n, -1, 128)[:, : width // 16])
-    other = lanes(w_ref[...].astype(jnp.float32))
-    left = jnp.broadcast_to(side_ref[0] == 0, other.shape)
-    halves = (jnp.where(left, mine, other), jnp.where(left, other, mine))
-    pad = jnp.zeros((n * 8, 256 - 9 * own), jnp.float32)
+    other = unpacked(w_ref[...].astype(jnp.float32), n, own)
+    mine = [half_ref[r] for r in range(len(other))]
+    left = jnp.broadcast_to(side_ref[0] == 0, (n * 8, 256))
+    low = [jnp.where(left, m, o) for m, o in zip(mine, other)]
+    high = [jnp.where(left, o, m) for m, o in zip(mine, other)]
+    whole = 3 * (own // 8) // 2
+    runs = low[:whole] + high[:whole]
+    if len(low) > whole:
+        rest = jnp.zeros((n * 8, 256 - 9 * own), jnp.float32)
+        runs.append(jnp.concatenate([low[whole][:, : 5 * own], high[whole][:, : 4 * own], rest], axis=1))
+    runs = [run.reshape(n, 1, 8, 256) for run in runs]
     depths = []
     for i in range(3):
-        runs = []
-        for c in range(own // 8):
-            side, lane = places[i, c, 0]
-            if places[i, c, 8][0] == side:
-                parts = [halves[side][:, lane : lane + 9 * own]]
-            else:
-                end = places[i, c, 5][1]
-                parts = [halves[0][:, lane : lane + 5 * own], halves[1][:, end : end + 4 * own]]
-            runs.append(jnp.concatenate(parts + [pad], axis=1).reshape(n, 1, 8, 256))
-        depths.append(jnp.concatenate(runs, axis=1).reshape(C, 256))
+        at = i * (own // 8)
+        depths.append(jnp.concatenate(runs[at : at + own // 8], axis=1).reshape(C, 256))
     w = jnp.concatenate(depths, axis=0)
     weight = jnp.transpose(w.astype(jnp.bfloat16))[: -(-9 * own // 16) * 16]
     lane = lax.broadcasted_iota(jnp.int32, (1, LANES), 1)
@@ -297,11 +305,16 @@
     other = lax.ppermute(split[:, :height].reshape(n * height, 128), "groups", [(0, 1), (1, 0)])
     lats = split[:, height:].reshape(-1, 128)
     lats = lax.ppermute(lats, "tm", [(i, i ^ 1) for i in range(n)])
-    active, stream = call(
+    halves = 3 * (own // 8) // 2 + 3 * (own // 8) % 2
+    active, stream, half = call(
         functools.partial(active_kernel, n),
-        (shape((frames * C, LANES), bf16), shape((frames, own, LANES), f32)),
+        (
+            shape((frames * C, LANES), bf16),
+            shape((frames, own, LANES), f32),
+            shape((halves, n * 8, 256), f32),
+        ),
         [VMEM, VMEM, VMEM, SMEM],
-        (VMEM, VMEM),
+        (VMEM, VMEM, VMEM),
         [pltpu.VMEM((frames * 9 * LATENT_CHANNELS, LANES), bf16)],
         flops=2 * frames * LANES * 432 * C,
         moved=20_000_000,
@@ -316,7 +329,7 @@
         flops=2 * frames * LANES * 27 * C * own,
         moved=20_000_000,
         limit=24,
-    )(got, other, active, stream, side, counts)
+    )(half, other, active, stream, side, counts)
     out = lax.all_to_all(out, "tm", split_axis=0, concat_axis=0, tiled=True)
     out = call(transpose_kernel, shape((BLOCK_FRAMES * HW, C), bf16), [VMEM], VMEM)(out)
     return out.reshape(BLOCK_FRAMES, LATENT_ROWS, LATENT_COLUMNS, C)

time: 49.5 us -> 49.5 us (level)
  no operation moved by 1% of the time
where the time goes in v10:
time: 49.5 us; the launch traced here: 49.1 us
  blocking collectives  32.8 us (66%)
  Pallas kernels  11.9 us (24%)
  starting transfers between devices  1.74 us (4%)
  local copies, waits for them, and re-layouts  1 us (2%)
  waiting for transfers between devices  0.98 us (2%)
  other arithmetic  0.72 us (1%)
    all_to_all x1, blocking collectives, by_channel(): got = lax.all_to_all(parcels, 'tm', split_axis=0, concat_axis=0, tiled=True)  19.1 us
    all_to_all x1, blocking collectives, by_channel(): out = lax.all_to_all(out, 'tm', split_axis=0, concat_axis=0, tiled=True)  13.7 us
    pallas_call x1, Pallas kernels, by_channel(): call(functools.partial(branch_kernel, n), shape((n * own, BLOCK_FRAMES *...  4.4 us
    pallas_call x1, Pallas kernels, by_channel(): call(functools.partial(active_kernel, n), (shape((frames * C, LANES), bf1...  3.97 us
    pallas_call x1, Pallas kernels, by_channel(): call(functools.partial(parcels_kernel, n), shape((n * (height + extra), 1...  2.18 us
    ppermute x1, starting transfers between devices, by_channel(): lax.ppermute(split[:, :height].reshape(n * height, 128), 'groups', [(0, 1...  1.56 us
  transfers between devices with their start and end apart: 2, of which 1 were waited for; matrix products, arithmetic and copies ran while one was open for 2% of the time, Pallas kernels for 9%

profile of v10, /device:TPU:0, one launch (start us, length us, event | category | flops | bytes accessed | tf_op | source)
XLA Modules:
  0.0 49.1 jit_solution(7077455063210052618)
XLA Ops:
  0.0 2.2 %shard_map.73 = bf16[1408,128]{1,0:T(8,128)(2,1)} custom-call(bf16[16,384]{1,0:T(8,128)(2,1)} %x_hbm.1, bf16[27,24,384]{2,1,0:T(8,128)(2,1)} %w_hbm.1, s32[1]{0:T(128)} %bitcast.side_ref), custom_call_target="tpu_custom_call" | custom-call | tf_op jit(solution)/shard_map/pallas_call | solution.py:276
  2.2 19.1 %all_to_all.22 = bf16[16,88,128]{2,1,0:T(8,128)(2,1)S(1)} all-to-all(bf16[16,88,128]{2,1,0:T(8,128)(2,1)} %bitcast.18), channel_id=1, replica_groups=mesh['groups'=2,'tm'=16] {'tm'}, dimensions={0} | all-to-all | bytes 720896 | tf_op jit(solution)/shard_map/all_to_all | solution.py:290
  21.3 0.2 collective-permute-start
  21.5 1.6 %collective-permute-start.1 = (bf16[1024,128]{1,0:T(8,128)(2,1)S(1)}, bf16[1024,128]{1,0:T(8,128)(2,1)S(1)}, u32[]{:S(2)}, u32[]{:S(2)}) collective-permute-start(bf16[1024,128]{1,0:T(8,128)(2,1)S(1)} %bitcast.19), channel_id=1, source_target_pairs={{0,16},{16,0},{1,17},{17,1},{2,18},{18,2},{3,19},{19,3},{4,20},{20... | collective-permute-start | bytes 786440 | tf_op jit(solution)/shard_map/ppermute | solution.py:305
  23.0 0.7 %pad_maximum_fusion.vectors_ref = f32[9,128]{1,0:T(8,128)S(1)} fusion(f32[3,128]{1,0:T(4,128)} %bitcast.21, f32[3,128]{1,0:T(4,128)} %bitcast.22, f32[3,128]{1,0:T(4,128)} %bitcast.23), kind=kLoop, calls=%fused_computation | loop fusion | flops 2304 | bytes 9216 | tf_op jit(solution)/shard_map/concatenate | solution.py:301
  23.8 0.0 copy-start.1
  23.8 0.0 copy-start
  23.8 1.0 %copy-done = bf16[27,16,384]{2,1,0:T(8,128)(2,1)S(1)} copy-done((bf16[27,16,384]{2,1,0:T(8,128)(2,1)S(1)}, bf16[27,16,384]{2,1,0:T(8,128)(2,1)}, u32[]{:S(2)}) %copy-start) | copy-done | bytes 331800
  24.7 0.5 shard_map.74.params_ref
  25.2 0.0 collective-permute-done.lat_ref
  25.2 4.0 %shard_map.75 = (bf16[3072,768]{1,0:T(8,128)(2,1)S(1)}, f32[8,24,768]{2,1,0:T(8,128)S(1)}, f32[5,128,256]{2,1,0:T(8,128)S(1)}) custom-call(bf16[1408,128]{1,0:T(8,128)(2,1)S(1)} %bitcast.14, bf16[384,128]{1,0:T(8,128)(2,1)S(1)} %collective-permute-done.lat_ref, bf16[432,640]{1,0:T(8,128)(2,1)S(1)} %shard_map.74.params_ref, s32[1]{0:T(128)} %bitcast.9.odd_ref), custom_call_target="tpu_custom_call" | custom-call | flops 2038431744 | bytes 20000000 | tf_op jit(solution)/shard_map/pallas_call | solution.py:309
  29.2 1.0 %collective-permute-done.1.w_ref = bf16[1024,128]{1,0:T(8,128)(2,1)S(1)} collective-permute-done((bf16[1024,128]{1,0:T(8,128)(2,1)S(1)}, bf16[1024,128]{1,0:T(8,128)(2,1)S(1)}, u32[]{:S(2)}, u32[]{:S(2)}) %collective-permute-start.1) | collective-permute-done | bytes 262176 | tf_op jit(solution)/shard_map/ppermute | solution.py:305
  30.2 0.0 copy-done.1
  30.2 4.4 %shard_map.76 = bf16[384,384]{1,0:T(8,128)(2,1)S(1)} custom-call(f32[5,128,256]{2,1,0:T(8,128)S(1)} %get-tuple-element.8.half_ref, bf16[1024,128]{1,0:T(8,128)(2,1)S(1)} %collective-permute-done.1.w_ref, bf16[3072,768]{1,0:T(8,128)(2,1)S(1)} %get-tuple-element.9.x_ref, f32[8,24,768]{2,1,0:T(8,128)S(1)} %get-tuple-element.10.stream_ref, s32[1]{0:T(128)} %bitcast.side_ref, ...), custom_call_target="tpu_custom_call" | custom-call | flops 3057647616 | bytes 20000000 | tf_op jit(solution)/shard_map/pallas_call | solution.py:323
  34.6 13.7 %all_to_all.23 = bf16[16,24,384]{2,1,0:T(8,128)(2,1)S(1)} all-to-all(bf16[16,24,384]{2,1,0:T(8,128)(2,1)S(1)} %bitcast.16), channel_id=1, replica_groups=mesh['groups'=2,'tm'=16] {'tm'}, dimensions={0} | all-to-all | bytes 589824 | tf_op jit(solution)/shard_map/all_to_all | solution.py:333
  48.3 0.9 %shard_map.77 = bf16[384,384]{1,0:T(8,128)(2,1)} custom-call(bf16[384,384]{1,0:T(8,128)(2,1)S(1)} %bitcast.15), custom_call_target="tpu_custom_call" | custom-call | tf_op jit(solution)/shard_map/pallas_call | solution.py:334
  (2 shorter events, 0.0 us)
Async XLA Ops:
  21.3 3.9 %collective-permute-start = (bf16[384,128]{1,0:T(8,128)(2,1)S(1)}, bf16[384,128]{1,0:T(8,128)(2,1)S(1)}, u32[]{:S(2)}, u32[]{:S(2)}) collective-permute-start(bf16[384,128]{1,0:T(8,128)(2,1)S(1)} %bitcast.20), channel_id=1, source_target_pairs={{0,1},{1,0},{2,3},{3,2},{4,5},{5,4},{6,7},{7,6},{8,9},{9,8},{10,11... | collective-permute-start | bytes 294920 | tf_op jit(solution)/shard_map/ppermute | solution.py:307
  21.5 8.7 %collective-permute-start.1 = (bf16[1024,128]{1,0:T(8,128)(2,1)S(1)}, bf16[1024,128]{1,0:T(8,128)(2,1)S(1)}, u32[]{:S(2)}, u32[]{:S(2)}) collective-permute-start(bf16[1024,128]{1,0:T(8,128)(2,1)S(1)} %bitcast.19), channel_id=1, source_target_pairs={{0,16},{16,0},{1,17},{17,1},{2,18},{18,2},{3,19},{19,3},{4,20},{20... | collective-permute-start | bytes 786440 | tf_op jit(solution)/shard_map/ppermute | solution.py:305
  23.8 6.4 %copy-start.1 = (s32[8]{0:T(128)S(1)}, s32[8]{0:T(128)}, u32[]{:S(2)}) copy-start(s32[8]{0:T(128)} %count_ref.1) | copy-start | bytes 100
  23.8 1.0 %copy-start = (bf16[27,16,384]{2,1,0:T(8,128)(2,1)S(1)}, bf16[27,16,384]{2,1,0:T(8,128)(2,1)}, u32[]{:S(2)}) copy-start(bf16[27,16,384]{2,1,0:T(8,128)(2,1)} %param.9) | copy-start | bytes 995332

commit v11 on v10

--- a/solution.py
+++ b/solution.py
@@ -210,8 +210,8 @@
     for i in range(3):
         at = i * (own // 8)
         depths.append(jnp.concatenate(runs[at : at + own // 8], axis=1).reshape(C, 256))
-    w = jnp.concatenate(depths, axis=0)
-    weight = jnp.transpose(w.astype(jnp.bfloat16))[: -(-9 * own // 16) * 16]
+    tall = -(-9 * own // 16) * 16
+    turned = [jnp.transpose(depths[i].astype(jnp.bfloat16))[:tall] for i in (2, 1, 0)]
     lane = lax.broadcasted_iota(jnp.int32, (1, LANES), 1)
     count = jnp.zeros((1, LANES), jnp.int32)
     for s in range(PROMPT_SAMPLES):
@@ -219,7 +219,7 @@
     for f in range(frames):
         least = max(f - 2, 0)
         z = jnp.dot(
-            weight[:, (2 - (f - least)) * C :],
+            jnp.concatenate(turned[: f - least + 1][::-1], axis=1),
             x_ref[least * C : (f + 1) * C, :],
             preferred_element_type=jnp.float32,
         )

time: 49.5 us -> 49.5 us (level)
  no operation moved by 1% of the time
where the time goes in v11:
time: 49.5 us; the launch traced here: 49.1 us
  blocking collectives  32.8 us (66%)
  Pallas kernels  11.9 us (24%)
  starting transfers between devices  1.74 us (4%)
  local copies, waits for them, and re-layouts  1 us (2%)
  waiting for transfers between devices  0.98 us (2%)
  other arithmetic  0.72 us (1%)
    all_to_all x1, blocking collectives, by_channel(): got = lax.all_to_all(parcels, 'tm', split_axis=0, concat_axis=0, tiled=True)  19.1 us
    all_to_all x1, blocking collectives, by_channel(): out = lax.all_to_all(out, 'tm', split_axis=0, concat_axis=0, tiled=True)  13.7 us
    pallas_call x1, Pallas kernels, by_channel(): call(functools.partial(branch_kernel, n), shape((n * own, BLOCK_FRAMES *...  4.4 us
    pallas_call x1, Pallas kernels, by_channel(): call(functools.partial(active_kernel, n), (shape((frames * C, LANES), bf1...  3.97 us
    pallas_call x1, Pallas kernels, by_channel(): call(functools.partial(parcels_kernel, n), shape((n * (height + extra), 1...  2.18 us
    ppermute x1, starting transfers between devices, by_channel(): lax.ppermute(split[:, :height].reshape(n * height, 128), 'groups', [(0, 1...  1.56 us
  transfers between devices with their start and end apart: 2, of which 1 were waited for; matrix products, arithmetic and copies ran while one was open for 2% of the time, Pallas kernels for 9%

profile of v11, /device:TPU:0, one launch (start us, length us, event | category | flops | bytes accessed | tf_op | source)
XLA Modules:
  0.0 49.1 jit_solution(7077455063210052618)
XLA Ops:
  0.0 2.2 %shard_map.73 = bf16[1408,128]{1,0:T(8,128)(2,1)} custom-call(bf16[16,384]{1,0:T(8,128)(2,1)} %x_hbm.1, bf16[27,24,384]{2,1,0:T(8,128)(2,1)} %w_hbm.1, s32[1]{0:T(128)} %bitcast.side_ref), custom_call_target="tpu_custom_call" | custom-call | tf_op jit(solution)/shard_map/pallas_call | solution.py:276
  2.2 19.1 %all_to_all.22 = bf16[16,88,128]{2,1,0:T(8,128)(2,1)S(1)} all-to-all(bf16[16,88,128]{2,1,0:T(8,128)(2,1)} %bitcast.18), channel_id=1, replica_groups=mesh['groups'=2,'tm'=16] {'tm'}, dimensions={0} | all-to-all | bytes 720896 | tf_op jit(solution)/shard_map/all_to_all | solution.py:290
  21.3 0.2 collective-permute-start
  21.5 1.6 %collective-permute-start.1 = (bf16[1024,128]{1,0:T(8,128)(2,1)S(1)}, bf16[1024,128]{1,0:T(8,128)(2,1)S(1)}, u32[]{:S(2)}, u32[]{:S(2)}) collective-permute-start(bf16[1024,128]{1,0:T(8,128)(2,1)S(1)} %bitcast.19), channel_id=1, source_target_pairs={{0,16},{16,0},{1,17},{17,1},{2,18},{18,2},{3,19},{19,3},{4,20},{20... | collective-permute-start | bytes 786440 | tf_op jit(solution)/shard_map/ppermute | solution.py:305
  23.0 0.7 %pad_maximum_fusion.vectors_ref = f32[9,128]{1,0:T(8,128)S(1)} fusion(f32[3,128]{1,0:T(4,128)} %bitcast.21, f32[3,128]{1,0:T(4,128)} %bitcast.22, f32[3,128]{1,0:T(4,128)} %bitcast.23), kind=kLoop, calls=%fused_computation | loop fusion | flops 2304 | bytes 9216 | tf_op jit(solution)/shard_map/concatenate | solution.py:301
  23.8 0.0 copy-start.1
  23.8 0.0 copy-start
  23.8 1.0 %copy-done = bf16[27,16,384]{2,1,0:T(8,128)(2,1)S(1)} copy-done((bf16[27,16,384]{2,1,0:T(8,128)(2,1)S(1)}, bf16[27,16,384]{2,1,0:T(8,128)(2,1)}, u32[]{:S(2)}) %copy-start) | copy-done | bytes 331800
  24.7 0.5 shard_map.74.params_ref
  25.2 0.0 collective-permute-done.lat_ref
  25.2 4.0 %shard_map.75 = (bf16[3072,768]{1,0:T(8,128)(2,1)S(1)}, f32[8,24,768]{2,1,0:T(8,128)S(1)}, f32[5,128,256]{2,1,0:T(8,128)S(1)}) custom-call(bf16[1408,128]{1,0:T(8,128)(2,1)S(1)} %bitcast.14, bf16[384,128]{1,0:T(8,128)(2,1)S(1)} %collective-permute-done.lat_ref, bf16[432,640]{1,0:T(8,128)(2,1)S(1)} %shard_map.74.params_ref, s32[1]{0:T(128)} %bitcast.9.odd_ref), custom_call_target="tpu_custom_call" | custom-call | flops 2038431744 | bytes 20000000 | tf_op jit(solution)/shard_map/pallas_call | solution.py:309
  29.2 1.0 %collective-permute-done.1.w_ref = bf16[1024,128]{1,0:T(8,128)(2,1)S(1)} collective-permute-done((bf16[1024,128]{1,0:T(8,128)(2,1)S(1)}, bf16[1024,128]{1,0:T(8,128)(2,1)S(1)}, u32[]{:S(2)}, u32[]{:S(2)}) %collective-permute-start.1) | collective-permute-done | bytes 262176 | tf_op jit(solution)/shard_map/ppermute | solution.py:305
  30.2 0.0 copy-done.1
  30.2 4.4 %shard_map.76 = bf16[384,384]{1,0:T(8,128)(2,1)S(1)} custom-call(f32[5,128,256]{2,1,0:T(8,128)S(1)} %get-tuple-element.8.half_ref, bf16[1024,128]{1,0:T(8,128)(2,1)S(1)} %collective-permute-done.1.w_ref, bf16[3072,768]{1,0:T(8,128)(2,1)S(1)} %get-tuple-element.9.x_ref, f32[8,24,768]{2,1,0:T(8,128)S(1)} %get-tuple-element.10.stream_ref, s32[1]{0:T(128)} %bitcast.side_ref, ...), custom_call_target="tpu_custom_call" | custom-call | flops 3057647616 | bytes 20000000 | tf_op jit(solution)/shard_map/pallas_call | solution.py:323
  34.6 13.7 %all_to_all.23 = bf16[16,24,384]{2,1,0:T(8,128)(2,1)S(1)} all-to-all(bf16[16,24,384]{2,1,0:T(8,128)(2,1)S(1)} %bitcast.16), channel_id=1, replica_groups=mesh['groups'=2,'tm'=16] {'tm'}, dimensions={0} | all-to-all | bytes 589824 | tf_op jit(solution)/shard_map/all_to_all | solution.py:333
  48.3 0.9 %shard_map.77 = bf16[384,384]{1,0:T(8,128)(2,1)} custom-call(bf16[384,384]{1,0:T(8,128)(2,1)S(1)} %bitcast.15), custom_call_target="tpu_custom_call" | custom-call | tf_op jit(solution)/shard_map/pallas_call | solution.py:334
  (2 shorter events, 0.0 us)
Async XLA Ops:
  21.3 3.9 %collective-permute-start = (bf16[384,128]{1,0:T(8,128)(2,1)S(1)}, bf16[384,128]{1,0:T(8,128)(2,1)S(1)}, u32[]{:S(2)}, u32[]{:S(2)}) collective-permute-start(bf16[384,128]{1,0:T(8,128)(2,1)S(1)} %bitcast.20), channel_id=1, source_target_pairs={{0,1},{1,0},{2,3},{3,2},{4,5},{5,4},{6,7},{7,6},{8,9},{9,8},{10,11... | collective-permute-start | bytes 294920 | tf_op jit(solution)/shard_map/ppermute | solution.py:307
  21.5 8.7 %collective-permute-start.1 = (bf16[1024,128]{1,0:T(8,128)(2,1)S(1)}, bf16[1024,128]{1,0:T(8,128)(2,1)S(1)}, u32[]{:S(2)}, u32[]{:S(2)}) collective-permute-start(bf16[1024,128]{1,0:T(8,128)(2,1)S(1)} %bitcast.19), channel_id=1, source_target_pairs={{0,16},{16,0},{1,17},{17,1},{2,18},{18,2},{3,19},{19,3},{4,20},{20... | collective-permute-start | bytes 786440 | tf_op jit(solution)/shard_map/ppermute | solution.py:305
  23.8 6.4 %copy-start.1 = (s32[8]{0:T(128)S(1)}, s32[8]{0:T(128)}, u32[]{:S(2)}) copy-start(s32[8]{0:T(128)} %count_ref.1) | copy-start | bytes 100
  23.8 1.0 %copy-start = (bf16[27,16,384]{2,1,0:T(8,128)(2,1)S(1)}, bf16[27,16,384]{2,1,0:T(8,128)(2,1)}, u32[]{:S(2)}) copy-start(bf16[27,16,384]{2,1,0:T(8,128)(2,1)} %param.9) | copy-start | bytes 995332
